TPU v7x, 32 devices: a whole 2x2x4 slice. The times are simulated.
32 devices in a mesh: dp: 8 (over z, y), head: 4 (over x, core).
Axes of the slice: x: 2, y: 2, z: 4, core: 2. Of those that a mesh axis runs over, the one named last changes fastest.
Arguments:
- tokens: bfloat16 [2, 4096, 512], P(None, ('dp', 'head')), may hold values from -6 to 6
- cotangent: bfloat16 [2, 4096, 512], P(None, ('dp', 'head')), may hold values from -6 to 6
- lengths: int32 [2, 8, 8], P(None, 'dp'), may hold values from 1 to 448, 512 in all within a row
- halting: int32 [2, 2, 4096], P(None, None, ('dp', 'head')), may hold values 0 or 1
- w_query: bfloat16 [512, 512], P(('dp', 'head')), may hold values from -0.25 to 0.25
- w_key: bfloat16 [512, 512], P(('dp', 'head')), may hold values from -0.25 to 0.25
- w_value: bfloat16 [512, 512], P(('dp', 'head')), may hold values from -0.25 to 0.25
- w_out: bfloat16 [512, 512], P(('dp', 'head')), may hold values from -4 to 4
- w_in: bfloat16 [512, 2048], P(('dp', 'head')), may hold values from -0.25 to 0.25
- w_hidden: bfloat16 [2048, 512], P(('dp', 'head')), may hold values from -0.125 to 0.125
- w_halt: bfloat16 [512], P(('dp', 'head')), may hold values from -0.25 to 0.25
- gain_attn: bfloat16 [512], P(('dp', 'head')), may hold values from 0.5 to 1.5
- shift_attn: bfloat16 [512], P(('dp', 'head')), may hold values from -3 to 3
- gain_ffn: bfloat16 [512], P(('dp', 'head')), may hold values from 0.5 to 1.5
- shift_ffn: bfloat16 [512], P(('dp', 'head')), may hold values from -3 to 3
Outputs:
- output: float32 [2, 4096, 512], P(None, ('dp', 'head'))
- input_grad: float32 [2, 4096, 512], P(None, ('dp', 'head'))
- grad_query: float32 [512, 512], P(('dp', 'head'))
- grad_key: float32 [512, 512], P(('dp', 'head'))
- grad_value: float32 [512, 512], P(('dp', 'head'))
- grad_out: float32 [512, 512], P(('dp', 'head'))
- grad_in: float32 [512, 2048], P(('dp', 'head'))
- grad_hidden: float32 [2048, 512], P(('dp', 'head'))
- grad_halt: float32 [512], P(('dp', 'head'))
- grad_gain_attn: float32 [512], P(('dp', 'head'))
- grad_shift_attn: float32 [512], P(('dp', 'head'))
- grad_gain_ffn: float32 [512], P(('dp', 'head'))
- grad_shift_ffn: float32 [512], P(('dp', 'head'))
Inputs may be any that keep to these rules, and one draw needn't show every extreme that they name: Each row holds the 8 sentence lengths of one pack, in order; they sum to 512 and the longest is exactly 448.
All inputs are finite; a program needn't handle non-finite values. No bound on the sum of `halting` on one device may be relied on, other than what follows from the above.
Results may differ from a plain program's by a relative error of at most 0.025.
Values may be sent and summed in bfloat16 or wider, within the bound.
No kernel may reach another device: no remote copies, remote signals or barrier semaphores. Data moves between devices by JAX's collectives and lax.ppermute only.
A program may use at most 128 MiB of HBM per device.

v0:
```python
import functools

import jax
import jax.numpy as jnp
from jax import lax
from jax.experimental import pallas as pl
from jax.experimental.pallas import tpu as pltpu
from jax.sharding import PartitionSpec as P

HD = 64
EPSILON = 1e-06
F32 = jnp.float32
BF16 = jnp.bfloat16
LANES = 128
ROWS = 32
ATT_ROWS = 256
BLOCK = 512
VECS = 5
MIB = 1024 * 1024
SCOPED = 20 * MIB
MICRO = 1.15e9
GELU_A = 0.7978845608028654
GELU_B = 0.044715


def dot(a, b, ca=1, cb=0):
    return lax.dot_general(a, b, (((ca,), (cb,)), ((), ())), preferred_element_type=F32)


def chunks(total, size):
    size = min(size, total)
    return [slice(i, i + size) for i in range(0, total, size)]


def wide(column):
    return jnp.broadcast_to(column, (column.shape[0], LANES))


def mean(values):
    return jnp.sum(values, axis=-1, keepdims=True) * (1.0 / values.shape[-1])


def fold(values):
    return jnp.sum(values.reshape(values.shape[0] // 8, 8, values.shape[1]), axis=0)


class Flat:
    def __init__(self, ref):
        self.ref = ref

    def __getitem__(self, index):
        if index is Ellipsis:
            index = (slice(None), slice(None))
        value = self.ref[..., index[1]]
        return value.reshape(-1, value.shape[-1])[index[0]]


def matrix(ref, index):
    value = ref[index]
    return value.reshape(-1, value.shape[-1])


def head_mask(rows):
    lane = lax.broadcasted_iota(jnp.int32, (rows, LANES), 1)
    return lane < HD


def normalize(values):
    center = values - mean(values)
    inverse = lax.rsqrt(mean(center * center) + EPSILON)
    return center * inverse, inverse


def normalize_back(unit, inverse, grad):
    return inverse * (grad - mean(grad) - unit * mean(grad * unit))


def split_heads(values_ref, stacked_ref):
    rows = values_ref.shape[0]
    for part in chunks(rows, ATT_ROWS):
        first = head_mask(part.stop - part.start)
        for pair in range(stacked_ref.shape[0]):
            block = values_ref[part, pair * LANES : (pair + 1) * LANES].astype(F32)
            stacked_ref[pair, part, :] = jnp.where(first, block, 0.0).astype(BF16)
            stacked_ref[pair, rows + part.start : rows + part.stop, :] = jnp.where(
                first, 0.0, block
            ).astype(BF16)


def project(rown_ref, roth_ref, wa_ref, q_ref, q2_ref, k_ref, v_ref):
    rows, width = rown_ref.shape
    q_ref[...] = (
        dot(rown_ref[...], matrix(wa_ref, 0)).astype(BF16).astype(F32) * HD**-0.5
    ).astype(BF16)
    split_heads(q_ref, q2_ref)
    for at, source in ((0, rown_ref), (rows, roth_ref)):
        span = slice(at, at + source.shape[0])
        k_ref[span, :] = dot(source[...], matrix(wa_ref, 1)).astype(BF16)
        v_ref[span, :] = dot(source[...], matrix(wa_ref, 2)).astype(BF16)


def set_bias(segq_ref, segk_ref, bias_ref):
    for part in chunks(bias_ref.shape[0], ROWS):
        bias_ref[part, :] = jnp.where(segq_ref[part, 0:1] == segk_ref[0:1, :], 0.0, -1e30)


def attend(q2_ref, k_ref, v_ref, bias_ref, p_ref, ctx_ref, o_ref):
    rows, length = bias_ref.shape
    for pair in range(q2_ref.shape[0]):
        cols = slice(pair * LANES, (pair + 1) * LANES)
        for part in chunks(2 * rows, 2 * rows):
            scores = dot(q2_ref[pair, part, :], k_ref[:, cols], 1, 1)
            scores = (scores.reshape(2, rows, length) + bias_ref[...][None]).reshape(2 * rows, length)
            weights = jnp.exp(scores - jnp.max(scores, axis=-1, keepdims=True))
            inverse = 1.0 / jnp.sum(weights, axis=-1, keepdims=True)
            low = (weights * inverse).astype(BF16)
            p_ref[pair, part, :] = low
            o_ref[part, :] = dot(low, v_ref[:, cols])
        for part in chunks(rows, ATT_ROWS):
            first = head_mask(part.stop - part.start)
            second = o_ref[rows + part.start : rows + part.stop, :]
            ctx_ref[part, cols] = jnp.where(first, o_ref[part, :], second).astype(BF16)


def first_norm(x_ref, ctx_ref, wa_ref, vec_ref, acc_ref, n1_ref, r1_ref, nlow_ref):
    acc_ref[...] = dot(ctx_ref[...], matrix(wa_ref, 3))
    for part in chunks(x_ref.shape[0], ROWS):
        unit, inverse = normalize(x_ref[part, :] + acc_ref[part, :])
        n1_ref[part, :] = unit
        r1_ref[part, :] = wide(inverse)
        nlow_ref[part, :] = (unit * vec_ref[1:2, :] + vec_ref[2:3, :]).astype(BF16)


def feed_forward(nlow_ref, win_ref, whid_ref, inner_ref, hid_ref, dg_ref, acc_ref):
    rows = nlow_ref.shape[0]
    for cols in chunks(hid_ref.shape[1], BLOCK):
        inner_ref[...] = dot(nlow_ref[...], matrix(win_ref, cols.start // BLOCK))
        for part in chunks(rows, ROWS):
            x = inner_ref[part, :]
            square = x * x
            t = jnp.tanh(x * (GELU_A + GELU_A * GELU_B * square))
            half = 0.5 + 0.5 * t
            hid_ref[part, cols] = (x * half).astype(BF16)
            slope = 0.5 * x * (1.0 - t * t) * (GELU_A + 3.0 * GELU_A * GELU_B * square)
            dg_ref[part, cols] = (half + slope).astype(BF16)
    acc_ref[...] = dot(hid_ref[...], whid_ref[...])


def second_norm(part, vec_ref, n1_ref, acc_ref):
    normed = n1_ref[part, :] * vec_ref[1:2, :] + vec_ref[2:3, :]
    unit, inverse = normalize(normed + acc_ref[part, :])
    updated = unit * vec_ref[3:4, :] + vec_ref[4:5, :]
    rate = jax.nn.sigmoid(jnp.sum(updated * vec_ref[0:1, :], axis=-1, keepdims=True))
    return unit, inverse, updated, rate


def tail_back(
    part, step, gs, gp, halt_ref, vec_ref, n2_ref, r2_ref, rate_ref, b2_ref, gsec_ref, base_ref, sums_ref
):
    width = n2_ref.shape[1]
    keep = halt_ref[part, 2 * width + step : 2 * width + step + 1].astype(F32)
    unit = n2_ref[part, :]
    updated = unit * vec_ref[3:4, :] + vec_ref[4:5, :]
    rate = rate_ref[part, 0:1]
    logit = keep * jnp.sum(gp * updated, axis=-1, keepdims=True) * rate * (1.0 - rate)
    grad = keep * gs + (keep * rate) * gp + logit * vec_ref[0:1, :]
    base_ref[part, :] = gs - keep * gs
    sums_ref[0] += fold(logit * updated)
    sums_ref[3] += fold(grad * unit)
    sums_ref[4] += fold(grad)
    back = normalize_back(unit, r2_ref[part, 0:1], grad * vec_ref[3:4, :])
    gsec_ref[part, :] = back
    b2_ref[part, :] = back.astype(BF16)


def feed_back(b2_ref, dg_ref, win_ref, whid_ref, inner_ref, b1_ref, acc_ref):
    rows = b2_ref.shape[0]
    for cols in chunks(dg_ref.shape[1], BLOCK):
        inner_ref[...] = dot(b2_ref[...], whid_ref[cols, :], 1, 1)
        for part in chunks(rows, ROWS):
            b1_ref[part, cols] = (inner_ref[part, :] * dg_ref[part, cols].astype(F32)).astype(BF16)
    total = None
    for cols in chunks(dg_ref.shape[1], BLOCK):
        value = dot(b1_ref[:, cols], matrix(win_ref, cols.start // BLOCK), 1, 1)
        total = value if total is None else total + value
    acc_ref[...] = total


def middle_back(gsec_ref, acc_ref, vec_ref, n1_ref, r1_ref, b0_ref, base_ref, sums_ref):
    for part in chunks(gsec_ref.shape[0], ROWS):
        grad = gsec_ref[part, :] + acc_ref[part, :]
        unit = n1_ref[part, :]
        sums_ref[1] += fold(grad * unit)
        sums_ref[2] += fold(grad)
        back = normalize_back(unit, r1_ref[part, 0:1], grad * vec_ref[1:2, :])
        base_ref[part, :] += back
        b0_ref[part, :] = back.astype(BF16)


def attend_back(
    pairs, g2_ref, q2_ref, k_ref, v_ref, p_ref, ctx_ref, ds_ref, dq2_ref, dqkv_ref, doth_ref
):
    rows, width = ctx_ref.shape
    for pair in pairs:
        cols = slice(pair * LANES, (pair + 1) * LANES)
        for part in chunks(2 * rows, 2 * rows):
            grad = g2_ref[pair, part, :]
            both = jnp.concatenate([ctx_ref[:, cols]] * 2, axis=0)
            delta = jnp.sum(grad.astype(F32) * both.astype(F32), axis=-1, keepdims=True)
            back = dot(grad, v_ref[:, cols], 1, 1)
            low = (p_ref[pair, part, :].astype(F32) * (back - delta)).astype(BF16)
            ds_ref[part, :] = low
            dq2_ref[part, :] = dot(low, k_ref[:, cols])
        for part in chunks(rows, ATT_ROWS):
            first = head_mask(part.stop - part.start)
            second = dq2_ref[rows + part.start : rows + part.stop, :]
            dqkv_ref[part, cols] = (
                jnp.where(first, dq2_ref[part, :], second) * HD**-0.5
            ).astype(BF16)
        for index, (left, right) in enumerate(
            ((ds_ref[...], q2_ref[pair]), (p_ref[pair], g2_ref[pair]))
        ):
            both = dot(right, left, 0, 0).T.astype(BF16)
            at = index * width + pair * LANES
            dqkv_ref[:, width + at : width + at + LANES] = both[:rows]
            doth_ref[:, at : at + LANES] = both[rows:]


def inputs_back(dqkv_ref, doth_ref, wa_ref, base_ref, gs_ref, goth_ref):
    width = base_ref.shape[1]
    parts = [slice(index * width, (index + 1) * width) for index in range(3)]
    total = base_ref[...]
    for index, cols in enumerate(parts):
        total = total + dot(dqkv_ref[:, cols], matrix(wa_ref, index), 1, 1)
    gs_ref[...] = total
    total = dot(doth_ref[:, parts[0]], matrix(wa_ref, 1), 1, 1)
    goth_ref[...] = (total + dot(doth_ref[:, parts[1]], matrix(wa_ref, 2), 1, 1)).astype(BF16)


def fetch(pieces, cores, bits, start, store, me_ref):
    line, place_in = me_ref[0] // 8, me_ref[0] % 8
    for piece, core, bit in zip(pieces, cores, bits):
        for z in range(piece.shape[0]):
            store(piece, z, line ^ (start + z), place_in ^ (bit | core))


def embed_kernel(place_ref, sizes_ref, tok_ref, got_ref, own_ref, x_ref, rown_ref, sig_ref, segq_ref, segk_ref):
    mine, place_in, group = place_ref[1], place_ref[2], place_ref[3]
    local = tok_ref.shape[0]
    half = x_ref.shape[1] // 2
    ends, starts, total = [], [], 0
    for index in range(sizes_ref.shape[1]):
        starts.append(total)
        total = total + sizes_ref[mine, index]
        ends.append(total)
    ones = jnp.exp(
        lax.broadcasted_iota(jnp.int32, (8, half), 1).astype(F32)
        * (-jnp.log(jnp.full((8, half), 10000.0, F32)) / max(half - 1, 1))
    )
    rates = ones[0:1, :]
    first_sin, first_cos = jnp.sin(rates), jnp.cos(rates)
    for part in chunks(x_ref.shape[0], ROWS):
        size = part.stop - part.start
        block = mine * group + place_in
        block = block if part.start < local else block ^ group
        at = block * local + part.start % local
        token = at + lax.broadcasted_iota(jnp.int32, (size, LANES), 0)
        segment = jnp.zeros((size, LANES), jnp.int32)
        begin = jnp.zeros((size, LANES), jnp.int32)
        for start, end in zip(starts, ends):
            segment = segment + jnp.where(token >= end, 1, 0)
            begin = jnp.maximum(begin, jnp.where(token >= start, start, 0))
        segq_ref[part, :] = segment
        angles = (token - begin).astype(F32)[:, 0:1] * rates
        if part.start < local:
            low = tok_ref[part, :]
        else:
            low = got_ref[part.start - local : part.stop - local, :]
        own_ref[part, :] = low
        for cols, moving, still, step in (
            (slice(0, half), jnp.sin(angles), 0.0, first_sin),
            (slice(half, 2 * half), jnp.cos(angles), 1.0, first_cos),
        ):
            inputs = low[:, cols].astype(F32) + (moving + still)
            x_ref[part, cols] = inputs
            rown_ref[part, cols] = inputs.astype(BF16)
            sig_ref[part, cols] = moving + step
    blocks = segk_ref.shape[1] // local
    for index in range(blocks):
        peer = mine * group + (place_in ^ (index // 2))
        peer = peer if index % 2 == 0 else peer ^ group
        token = peer * local + lax.broadcasted_iota(jnp.int32, (8, local), 1)
        segment = jnp.zeros((8, local), jnp.int32)
        for end in ends:
            segment = segment + jnp.where(token >= end, 1, 0)
        segk_ref[:, index * local : (index + 1) * local] = segment


def pull(sources, sems):
    copies = [
        pltpu.make_async_copy(source, target, sems.at[index]) for index, (source, target) in enumerate(sources)
    ]
    for copy in copies:
        copy.start()
    return copies


def sort_rows(place_ref, tok_ref, cot_ref, halt_ref, refs, sems):
    mine = place_ref[1]
    width = tok_ref.shape[2]
    send_ref, own_ref, flip_ref, flags_ref = refs
    moves = [(halt_ref, flags_ref)]
    for micro, target in ((1 - mine, send_ref), (mine, own_ref)):
        moves.append((tok_ref.at[micro], target.at[:, :width]))
        moves.append((cot_ref.at[micro], target.at[:, width : 2 * width]))
    copies = pull(moves, sems)
    flip_ref[...] = jnp.zeros_like(flip_ref)
    for copy in copies:
        copy.wait()
    for target, micro in ((own_ref, mine), (send_ref, 1 - mine)):
        for step in range(halt_ref.shape[0]):
            flip_ref[step : step + 1, :] = flags_ref[step, pl.ds(micro, 1), :].astype(F32)
        target[:, 2 * width :] = flip_ref[...].T.astype(BF16)


def sort_kernel(place_ref, tok_ref, cot_ref, halt_ref, *refs):
    sort_rows(place_ref, tok_ref, cot_ref, halt_ref, refs[:4], refs[4])


def pack_kernel(place_ref, tok_ref, cot_ref, halt_ref, q_ref, k_ref, v_ref, o_ref, win_ref, whid_ref, *rest):
    vectors, rest = rest[:VECS], rest[VECS:]
    sorted_refs, (block_ref, tall_ref, flip_ref, flags_ref, turn_ref, low_ref, sems) = rest[:2], rest[2:]
    rows, width = q_ref.shape
    moves = [(vector, low_ref.at[index]) for index, vector in enumerate(vectors)]
    for index, source in enumerate((q_ref, k_ref, v_ref, o_ref)):
        moves.append((source, block_ref.at[index]))
    for index in range(4):
        moves.append((win_ref.at[:, index * BLOCK : (index + 1) * BLOCK], tall_ref.at[index]))
        moves.append((whid_ref.at[index * rows : (index + 1) * rows, :], tall_ref.at[4 + index]))
    copies = pull(moves, sems.at[:17])
    sort_rows(place_ref, tok_ref, cot_ref, halt_ref, [*sorted_refs, flip_ref, flags_ref], sems.at[17:])
    turn_ref[...] = jnp.zeros_like(turn_ref)
    for copy in copies:
        copy.wait()
    for index in range(VECS):
        turn_ref[index : index + 1, :rows] = low_ref[index].astype(F32)
    block_ref[4, :, :LANES] = turn_ref[...].T[:rows, :].astype(BF16)
    block_ref[4, :, LANES:] = jnp.zeros((rows, width - LANES), BF16)


def attend_kernel(
    fast, rown_ref, roth_ref, segq_ref, segk_ref, *rest,
):
    if fast:
        me_ref, plane, rest = rest[0], rest[1:9], rest[9:]
        wa_ref, vec_ref, q2_ref, k_ref, v_ref, p_ref, ctx_ref, q_ref, bias_ref, o_ref = rest

        def store(piece, z, line, place):
            for chunk in range(5):
                wa_ref[chunk, line, place] = piece[z, chunk]

        fetch(plane, (0, 0, 0, 0, 1, 1, 1, 1), (0, 2, 4, 6) * 2, 0, store, me_ref)
        vec_ref[...] = matrix(wa_ref, 4)[:, :LANES].astype(F32).T[0:8, :]
    else:
        wa_ref, q2_ref, k_ref, v_ref, p_ref, ctx_ref, q_ref, bias_ref, o_ref = rest
    set_bias(segq_ref, segk_ref, bias_ref)
    project(rown_ref, roth_ref, wa_ref, q_ref, q2_ref, k_ref, v_ref)
    attend(q2_ref, k_ref, v_ref, bias_ref, p_ref, ctx_ref, o_ref)


def ffn_kernel(
    fast, x_ref, ctx_ref, tok_ref, sig_ref, vec_ref, wa_ref, *rest,
):
    if fast:
        me_ref, near, far, rest = rest[0], rest[1:7], rest[7:11], rest[11:]
        (win_ref, full_ref), rest = rest[:2], rest[2:]
    else:
        (win_ref, whid_ref), rest = rest[:2], rest[2:]
    (
        n1_ref, r1_ref, nlow_ref, hid_ref, dg_ref, n2_ref, r2_ref, rate_ref, state_ref,
        pooled_ref, next_ref, rown_ref, inner_ref, acc_ref,
    ) = rest
    if fast:

        def store(piece, z, line, place):
            for chunk in range(4):
                win_ref[chunk, line, place] = piece[z, chunk]
                full_ref[line, place, chunk] = piece[z, 4 + chunk]

        fetch(near, (0, 0, 0, 1, 1, 1), (0, 2, 4, 0, 2, 4), 0, store, me_ref)
        fetch((far[0], far[2]), (0, 1), (6, 6), 0, store, me_ref)
        fetch((far[1], far[3]), (0, 1), (6, 6), 2, store, me_ref)
        whid_ref = Flat(full_ref)
    width = x_ref.shape[1]
    first_norm(x_ref, ctx_ref, wa_ref, vec_ref, acc_ref, n1_ref, r1_ref, nlow_ref)
    feed_forward(nlow_ref, win_ref, whid_ref, inner_ref, hid_ref, dg_ref, acc_ref)
    for part in chunks(tok_ref.shape[0], ROWS):
        unit, inverse, updated, rate = second_norm(part, vec_ref, n1_ref, acc_ref)
        keep = tok_ref[part, 2 * width : 2 * width + 1].astype(F32)
        n2_ref[part, :] = unit
        r2_ref[part, :] = wide(inverse)
        rate_ref[part, :] = wide(rate)
        pooled_ref[part, :] = (keep * rate) * updated
        state = tok_ref[part, :width].astype(F32)
        state = state + keep * (updated - state)
        state_ref[part, :] = state
        inputs = state + sig_ref[part, :]
        next_ref[part, :] = inputs
        rown_ref[part, :] = inputs.astype(BF16)


def turn_kernel(
    x_ref, rown_ref, roth_ref, wa_ref, win_ref, whid_ref, vec_ref, segq_ref, segk_ref,
    state_ref, pooled_ref, tok_ref,
    out_ref, gs_ref, goth_ref, nlow_ref, hid_ref, b1_ref, b2_ref, ctx_ref, b0_ref, dqkv_ref, doth_ref, vg_ref,
    q_ref, q2_ref, k_ref, v_ref, p_ref, bias_ref, o_ref, acc_ref, n1_ref, r1_ref, inner_ref, dg_ref,
    n2_ref, r2_ref, rate_ref, gsec_ref, base_ref, sums_ref, gctx_ref, g2_ref, ds_ref,
):
    width = x_ref.shape[1]
    sums_ref[...] = jnp.zeros_like(sums_ref)
    set_bias(segq_ref, segk_ref, bias_ref)
    project(rown_ref, roth_ref, wa_ref, q_ref, q2_ref, k_ref, v_ref)
    attend(q2_ref, k_ref, v_ref, bias_ref, p_ref, ctx_ref, o_ref)
    first_norm(x_ref, ctx_ref, wa_ref, vec_ref, acc_ref, n1_ref, r1_ref, nlow_ref)
    feed_forward(nlow_ref, win_ref, whid_ref, inner_ref, hid_ref, dg_ref, acc_ref)
    for part in chunks(x_ref.shape[0], ROWS):
        unit, inverse, updated, rate = second_norm(part, vec_ref, n1_ref, acc_ref)
        keep = tok_ref[part, 2 * width + 1 : 2 * width + 2].astype(F32)
        n2_ref[part, :] = unit
        r2_ref[part, :] = wide(inverse)
        rate_ref[part, :] = wide(rate)
        state = state_ref[part, :]
        state = state + keep * (updated - state)
        out_ref[part, :] = state + (pooled_ref[part, :] + (keep * rate) * updated)
        cot = tok_ref[part, width : 2 * width].astype(F32)
        tail_back(
            part, 1, cot, cot, tok_ref, vec_ref, n2_ref, r2_ref, rate_ref, b2_ref, gsec_ref, base_ref,
            sums_ref,
        )
    feed_back(b2_ref, dg_ref, win_ref, whid_ref, inner_ref, b1_ref, acc_ref)
    middle_back(gsec_ref, acc_ref, vec_ref, n1_ref, r1_ref, b0_ref, base_ref, sums_ref)
    gctx_ref[...] = dot(b0_ref[...], matrix(wa_ref, 3), 1, 1).astype(BF16)
    split_heads(gctx_ref, g2_ref)
    pairs = range(q2_ref.shape[0])
    attend_back(pairs, g2_ref, q2_ref, k_ref, v_ref, p_ref, ctx_ref, ds_ref, o_ref, dqkv_ref, doth_ref)
    inputs_back(dqkv_ref, doth_ref, wa_ref, base_ref, gs_ref, goth_ref)
    vg_ref[...] = jnp.zeros_like(vg_ref)
    for index in range(VECS):
        vg_ref[index : index + 1, :] = jnp.sum(sums_ref[index], axis=0, keepdims=True)


def place(fast, me_ref, value, scratch_ref, outs, at):
    cols = slice(at, at + value.shape[1])
    if not fast:
        outs[0][:, cols] = value
        return
    scratch_ref[:, :, :, : value.shape[1]] = value.reshape(scratch_ref.shape[:3] + value.shape[1:])
    for relative in range(8):
        block = scratch_ref[:, relative ^ (me_ref[0] % 8), :, : value.shape[1]].astype(BF16)
        outs[relative % 2][relative // 2, :, :, cols] = block


def hidden_back_kernel(
    fast, me_ref, gs_ref, more_ref, tok_ref, vec_ref,
    n2_ref, r2_ref, rate_ref, hid_ref, hid1_ref, b21_ref,
    b2_ref, gsec_ref, base_ref, sums_ref,
    *rest,
):
    outs, tall_ref = rest[:-1], rest[-1]
    sums_ref[...] = jnp.zeros_like(sums_ref)
    width = gs_ref.shape[1]
    for part in chunks(gs_ref.shape[0], ROWS):
        tail_back(
            part, 0, gs_ref[part, :] + more_ref[part, :].astype(F32),
            tok_ref[part, width : 2 * width].astype(F32), tok_ref, vec_ref,
            n2_ref, r2_ref, rate_ref, b2_ref, gsec_ref, base_ref, sums_ref,
        )
    hidden_rows = hid_ref.shape[1] // 4
    for z in range(4):
        span = slice(z * hidden_rows, (z + 1) * hidden_rows)
        value = dot(hid_ref[:, span], b2_ref[...], 0, 0) + dot(hid1_ref[:, span], b21_ref[...], 0, 0)
        if fast:
            tall_ref[...] = value.reshape(tall_ref.shape)
            for relative in range(8):
                block = tall_ref[relative ^ (me_ref[0] % 8)].astype(BF16)
                outs[relative % 2][relative // 2, z] = block
        else:
            outs[0][span, :] = value


def feed_back_kernel(
    b2_ref, gsec_ref, base0_ref, sums0_ref, vec_ref, win_ref, whid_ref, wa_ref, n1_ref, r1_ref, dg_ref,
    b1_ref, b0_ref, base_ref, gctx_ref, sums_ref, inner_ref, acc_ref,
):
    sums_ref[...] = sums0_ref[...]
    base_ref[...] = base0_ref[...]
    feed_back(b2_ref, dg_ref, win_ref, whid_ref, inner_ref, b1_ref, acc_ref)
    middle_back(gsec_ref, acc_ref, vec_ref, n1_ref, r1_ref, b0_ref, base_ref, sums_ref)
    gctx_ref[...] = dot(b0_ref[...], matrix(wa_ref, 3), 1, 1).astype(BF16)


def weights_back_kernel(
    fast, me_ref, b1_ref, b0_ref, sums_ref, nlow_ref, ctx_ref, nlow1_ref, b11_ref, ctx1_ref, b01_ref, vg1_ref,
    *rest,
):
    outs, (whole_ref, flip_ref) = rest[:-2], rest[-2:]
    width = ctx_ref.shape[1]
    for cols in chunks(b1_ref.shape[1], BLOCK):
        value = dot(nlow_ref[...], b1_ref[:, cols], 0, 0) + dot(nlow1_ref[...], b11_ref[:, cols], 0, 0)
        place(fast, me_ref, value, whole_ref, outs, cols.start)
    value = dot(ctx_ref[...], b0_ref[...], 0, 0) + dot(ctx1_ref[...], b01_ref[...], 0, 0)
    at = b1_ref.shape[1]
    place(fast, me_ref, value, whole_ref, outs, at)
    flip_ref[...] = jnp.zeros_like(flip_ref)
    flip_ref[0:8, :] = vg1_ref[...]
    for index in range(VECS):
        flip_ref[index : index + 1, :] += jnp.sum(sums_ref[index], axis=0, keepdims=True)
    place(fast, me_ref, flip_ref[...].T, whole_ref, outs, at + width)


def heads_back_kernel(
    gctx_ref, q2_ref, k_ref, v_ref, p_ref, ctx_ref, dqkv_ref, doth_ref, g2_ref, ds_ref, dq2_ref
):
    split_heads(gctx_ref, g2_ref)
    pairs = range(q2_ref.shape[0])
    attend_back(pairs, g2_ref, q2_ref, k_ref, v_ref, p_ref, ctx_ref, ds_ref, dq2_ref, dqkv_ref, doth_ref)


def project_back_kernel(
    fast, me_ref, base_ref, wa_ref,
    rown_ref, roth_ref, rown1_ref, roth1_ref, dqkv1_ref, doth1_ref, dqkv_ref, doth_ref,
    gs_ref, goth_ref,
    *rest,
):
    outs, whole_ref = rest[:-1], rest[-1]
    width = base_ref.shape[1]
    for index in range(3):
        cols = slice(index * width, (index + 1) * width)
        value = dot(rown_ref[...], dqkv_ref[:, cols], 0, 0) + dot(
            rown1_ref[...], dqkv1_ref[:, cols], 0, 0
        )
        if index:
            other = slice((index - 1) * width, index * width)
            value = (
                value
                + dot(roth_ref[...], doth_ref[:, other], 0, 0)
                + dot(roth1_ref[...], doth1_ref[:, other], 0, 0)
            )
        place(fast, me_ref, value, whole_ref, outs, cols.start)
    inputs_back(dqkv_ref, doth_ref, wa_ref, base_ref, gs_ref, goth_ref)


def stack_kernel(*refs):
    *parts, out_ref, sems = refs
    for copy in pull([(part, out_ref.at[index]) for index, part in enumerate(parts)], sems):
        copy.wait()


def halves_kernel(by_y_ref, by_x_ref, low_ref, high_ref, sems):
    half = low_ref.shape[0]
    moves = [(by_y_ref.at[pl.ds(0, half)], low_ref), (by_x_ref.at[pl.ds(half, half)], high_ref)]
    for copy in pull(moves, sems):
        copy.wait()


def return_kernel(info_ref, out_ref, in_ref, back_ref, out_both_ref, in_both_ref):
    local, width = back_ref.shape[0], out_ref.shape[1]
    for own_ref, target, cols in (
        (out_ref, out_both_ref, slice(0, width)),
        (in_ref, in_both_ref, slice(width, 2 * width)),
    ):
        target[info_ref[1]] = own_ref[:local, :]
        target[1 - info_ref[1]] = back_ref[:, cols].astype(F32)


def send_kernel(own_ref, more_ref, out_ref, total_ref, back_ref):
    local, width = back_ref.shape[0], own_ref.shape[1]
    for part in chunks(own_ref.shape[0], ROWS):
        total = own_ref[part, :] + more_ref[part, :].astype(F32)
        total_ref[part, :] = total
        if part.start >= local:
            target = slice(part.start - local, part.stop - local)
            back_ref[target, :width] = out_ref[part, :].astype(BF16)
            back_ref[target, width:] = total.astype(BF16)


def add_core_kernel(keep_ref, got_ref, s11a_ref, s11b_ref, s10_ref, s01_ref, s00_ref):
    half = s11a_ref.shape[0]
    for z in range(keep_ref.shape[1]):
        for index, target in ((0, s00_ref), (1, s01_ref), (2, s10_ref)):
            total = keep_ref[index, z].astype(F32) + got_ref[index, z].astype(F32)
            target[z] = total.astype(BF16)
        total = (keep_ref[3, z].astype(F32) + got_ref[3, z].astype(F32)).astype(BF16)
        if z < half:
            s11a_ref[z] = total
        else:
            s11b_ref[z - half] = total


def beside(target_ref, z, values, rows, width):
    for index in range(values.shape[0] // rows):
        target_ref[z, :, index * width : (index + 1) * width] = values[index * rows : (index + 1) * rows]


def add_half_kernel(a10_ref, ax_ref, a01_ref, ay_ref, b10_ref, bx_ref, b01_ref, by_ref, o10_ref, o01_ref):
    half = ax_ref.shape[0]
    rows, width = b10_ref.shape[1], a10_ref.shape[2]
    at = a10_ref.shape[1] // rows * width
    for z in range(2 * half):
        for tall_ref, tall_got_ref, low_ref, got_ref, out_ref, first in (
            (a10_ref, ax_ref, b10_ref, bx_ref, o10_ref, 0),
            (a01_ref, ay_ref, b01_ref, by_ref, o01_ref, half),
        ):
            if first <= z < first + half:
                tall = (tall_ref[z].astype(F32) + tall_got_ref[z - first].astype(F32)).astype(BF16)
                low = (low_ref[z].astype(F32) + got_ref[z - first].astype(F32)).astype(BF16)
            else:
                tall, low = tall_ref[z], low_ref[z]
            beside(out_ref, z, tall, rows, width)
            out_ref[z, :, at:] = low


def add_both_kernel(info_ref, a_ref, b_ref, got_x_ref, got_y_ref, own_ref, near_ref, next_ref, far_ref):
    line = info_ref[0] // 8
    rows, width = b_ref.shape[1], a_ref.shape[2]
    count = a_ref.shape[1] // rows
    for z, out_ref in enumerate((own_ref, near_ref, next_ref, far_ref)):
        at = line ^ z
        for index in range(count + 1):
            if index < count:
                cols = slice(index * width, (index + 1) * width)
                own = a_ref[at, index * rows : (index + 1) * rows]
            else:
                cols = slice(count * width, got_x_ref.shape[2])
                own = b_ref[at]
            total = own.astype(F32) + got_x_ref[at, :, cols].astype(F32) + got_y_ref[at, :, cols].astype(F32)
            out_ref[:, cols] = total.astype(BF16)


def add_pair_kernel(own_ref, got_ref, sum_ref):
    sum_ref[...] = (own_ref[...].astype(F32) + got_ref[...].astype(F32)).astype(BF16)


def add_core_all_kernel(keep_ref, got_ref, *outs):
    for z in range(keep_ref.shape[1]):
        for index, target in enumerate(outs):
            target[z] = (keep_ref[index, z].astype(F32) + got_ref[index, z].astype(F32)).astype(BF16)


def add_four_kernel(info_ref, a_ref, b_ref, c_ref, d_ref, own_ref, near_ref, next_ref, far_ref):
    line = info_ref[0] // 8
    for z, out_ref in enumerate((own_ref, near_ref, next_ref, far_ref)):
        at = line ^ z
        total = a_ref[at].astype(F32) + b_ref[at].astype(F32) + c_ref[at].astype(F32)
        out_ref[...] = (total + d_ref[at].astype(F32)).astype(BF16)


def end_both_kernel(own_ref, got_ref, far_ref, tall_ref, win_ref, wo_ref, *rest):
    vectors, flip_ref = rest[:-1], rest[-1]
    rows, width = far_ref.shape[0], tall_ref.shape[1]

    def total(cols):
        return own_ref[:, cols].astype(F32) + got_ref[:, cols].astype(F32) + far_ref[:, cols].astype(F32)

    at = tall_ref.shape[0] // rows * width
    for index in range(tall_ref.shape[0] // rows):
        tall_ref[index * rows : (index + 1) * rows, :] = total(slice(index * width, (index + 1) * width))
    for out in (win_ref, wo_ref):
        out[...] = total(slice(at, at + out.shape[1]))
        at = at + out.shape[1]
    flip_ref[...] = jnp.zeros_like(flip_ref)
    flip_ref[:rows, :] = total(slice(at, at + LANES))
    turned = flip_ref[...].T
    for index, vector in enumerate(vectors):
        vector[...] = turned[index : index + 1, :rows]


def end_kernel(own_ref, got_ref, far_ref, *outs):
    at = 0
    for out in outs:
        cols = slice(at, at + out.shape[1])
        out[...] = own_ref[:, cols].astype(F32) + got_ref[:, cols].astype(F32) + far_ref[:, cols].astype(F32)
        at = at + out.shape[1]


def vm():
    return pl.BlockSpec(memory_space=pltpu.VMEM)


def run(kernel, ins, outs, scratch=(), scalars=(), loose=(), pinned=(), far=(), sems=0, micros=0.05):
    specs = [vm() for _ in ins]
    for index in scalars:
        specs[index] = pl.BlockSpec(memory_space=pltpu.SMEM)
    ins = list(ins)
    for index in loose:
        specs[index] = pl.BlockSpec(memory_space=pl.ANY)
    for index in pinned:
        specs[index] = pl.BlockSpec(memory_space=pltpu.HBM)
        ins[index] = pltpu.with_memory_space_constraint(ins[index], pltpu.HBM)
    size = sum(v.size * v.dtype.itemsize for v in ins) + sum(
        functools.reduce(lambda a, b: a * b, s, 1) * jnp.dtype(t).itemsize for s, t in outs
    )
    buffers = [pltpu.VMEM(s, t) for s, t in scratch]
    need = sum(functools.reduce(lambda a, b: a * b, s, 1) * jnp.dtype(t).itemsize for s, t in scratch)
    if sems:
        buffers.append(pltpu.SemaphoreType.DMA((sems,)))
    return pl.pallas_call(
        kernel,
        out_shape=[jax.ShapeDtypeStruct(s, t) for s, t in outs],
        in_specs=specs,
        out_specs=[pl.BlockSpec(memory_space=pl.ANY) if index in far else vm() for index in range(len(outs))],
        scratch_shapes=buffers,
        compiler_params=pltpu.CompilerParams(vmem_limit_bytes=max(need + 8 * MIB, SCOPED)),
        cost_estimate=pl.CostEstimate(
            flops=int(micros * MICRO), bytes_accessed=size, transcendentals=0
        ),
    )(*ins)


AXES = ("dp", "head")


def after(value, *others):
    return lax.optimization_barrier((value, *others))[0]


class Links:
    def __init__(self, model_rows):
        self.heads = lax.axis_size("head")
        self.pods = lax.axis_size("dp")
        self.count = self.heads * self.pods
        self.fast = self.heads == 4 and self.pods == 8 and model_rows == 16
        self.head = lax.axis_index("head")
        self.me = lax.axis_index("dp") * self.heads + self.head

    def flip(self, value, bit):
        return lax.ppermute(value, AXES, [(i, i ^ bit) for i in range(self.count)])

    def flip_head(self, value, bit):
        return lax.ppermute(value, "head", [(i, i ^ bit) for i in range(self.heads)])

    def along_z(self, block):
        return [block, *(self.flip(block, 8 * k) for k in (1, 2, 3))]

    def stack(self, parts):
        (out,) = run(
            stack_kernel, parts, [((4, *parts[0].shape), BF16)], loose=range(4), far=(0,), sems=4
        )
        return out

    def core_sums(self, keep, got):
        block = keep.shape[2:]
        whole, half = ((4, *block), BF16), ((2, *block), BF16)
        return run(add_core_kernel, [keep, got], [half, half, whole, whole, whole])

    def line_first(self, kernel, parts, shape):
        own, near, following, far = run(kernel, [self.info, *parts], [(shape, BF16)] * 4, scalars=(0,))
        return own, far, self.flip(near, 8), self.flip(following, 8)

    def line_last(self, own, far, got, got_far):
        (far,) = run(add_pair_kernel, [after(far, got), got_far], [(far.shape, BF16)])
        return own, got, self.flip(far, 24)

    def spread(self, own, group):
        held, bit = own[None], 1
        while bit < group:
            got = self.flip_head(held, bit)
            held = got if bit == 1 and group == 2 else jnp.concatenate([held, got], axis=0)
            bit = bit * 2
        if group > 2:
            held = held[1:]
        return held.reshape(-1, own.shape[1])

    def collapse(self, parts, group, rows):
        if group == 2:
            return self.flip_head(parts, 1)
        held = parts.reshape(group - 1, rows, -1)
        held = jnp.concatenate([jnp.zeros_like(held[:1]), held], axis=0).astype(F32)
        bit = group // 2
        while bit >= 1:
            held = held[:bit] + self.flip_head(held[bit : 2 * bit], bit)
            bit = bit // 2
        return held[0]


def body(
    tokens, cotangent, lengths, halting, w_query, w_key, w_value, w_out, w_in, w_hidden,
    w_halt, gain_attn, shift_attn, gain_ffn, shift_ffn,
):
    micro, local, width = tokens.shape
    links = Links(w_query.shape[0])
    fast, heads = links.fast, links.heads
    group = heads // micro
    rows, length = micro * local, local * heads
    mine = links.head // group
    wide_ff = w_in.shape[1]
    fine = width // links.count
    matrices = (w_query, w_key, w_value, w_out, w_in, w_hidden)
    vectors = (w_halt, gain_attn, shift_attn, gain_ffn, shift_ffn)
    place_array = jnp.stack([links.me, mine, links.head % group, jnp.int32(group)]).astype(jnp.int32)
    links.info = place_array

    pairs = width // LANES
    row_f, row_b = ((rows, width), F32), ((rows, width), BF16)
    stat = ((rows, LANES), F32)
    others = length - rows
    long_b = ((length, width), BF16)
    q2_t = ((pairs, 2 * rows, LANES), BF16)
    p_t = ((pairs, 2 * rows, length), BF16)
    o_t = ((2 * rows, LANES), F32)
    bias_t = ((rows, length), F32)
    inner_t = ((rows, BLOCK), F32)
    ff_b = ((rows, wide_ff), BF16)
    sums_t = ((VECS, 8, width), F32)
    ds_t = ((2 * rows, length), BF16)
    dqkv_t = ((rows, 3 * width), BF16)
    doth_t = ((others, 2 * width), BF16)
    vg_t = ((8, width), F32)
    segq_t, segk_t = ((rows, LANES), jnp.int32), ((8, length), jnp.int32)

    sort_in = [place_array, tokens, cotangent, halting]
    sort_out = [((local, 2 * width + LANES), BF16)] * 2
    sort_tmp = [((LANES, local), F32), (halting.shape, jnp.int32)]
    if fast:
        send_tok, own_tok, block_a, block_b = run(
            pack_kernel,
            [*sort_in, *matrices, *(vector[None] for vector in vectors)],
            [*sort_out, ((5, fine, BLOCK), BF16), ((8, fine, BLOCK), BF16)],
            [*sort_tmp, ((LANES, LANES), F32), ((VECS, 1, fine), BF16)],
            scalars=(0,),
            pinned=range(1, 15),
            sems=22,
        )
        got_tok = links.flip_head(send_tok, group)
        line_a = links.along_z(block_a)
        own_a = after(links.stack(line_a), got_tok)
        by_x, by_y = links.flip(own_a, 2), links.flip(own_a, 4)
        line_b = links.along_z(after(block_b, line_a[1]))
        plane_a = [own_a, by_x, by_y, links.flip(after(by_y, line_b[3]), 2)]
    else:
        send_tok, own_tok = run(
            sort_kernel, sort_in, sort_out, sort_tmp, scalars=(0,), pinned=(1, 2, 3), sems=5
        )
        full = [lax.all_gather(part, AXES, axis=0, tiled=True) for part in matrices]
        full_v = [lax.all_gather(part, AXES, axis=0, tiled=True) for part in vectors]
        full_a = jnp.stack(full[:4])
        full_in = jnp.transpose(full[4].reshape(width, wide_ff // BLOCK, BLOCK), (1, 0, 2))
        full_hid = full[5]
        vec = jnp.pad(jnp.stack(full_v), ((0, 8 - VECS), (0, 0))).astype(F32)

        got_tok = links.flip_head(send_tok, group)
    tok, x0, rown0, sig1, segq, segk = run(
        embed_kernel,
        [place_array, lengths[:, 0], own_tok, got_tok],
        [((rows, 2 * width + LANES), BF16), row_f, row_b, row_f, segq_t, segk_t],
        scalars=(0, 1),
    )
    roth0 = links.spread(rown0, group)
    if fast:
        own_b = after(links.stack(line_b), by_x, by_y, roth0)
        near = [own_b, links.flip(own_b, 2), links.flip(own_b, 4)]
        near = near + [links.flip(piece, 1) for piece in near]
        halves = run(
            halves_kernel,
            [near[2], near[1]],
            [((2, 8, fine, BLOCK), BF16)] * 2,
            loose=(0, 1),
            far=(0, 1),
            sems=2,
        )
        far_b = [links.flip(halves[0], 2), links.flip(halves[1], 4)]
        plane_a[3] = after(plane_a[3], halves[0])
        plane_a = plane_a + [links.flip(piece, 1) for piece in plane_a]

    attend_in = [rown0, roth0, segq, segk]
    attend_out = [q2_t, long_b, long_b, p_t, row_b]
    if fast:
        full_a, vec, q2, k, v, p, ctx = run(
            functools.partial(attend_kernel, True),
            [*attend_in, links.info, *plane_a],
            [((5, 4, 8, fine, BLOCK), BF16), vg_t, *attend_out],
            [row_b, bias_t, o_t],
            scalars=(4,),
            micros=8,
        )
        full_a = full_a.reshape(5, width, BLOCK)
    else:
        q2, k, v, p, ctx = run(
            functools.partial(attend_kernel, False),
            [*attend_in, full_a],
            attend_out,
            [row_b, bias_t, o_t],
            micros=8,
        )
    ffn_out = [row_f, stat, row_b, ff_b, ff_b, row_f, stat, stat, row_f, row_f, row_f, row_b]
    ffn_in = [x0, ctx, tok, sig1, vec, full_a]
    if fast:
        far_b = [after(piece, ctx) for piece in far_b]
        far_b = far_b + [links.flip(piece, 1) for piece in far_b]
        full_in, full_hid, *got = run(
            functools.partial(ffn_kernel, True),
            [*ffn_in, links.info, *near, *far_b],
            [((4, 4, 8, fine, BLOCK), BF16), ((4, 8, 4, fine, BLOCK), BF16), *ffn_out],
            [inner_t, row_f],
            scalars=(6,),
            micros=5.5,
        )
        full_in = full_in.reshape(4, width, BLOCK)
        full_hid = full_hid.reshape(wide_ff, width)
    else:
        got = run(
            functools.partial(ffn_kernel, False),
            [*ffn_in, full_in, full_hid],
            ffn_out,
            [inner_t, row_f],
            micros=5.5,
        )
    n1, r1, nlow, hid, dg, n2, r2, rate, state, pooled, x1, rown1 = got
    roth1 = links.spread(rown1, group)
    out, gs, goth, nlow1, hid1, b11, b21, ctx1, b01, dqkv1, doth1, vg1 = run(
        turn_kernel,
        [x1, rown1, roth1, full_a, full_in, full_hid, vec, segq, segk, state, pooled, tok],
        [row_f, row_f, ((others, width), BF16), row_b, ff_b, ff_b, row_b, row_b, row_b, dqkv_t, doth_t, vg_t],
        [
            row_b, q2_t, long_b, long_b, p_t, bias_t, o_t, row_f, row_f, stat, inner_t, ff_b,
            row_f, stat, stat, row_f, row_f, sums_t, row_b, q2_t, ds_t,
        ],
        micros=15.7,
    )
    more = links.collapse(goth, group, rows)

    b_cols = wide_ff + width + LANES
    def parts_of(shape, whole):
        return [((4, 4, *shape), BF16)] * 2 if fast else [(whole, F32)]

    hid_out = parts_of((4 * fine, width), (wide_ff, width))
    in_out = parts_of((fine, b_cols), (width, b_cols))
    attend_outs = parts_of((fine, 3 * width), (width, 3 * width))
    whole_shape = (4, 8, fine, BLOCK) if fast else (8, LANES)
    tall_shape = (8, 4 * fine, width) if fast else (8, LANES)
    b2, gsec, base, sums, *hid_parts = run(
        functools.partial(hidden_back_kernel, fast),
        [links.info, gs, more, tok, vec, n2, r2, rate, hid, hid1, b21],
        [row_b, row_f, row_f, sums_t, *hid_out],
        [(tall_shape, F32)],
        scalars=(0,),
        micros=2,
    )
    b1, b0, base, gctx, sums = run(
        feed_back_kernel,
        [b2, gsec, base, sums, vec, full_in, full_hid, full_a, n1, r1, dg],
        [ff_b, row_b, row_f, row_b, sums_t],
        [inner_t, row_f],
        micros=2.2,
    )
    if fast:
        c_sums = links.core_sums(hid_parts[0], links.flip(hid_parts[1], 1))
        b1 = after(b1, c_sums[0])
    in_parts = run(
        functools.partial(weights_back_kernel, fast),
        [links.info, b1, b0, sums, nlow, ctx, nlow1, b11, ctx1, b01, vg1],
        in_out,
        [(whole_shape, F32), ((LANES, width), F32)],
        scalars=(0,),
        micros=2,
    )
    if fast:
        b_sums = links.core_sums(in_parts[0], links.flip(in_parts[1], 1))
        gctx = after(gctx, b_sums[0])
    dqkv0, doth0 = run(
        heads_back_kernel,
        [gctx, q2, k, v, p, ctx],
        [dqkv_t, doth_t],
        [q2_t, ds_t, o_t],
        micros=3,
    )
    if fast:
        c11a, c11b, c10, c01, c00 = c_sums
        b11a, b11b, b10, b01, b00 = b_sums
        halves = [
            after(c10, dqkv0), links.flip(c11a, 2), c01, links.flip(c11b, 4),
            b10, links.flip(b11a, 2), b01, links.flip(b11b, 4),
        ]
        both_t = ((4, fine, 4 * width + b_cols), BF16)
        both10, both01 = run(add_half_kernel, halves, [both_t] * 2)
        dqkv0 = after(dqkv0, both01)
    g0, goth0, *attend_parts = run(
        functools.partial(project_back_kernel, fast),
        [links.info, base, full_a, rown0, roth0, rown1, roth1, dqkv1, doth1, dqkv0, doth0],
        [row_f, ((others, width), BF16), *attend_outs],
        [(whole_shape, F32)],
        scalars=(0,),
        micros=4,
    )
    inputs, back = run(
        send_kernel,
        [g0, links.collapse(goth0, group, rows), out],
        [row_f, ((local, 2 * width), BF16)],
    )
    if fast:
        keep, got = after(attend_parts[0], back), links.flip(attend_parts[1], 1)
        a00, a01, a10, a11 = run(add_core_all_kernel, [keep, got], [(keep.shape[1:], BF16)] * 4)
        by_plane = [a00, links.flip(a11, 6), links.flip(a01, 2), links.flip(a10, 4)]
        both = links.line_first(
            add_both_kernel, [after(c00, a00), b00, links.flip(both01, 2), links.flip(both10, 4)], both_t[0][1:]
        )
        first_sums = both[0]
        by_plane[0] = after(by_plane[0], both[0])
        attend_sums = links.line_first(add_four_kernel, by_plane, a00.shape[1:])
        both = links.line_last(both[0], after(both[1], attend_sums[0]), *both[2:])
        attend_sums = links.line_last(*attend_sums)
        back = after(back, first_sums)
        output, input_grad = run(
            return_kernel,
            [links.info, out, inputs, links.flip_head(back, group)],
            [((micro, local, width), F32)] * 2,
            scalars=(0,),
        )
        g_hidden, g_in, g_out, *g_vectors = run(
            end_both_kernel,
            [after(both[0], output), *both[1:]],
            [((4 * fine, width), F32), ((fine, wide_ff), F32), ((fine, width), F32)] + [((1, fine), F32)] * VECS,
            [((LANES, LANES), F32)],
        )
        g_query, g_key, g_value = run(
            end_kernel,
            [after(attend_sums[0], output, g_hidden), *attend_sums[1:]],
            [((fine, width), F32)] * 3,
        )
        g_vectors = [vector.reshape(fine) for vector in g_vectors]
    else:
        sums = [
            *(attend_parts[0][:, index * width : (index + 1) * width] for index in range(3)),
            in_parts[0][:, wide_ff : wide_ff + width], in_parts[0][:, :wide_ff], hid_parts[0],
            in_parts[0][:, wide_ff + width :],
        ]
        sums = [lax.psum_scatter(part, AXES, scatter_dimension=0, tiled=True) for part in sums]
        g_query, g_key, g_value, g_out, g_in, g_hidden, g_vec = sums
        g_vectors = [g_vec[:, index] for index in range(VECS)]
        output, input_grad = run(
            return_kernel,
            [links.info, out, inputs, links.flip_head(back, group)],
            [((micro, local, width), F32)] * 2,
            scalars=(0,),
        )
    return (output, input_grad, g_query, g_key, g_value, g_out, g_in, g_hidden, *g_vectors)


def solution(mesh):
    whole = P(("dp", "head"))
    matrix = P(("dp", "head"), None)
    rows = P(None, ("dp", "head"), None)
    return jax.shard_map(
        body,
        mesh=mesh,
        in_specs=(rows, rows, P(None, "dp", None), P(None, None, ("dp", "head")))
        + (matrix,) * 6
        + (whole,) * 5,
        out_specs=(rows, rows) + (matrix,) * 6 + (whole,) * 5,
        check_vma=False,
    )
```

profile of v0, /device:TPU:0, one launch (start us, length us, event | category | flops | bytes accessed | tf_op | source)
XLA Modules:
  0.0 145.0 jit_solution(1777972976962533405)
XLA Ops:
  0.7 2.2 %shard_map.246 = (bf16[128,1152]{1,0:T(8,128)(2,1)S(1)}, bf16[128,1152]{1,0:T(8,128)(2,1)S(1)}, bf16[5,16,512]{2,1,0:T(8,128)(2,1)S(1)}, bf16[8,16,512]{2,1,0:T(8,128)(2,1)S(1)}) custom-call(s32[4]{0:T(128)S(1)} %pad_add_fusion.place_ref.rest_0_.me_ref.info_ref, bf16[2,128,512]{2,1,0:T(8,128)(2,1)} %tok_ref.1, bf16[2,128,512]{2,1,0:T(8,128)(2,1)} %cot_ref.1, ...), custom_call_target="tpu_custom_call" | custom-call | flops 57500000 | bytes 1525936 | tf_op jit(solution)/shard_map/pallas_call | solution.py:707
  3.0 3.0 %collective-permute-start = (bf16[128,1152]{1,0:T(8,128)(2,1)S(1)}, bf16[128,1152]{1,0:T(8,128)(2,1)S(1)}, u32[]{:S(2)}, u32[]{:S(2)}) collective-permute-start(bf16[128,1152]{1,0:T(8,128)(2,1)S(1)} %get-tuple-element.137), channel_id=1, source_target_pairs={{0,2},{1,3},{2,0},{3,1},{4,6},{5,7},{6,4},{7,5},{8,10},{9,11},{10,... | collective-permute-start | bytes 884744 | tf_op jit(solution)/shard_map/ppermute | solution.py:740
  6.0 3.6 %collective-permute-start.4 = (bf16[5,16,512]{2,1,0:T(8,128)(2,1)S(1)}, bf16[5,16,512]{2,1,0:T(8,128)(2,1)S(1)}, u32[]{:S(2)}, u32[]{:S(2)}) collective-permute-start(bf16[5,16,512]{2,1,0:T(8,128)(2,1)S(1)} %get-tuple-element.142.refs_0_), channel_id=1, source_target_pairs={{0,24},{1,25},{2,26},{3,27},{4,28},{5,29},{6,30},{7,31},{8,16},{9,... | collective-permute-start | bytes 245768 | tf_op jit(solution)/shard_map/ppermute | solution.py:737
  9.6 0.8 collective-permute-start.2
  10.4 2.8 %collective-permute-done.4.refs_3_ = bf16[5,16,512]{2,1,0:T(8,128)(2,1)S(1)} collective-permute-done((bf16[5,16,512]{2,1,0:T(8,128)(2,1)S(1)}, bf16[5,16,512]{2,1,0:T(8,128)(2,1)S(1)}, u32[]{:S(2)}, u32[]{:S(2)}) %collective-permute-start.4) | collective-permute-done | bytes 81952 | tf_op jit(solution)/shard_map/ppermute | solution.py:737
  13.2 3.0 %collective-permute-done.3.refs_2_ = bf16[5,16,512]{2,1,0:T(8,128)(2,1)S(1)} collective-permute-done((bf16[5,16,512]{2,1,0:T(8,128)(2,1)S(1)}, bf16[5,16,512]{2,1,0:T(8,128)(2,1)S(1)}, u32[]{:S(2)}, u32[]{:S(2)}) %collective-permute-start.3) | collective-permute-done | bytes 81952 | tf_op jit(solution)/shard_map/ppermute | solution.py:737
  16.7 1.6 %collective-permute-start.6 = (bf16[4,5,16,512]{3,2,1,0:T(8,128)(2,1)S(1)}, bf16[4,5,16,512]{3,2,1,0:T(8,128)(2,1)S(1)}, u32[]{:S(2)}, u32[]{:S(2)}) collective-permute-start(bf16[4,5,16,512]{3,2,1,0:T(8,128)(2,1)S(1)} %shard_map.248.rest_1_), channel_id=1, source_target_pairs={{0,4},{1,5},{2,6},{3,7},{4,0},{5,1},{6,2},{7,3},{8,12},{9,13},{10,... | collective-permute-start | bytes 983048 | tf_op jit(solution)/shard_map/ppermute | solution.py:737
  18.2 0.5 collective-permute-start.5
  18.8 0.9 collective-permute-start.10
  19.7 0.7 copy-done
  20.4 1.8 %shard_map.247 = (bf16[256,1152]{1,0:T(8,128)(2,1)S(1)}, f32[256,512]{1,0:T(8,128)S(1)}, bf16[256,512]{1,0:T(8,128)(2,1)S(1)}, f32[256,512]{1,0:T(8,128)S(1)}, s...) custom-call(s32[4]{0:T(128)S(1)} %pad_add_fusion.place_ref.rest_0_.me_ref.info_ref, s32[2,8]{1,0:T(2,128)S(1)} %bitcast.29, ...), custom_call_target="tpu_custom_call" | custom-call | flops 57500000 | bytes 2637904 | tf_op jit(solution)/shard_map/pallas_call | solution.py:707
  22.2 2.3 %collective-permute-start.9 = (bf16[8,16,512]{2,1,0:T(8,128)(2,1)S(1)}, bf16[8,16,512]{2,1,0:T(8,128)(2,1)S(1)}, u32[]{:S(2)}, u32[]{:S(2)}) collective-permute-start(bf16[8,16,512]{2,1,0:T(8,128)(2,1)S(1)} %get-tuple-element.145.refs_0_), channel_id=1, source_target_pairs={{0,8},{1,9},{2,10},{3,11},{4,12},{5,13},{6,14},{7,15},{8,0},{9,1},... | collective-permute-start | bytes 393224 | tf_op jit(solution)/shard_map/ppermute | solution.py:737
  24.6 1.8 %collective-permute-done.10.refs_2_ = bf16[8,16,512]{2,1,0:T(8,128)(2,1)S(1)} collective-permute-done((bf16[8,16,512]{2,1,0:T(8,128)(2,1)S(1)}, bf16[8,16,512]{2,1,0:T(8,128)(2,1)S(1)}, u32[]{:S(2)}, u32[]{:S(2)}) %collective-permute-start.10) | collective-permute-done | bytes 131104 | tf_op jit(solution)/shard_map/ppermute | solution.py:737
  26.4 1.6 %collective-permute-start.7 = (bf16[8,16,512]{2,1,0:T(8,128)(2,1)S(1)}, bf16[8,16,512]{2,1,0:T(8,128)(2,1)S(1)}, u32[]{:S(2)}, u32[]{:S(2)}) collective-permute-start(bf16[8,16,512]{2,1,0:T(8,128)(2,1)S(1)} %get-tuple-element.145.refs_0_), channel_id=1, source_target_pairs={{0,24},{1,25},{2,26},{3,27},{4,28},{5,29},{6,30},{7,31},{8,16},{9,... | collective-permute-start | bytes 393224 | tf_op jit(solution)/shard_map/ppermute | solution.py:737
  28.0 1.2 collective-permute-done.9.refs_1_
  29.1 4.0 %collective-permute-done.7.refs_3_ = bf16[8,16,512]{2,1,0:T(8,128)(2,1)S(1)} collective-permute-done((bf16[8,16,512]{2,1,0:T(8,128)(2,1)S(1)}, bf16[8,16,512]{2,1,0:T(8,128)(2,1)S(1)}, u32[]{:S(2)}, u32[]{:S(2)}) %collective-permute-start.7) | collective-permute-done | bytes 131104 | tf_op jit(solution)/shard_map/ppermute | solution.py:737
  33.1 0.7 shard_map.249.rest_1_
  33.8 1.3 collective-permute-start.12
  35.6 0.8 collective-permute-start.8
  36.5 0.5 collective-permute-start.15
  37.0 11.8 %collective-permute-done.12.by_x_ref.rest_2_ = bf16[4,8,16,512]{3,2,1,0:T(8,128)(2,1)S(1)} collective-permute-done((bf16[4,8,16,512]{3,2,1,0:T(8,128)(2,1)S(1)}, bf16[4,8,16,512]{3,2,1,0:T(8,128)(2,1)S(1)}, u32[]{:S(2)}, u32[]{:S(2)}) %collective-permute-start.12) | collective-permute-done | bytes 524320 | tf_op jit(solution)/shard_map/ppermute | solution.py:737
  49.0 3.6 %collective-permute-done.8.rest_4_ = bf16[4,5,16,512]{3,2,1,0:T(8,128)(2,1)S(1)} collective-permute-done((bf16[4,5,16,512]{3,2,1,0:T(8,128)(2,1)S(1)}, bf16[4,5,16,512]{3,2,1,0:T(8,128)(2,1)S(1)}, u32[]{:S(2)}, u32[]{:S(2)}) %collective-permute-start.8) | collective-permute-done | bytes 327712 | tf_op jit(solution)/shard_map/ppermute | solution.py:737
  52.6 0.5 collective-permute-start.17
  53.1 1.5 %collective-permute-start.20 = (bf16[2,8,16,512]{3,2,1,0:T(8,128)(2,1)S(1)}, bf16[2,8,16,512]{3,2,1,0:T(8,128)(2,1)S(1)}, u32[]{:S(2)}, u32[]{:S(2)}) collective-permute-start(bf16[2,8,16,512]{3,2,1,0:T(8,128)(2,1)S(1)} %get-tuple-element.148), channel_id=1, source_target_pairs={{0,2},{1,3},{2,0},{3,1},{4,6},{5,7},{6,4},{7,5},{8,10},{9,11},{10,... | collective-permute-start | bytes 786440 | tf_op jit(solution)/shard_map/ppermute | solution.py:737
  55.6 3.7 %shard_map.251 = (bf16[5,4,8,16,512]{4,3,2,1,0:T(8,128)(2,1)S(1)}, f32[8,512]{1,0:T(8,128)S(1)}, bf16[4,512,128]{2,1,0:T(8,128)(2,1)S(1)}, bf16[512,512]{1,0:T(8...) custom-call(bf16[256,512]{1,0:T(8,128)(2,1)S(1)} %get-tuple-element.139, ...), custom_call_target="tpu_custom_call" | custom-call | flops 9200000000 | bytes 9863184 | tf_op jit(solution)/shard_map/pallas_call | solution.py:707
  59.3 3.2 %collective-permute-done.21.rest_8_ = bf16[2,8,16,512]{3,2,1,0:T(8,128)(2,1)S(1)} collective-permute-done((bf16[2,8,16,512]{3,2,1,0:T(8,128)(2,1)S(1)}, bf16[2,8,16,512]{3,2,1,0:T(8,128)(2,1)S(1)}, u32[]{:S(2)}, u32[]{:S(2)}) %collective-permute-start.21) | collective-permute-done | bytes 262176 | tf_op jit(solution)/shard_map/ppermute | solution.py:737
  62.5 0.5 collective-permute-start.23
  63.1 1.0 collective-permute-done.22.rest_9_
  64.5 3.7 %shard_map.252 = (bf16[4,4,8,16,512]{4,3,2,1,0:T(8,128)(2,1)S(1)}, bf16[4,8,4,16,512]{4,3,2,1,0:T(8,128)(2,1)S(1)}, f32[256,512]{1,0:T(8,128)S(1)}, f32[256,128]...) custom-call(f32[256,512]{1,0:T(8,128)S(1)} %get-tuple-element.138.x_, ...), custom_call_target="tpu_custom_call" | custom-call | flops 6325000192 | bytes 18563088 | tf_op jit(solution)/shard_map/pallas_call | solution.py:707
  68.4 1.4 collective-permute-done.24
  69.8 10.6 %shard_map.253 = (f32[256,512]{1,0:T(8,128)S(1)}, f32[256,512]{1,0:T(8,128)S(1)}, bf16[256,512]{1,0:T(8,128)(2,1)S(1)}, bf16[256,512]{1,0:T(8,128)(2,1)S(1)}, bf...) custom-call(f32[256,512]{1,0:T(8,128)S(1)} %get-tuple-element.158.x_, ...), custom_call_target="tpu_custom_call" | custom-call | flops 18055000064 | bytes 15450112 | tf_op jit(solution)/shard_map/pallas_call | solution.py:707
  80.6 1.4 collective-permute-done.25.more_ref
  82.0 2.6 %shard_map.254 = (bf16[256,512]{1,0:T(8,128)(2,1)S(1)}, f32[256,512]{1,0:T(8,128)S(1)}, f32[256,512]{1,0:T(8,128)S(1)}, f32[5,8,512]{2,1,0:T(8,128)S(1)}, bf16[4...) custom-call(s32[4]{0:T(128)S(1)} %pad_add_fusion.place_ref.rest_0_.me_ref.info_ref, ...), custom_call_target="tpu_custom_call" | custom-call | flops 2300000000 | bytes 8028176 | tf_op jit(solution)/shard_map/pallas_call | solution.py:707
  84.8 1.7 %shard_map.255 = (bf16[256,2048]{1,0:T(8,128)(2,1)S(1)}, bf16[256,512]{1,0:T(8,128)(2,1)S(1)}, f32[256,512]{1,0:T(8,128)S(1)}, bf16[256,512]{1,0:T(8,128)(2,1)S(1)}, f32[5,8,512]{2,1,0:T(8,128)S(1)}) custom-call(bf16[256,512]{1,0:T(8,128)(2,1)S(1)} %get-tuple-element.173.b2_ref, f32[256,512]{1,0:T(8,128)S(1)} %get-tuple-element.174.gsec_ref, ...), custom_call_target="tpu_custom_call" | custom-call | flops 2529999872 | bytes 12107776 | tf_op jit(solution)/shard_map/pallas_call | solution.py:707
  86.6 0.8 collective-permute-done.26.got_ref
  87.6 2.2 %shard_map.257 = (bf16[4,4,16,2688]{3,2,1,0:T(8,128)(2,1)S(1)}, bf16[4,4,16,2688]{3,2,1,0:T(8,128)(2,1)S(1)}) custom-call(s32[4]{0:T(128)S(1)} %pad_add_fusion.place_ref.rest_0_.me_ref.info_ref, bf16[256,2048]{1,0:T(8,128)(2,1)S(1)} %get-tuple-element.188.b1_ref, bf16[256,512]{1,0:T(8,128)(2,1)S(1)} %get-tuple-element.189.b0_ref, ...), custom_call_target="tpu_custom_call" | custom-call | flops 2300000000 | bytes 6520848 | tf_op jit(solution)/shard_map/pallas_call | solution.py:707
  90.0 0.6 collective-permute-start.28
  91.1 1.9 %collective-permute-done.27.got_ref = bf16[4,4,16,2688]{3,2,1,0:T(8,128)(2,1)S(1)} collective-permute-done((bf16[4,4,16,2688]{3,2,1,0:T(8,128)(2,1)S(1)}, bf16[4,4,16,2688]{3,2,1,0:T(8,128)(2,1)S(1)}, u32[]{:S(2)}, u32[]{:S(2)}) %collective-permute-start.27) | collective-permute-done | bytes 1376288 | tf_op jit(solution)/shard_map/ppermute | solution.py:737
  93.3 0.6 collective-permute-start.30
  93.9 0.5 collective-permute-start.31
  94.5 2.2 %shard_map.259 = (bf16[256,1536]{1,0:T(8,128)(2,1)S(1)}, bf16[256,1024]{1,0:T(8,128)(2,1)S(1)}) custom-call(bf16[256,512]{1,0:T(8,128)(2,1)S(1)} %get-tuple-element.200.gctx_ref, bf16[4,512,128]{2,1,0:T(8,128)(2,1)S(1)} %get-tuple-element.201.q2_ref, bf16[512,512]{1,0:T(8,128)(2,1)S(1)} %get-tuple-element.202.k_ref, ...), custom_call_target="tpu_custom_call" | custom-call | flops 3449999872 | bytes 5505024 | tf_op jit(solution)/shard_map/pallas_call | solution.py:707
  96.7 3.3 %collective-permute-done.31.by_ref = bf16[2,16,2688]{2,1,0:T(8,128)(2,1)S(1)} collective-permute-done((bf16[2,16,2688]{2,1,0:T(8,128)(2,1)S(1)}, bf16[2,16,2688]{2,1,0:T(8,128)(2,1)S(1)}, u32[]{:S(2)}, u32[]{:S(2)}) %collective-permute-start.31) | collective-permute-done | bytes 172064 | tf_op jit(solution)/shard_map/ppermute | solution.py:737
  100.3 3.2 %shard_map.261 = (f32[256,512]{1,0:T(8,128)S(1)}, bf16[256,512]{1,0:T(8,128)(2,1)S(1)}, bf16[4,4,16,1536]{3,2,1,0:T(8,128)(2,1)S(1)}, bf16[4,4,16,1536]{3,2,1,0:T(8,128)(2,1)S(1)}) custom-call(s32[4]{0:T(128)S(1)} %pad_add_fusion.place_ref.rest_0_.me_ref.info_ref, f32[256,512]{1,0:T(8,128)S(1)} %get-tuple-element.180.base_ref, ...), custom_call_target="tpu_custom_call" | custom-call | flops 4600000000 | bytes 9175056 | tf_op jit(solution)/shard_map/pallas_call | solution.py:707
  103.5 0.6 collective-permute-start.35
  104.1 1.5 %collective-permute-start.34 = (bf16[4,16,4736]{2,1,0:T(8,128)(2,1)S(1)}, bf16[4,16,4736]{2,1,0:T(8,128)(2,1)S(1)}, u32[]{:S(2)}, u32[]{:S(2)}) collective-permute-start(bf16[4,16,4736]{2,1,0:T(8,128)(2,1)S(1)} %get-tuple-element.213), channel_id=1, source_target_pairs={{0,2},{1,3},{2,0},{3,1},{4,6},{5,7},{6,4},{7,5},{8,10},{9,11},{10,... | collective-permute-start | bytes 1818632 | tf_op jit(solution)/shard_map/ppermute | solution.py:737
  105.6 1.5 %collective-permute-done.32.more_ref = bf16[256,512]{1,0:T(8,128)(2,1)S(1)} collective-permute-done((bf16[256,512]{1,0:T(8,128)(2,1)S(1)}, bf16[256,512]{1,0:T(8,128)(2,1)S(1)}, u32[]{:S(2)}, u32[]{:S(2)}) %collective-permute-start.32) | collective-permute-done | bytes 262176 | tf_op jit(solution)/shard_map/ppermute | solution.py:740
  107.4 1.6 %collective-permute-start.37 = (bf16[4,16,1536]{2,1,0:T(8,128)(2,1)S(1)}, bf16[4,16,1536]{2,1,0:T(8,128)(2,1)S(1)}, u32[]{:S(2)}, u32[]{:S(2)}) collective-permute-start(bf16[4,16,1536]{2,1,0:T(8,128)(2,1)S(1)} %get-tuple-element.233), channel_id=1, source_target_pairs={{0,6},{1,7},{2,4},{3,5},{4,2},{5,3},{6,0},{7,1},{8,14},{9,15},{10,... | collective-permute-start | bytes 589832 | tf_op jit(solution)/shard_map/ppermute | solution.py:737
  108.9 1.5 %collective-permute-start.38 = (bf16[4,16,1536]{2,1,0:T(8,128)(2,1)S(1)}, bf16[4,16,1536]{2,1,0:T(8,128)(2,1)S(1)}, u32[]{:S(2)}, u32[]{:S(2)}) collective-permute-start(bf16[4,16,1536]{2,1,0:T(8,128)(2,1)S(1)} %get-tuple-element.234), channel_id=1, source_target_pairs={{0,2},{1,3},{2,0},{3,1},{4,6},{5,7},{6,4},{7,5},{8,10},{9,11},{10,... | collective-permute-start | bytes 589832 | tf_op jit(solution)/shard_map/ppermute | solution.py:737
  110.9 9.2 %collective-permute-done.35.got_y_ref = bf16[4,16,4736]{2,1,0:T(8,128)(2,1)S(1)} collective-permute-done((bf16[4,16,4736]{2,1,0:T(8,128)(2,1)S(1)}, bf16[4,16,4736]{2,1,0:T(8,128)(2,1)S(1)}, u32[]{:S(2)}, u32[]{:S(2)}) %collective-permute-start.35) | collective-permute-done | bytes 606240 | tf_op jit(solution)/shard_map/ppermute | solution.py:737
  120.6 0.8 shard_map.264
  121.5 2.0 %collective-permute-start.41 = (bf16[16,4736]{1,0:T(8,128)(2,1)S(1)}, bf16[16,4736]{1,0:T(8,128)(2,1)S(1)}, u32[]{:S(2)}, u32[]{:S(2)}) collective-permute-start(bf16[16,4736]{1,0:T(8,128)(2,1)S(1)} %get-tuple-element.242), channel_id=1, source_target_pairs={{0,8},{1,9},{2,10},{3,11},{4,12},{5,13},{6,14},{7,15},{8,0},{9,1},... | collective-permute-start | bytes 454664 | tf_op jit(solution)/shard_map/ppermute | solution.py:737
  123.5 2.4 %collective-permute-done.37.b_ref = bf16[4,16,1536]{2,1,0:T(8,128)(2,1)S(1)} collective-permute-done((bf16[4,16,1536]{2,1,0:T(8,128)(2,1)S(1)}, bf16[4,16,1536]{2,1,0:T(8,128)(2,1)S(1)}, u32[]{:S(2)}, u32[]{:S(2)}) %collective-permute-start.37) | collective-permute-done | bytes 196640 | tf_op jit(solution)/shard_map/ppermute | solution.py:737
  125.8 1.5 %collective-permute-start.36 = (bf16[128,1024]{1,0:T(8,128)(2,1)S(1)}, bf16[128,1024]{1,0:T(8,128)(2,1)S(1)}, u32[]{:S(2)}, u32[]{:S(2)}) collective-permute-start(bf16[128,1024]{1,0:T(8,128)(2,1)S(1)} %get-tuple-element.229), channel_id=1, source_target_pairs={{0,2},{1,3},{2,0},{3,1},{4,6},{5,7},{6,4},{7,5},{8,10},{9,11},{10,... | collective-permute-start | bytes 786440 | tf_op jit(solution)/shard_map/ppermute | solution.py:740
  127.3 1.8 %collective-permute-done.38.c_ref = bf16[4,16,1536]{2,1,0:T(8,128)(2,1)S(1)} collective-permute-done((bf16[4,16,1536]{2,1,0:T(8,128)(2,1)S(1)}, bf16[4,16,1536]{2,1,0:T(8,128)(2,1)S(1)}, u32[]{:S(2)}, u32[]{:S(2)}) %collective-permute-start.38) | collective-permute-done | bytes 196640 | tf_op jit(solution)/shard_map/ppermute | solution.py:737
  129.1 0.7 shard_map.266
  129.8 3.1 %collective-permute-start.42 = (bf16[16,4736]{1,0:T(8,128)(2,1)S(1)}, bf16[16,4736]{1,0:T(8,128)(2,1)S(1)}, u32[]{:S(2)}, u32[]{:S(2)}) collective-permute-start(bf16[16,4736]{1,0:T(8,128)(2,1)S(1)} %shard_map.267), channel_id=1, source_target_pairs={{0,24},{1,25},{2,26},{3,27},{4,28},{5,29},{6,30},{7,31},{8,16},{9,... | collective-permute-start | bytes 454664 | tf_op jit(solution)/shard_map/ppermute | solution.py:737
  132.9 2.0 %collective-permute-start.44 = (bf16[16,1536]{1,0:T(8,128)(2,1)S(1)}, bf16[16,1536]{1,0:T(8,128)(2,1)S(1)}, u32[]{:S(2)}, u32[]{:S(2)}) collective-permute-start(bf16[16,1536]{1,0:T(8,128)(2,1)S(1)} %get-tuple-element.248), channel_id=1, source_target_pairs={{0,8},{1,9},{2,10},{3,11},{4,12},{5,13},{6,14},{7,15},{8,0},{9,1},... | collective-permute-start | bytes 147464 | tf_op jit(solution)/shard_map/ppermute | solution.py:737
  135.0 2.9 %collective-permute-done.43.got_ref = bf16[16,1536]{1,0:T(8,128)(2,1)S(1)} collective-permute-done((bf16[16,1536]{1,0:T(8,128)(2,1)S(1)}, bf16[16,1536]{1,0:T(8,128)(2,1)S(1)}, u32[]{:S(2)}, u32[]{:S(2)}) %collective-permute-start.43) | collective-permute-done | bytes 49184 | tf_op jit(solution)/shard_map/ppermute | solution.py:737
  137.8 0.5 collective-permute-done.44.got_ref
  138.4 0.7 collective-permute-start.45
  139.1 1.6 %shard_map.265 = (f32[2,128,512]{2,1,0:T(8,128)}, f32[2,128,512]{2,1,0:T(8,128)}) custom-call(s32[4]{0:T(128)S(1)} %pad_add_fusion.place_ref.rest_0_.me_ref.info_ref, f32[256,512]{1,0:T(8,128)S(1)} %get-tuple-element.164.out_ref, f32[256,512]{1,0:T(8,128)S(1)} %get-tuple-element.218.in_ref, bf16[128,1024]{1,0:T(8,128)(2,1)S(1)} %collective-permute-done.36.back_ref), custom_call_target="tpu_custom_call" | custom-call | flops 57500000 | bytes 2359312 | tf_op jit(solution)/shard_map/pallas_call | solution.py:707
  140.7 0.7 shard_map.268
  141.4 2.9 %collective-permute-done.45.far_ref = bf16[16,1536]{1,0:T(8,128)(2,1)S(1)} collective-permute-done((bf16[16,1536]{1,0:T(8,128)(2,1)S(1)}, bf16[16,1536]{1,0:T(8,128)(2,1)S(1)}, u32[]{:S(2)}, u32[]{:S(2)}) %collective-permute-start.45) | collective-permute-done | bytes 49184 | tf_op jit(solution)/shard_map/ppermute | solution.py:737
  144.3 0.6 shard_map.270
  (56 shorter events, 6.3 us)
Async XLA Ops:
  3.0 13.6 %collective-permute-start = (bf16[128,1152]{1,0:T(8,128)(2,1)S(1)}, bf16[128,1152]{1,0:T(8,128)(2,1)S(1)}, u32[]{:S(2)}, u32[]{:S(2)}) collective-permute-start(bf16[128,1152]{1,0:T(8,128)(2,1)S(1)} %get-tuple-element.137), channel_id=1, source_target_pairs={{0,2},{1,3},{2,0},{3,1},{4,6},{5,7},{6,4},{7,5},{8,10},{9,11},{10,... | collective-permute-start | bytes 884744 | tf_op jit(solution)/shard_map/ppermute | solution.py:740
  6.0 7.2 %collective-permute-start.4 = (bf16[5,16,512]{2,1,0:T(8,128)(2,1)S(1)}, bf16[5,16,512]{2,1,0:T(8,128)(2,1)S(1)}, u32[]{:S(2)}, u32[]{:S(2)}) collective-permute-start(bf16[5,16,512]{2,1,0:T(8,128)(2,1)S(1)} %get-tuple-element.142.refs_0_), channel_id=1, source_target_pairs={{0,24},{1,25},{2,26},{3,27},{4,28},{5,29},{6,30},{7,31},{8,16},{9,... | collective-permute-start | bytes 245768 | tf_op jit(solution)/shard_map/ppermute | solution.py:737
  9.6 6.6 %collective-permute-start.3 = (bf16[5,16,512]{2,1,0:T(8,128)(2,1)S(1)}, bf16[5,16,512]{2,1,0:T(8,128)(2,1)S(1)}, u32[]{:S(2)}, u32[]{:S(2)}) collective-permute-start(bf16[5,16,512]{2,1,0:T(8,128)(2,1)S(1)} %get-tuple-element.142.refs_0_), channel_id=1, source_target_pairs={{0,16},{1,17},{2,18},{3,19},{4,20},{5,21},{6,22},{7,23},{8,24},{9,... | collective-permute-start | bytes 245768 | tf_op jit(solution)/shard_map/ppermute | solution.py:737
  9.6 6.6 %collective-permute-start.2 = (bf16[5,16,512]{2,1,0:T(8,128)(2,1)S(1)}, bf16[5,16,512]{2,1,0:T(8,128)(2,1)S(1)}, u32[]{:S(2)}, u32[]{:S(2)}) collective-permute-start(bf16[5,16,512]{2,1,0:T(8,128)(2,1)S(1)} %get-tuple-element.142.refs_0_), channel_id=1, source_target_pairs={{0,8},{1,9},{2,10},{3,11},{4,12},{5,13},{6,14},{7,15},{8,0},{9,1},... | collective-permute-start | bytes 245768 | tf_op jit(solution)/shard_map/ppermute | solution.py:737
  16.7 17.2 %collective-permute-start.6 = (bf16[4,5,16,512]{3,2,1,0:T(8,128)(2,1)S(1)}, bf16[4,5,16,512]{3,2,1,0:T(8,128)(2,1)S(1)}, u32[]{:S(2)}, u32[]{:S(2)}) collective-permute-start(bf16[4,5,16,512]{3,2,1,0:T(8,128)(2,1)S(1)} %shard_map.248.rest_1_), channel_id=1, source_target_pairs={{0,4},{1,5},{2,6},{3,7},{4,0},{5,1},{6,2},{7,3},{8,12},{9,13},{10,... | collective-permute-start | bytes 983048 | tf_op jit(solution)/shard_map/ppermute | solution.py:737
  18.2 15.6 %collective-permute-start.5 = (bf16[4,5,16,512]{3,2,1,0:T(8,128)(2,1)S(1)}, bf16[4,5,16,512]{3,2,1,0:T(8,128)(2,1)S(1)}, u32[]{:S(2)}, u32[]{:S(2)}) collective-permute-start(bf16[4,5,16,512]{3,2,1,0:T(8,128)(2,1)S(1)} %shard_map.248.rest_1_), channel_id=1, source_target_pairs={{0,2},{1,3},{2,0},{3,1},{4,6},{5,7},{6,4},{7,5},{8,10},{9,11},{10,... | collective-permute-start | bytes 983048 | tf_op jit(solution)/shard_map/ppermute | solution.py:737
  18.8 7.6 %collective-permute-start.10 = (bf16[8,16,512]{2,1,0:T(8,128)(2,1)S(1)}, bf16[8,16,512]{2,1,0:T(8,128)(2,1)S(1)}, u32[]{:S(2)}, u32[]{:S(2)}) collective-permute-start(bf16[8,16,512]{2,1,0:T(8,128)(2,1)S(1)} %get-tuple-element.145.refs_0_), channel_id=1, source_target_pairs={{0,16},{1,17},{2,18},{3,19},{4,20},{5,21},{6,22},{7,23},{8,24},{9,... | collective-permute-start | bytes 393224 | tf_op jit(solution)/shard_map/ppermute | solution.py:737
  19.7 0.7 copy-start
  22.2 11.7 %collective-permute-start.1 = (bf16[1,256,512]{2,1,0:T(8,128)(2,1)S(1)}, bf16[1,256,512]{2,1,0:T(8,128)(2,1)S(1)}, u32[]{:S(2)}, u32[]{:S(2)}) collective-permute-start(bf16[1,256,512]{2,1,0:T(8,128)(2,1)S(1)} %bitcast.30), channel_id=1, source_target_pairs={{0,1},{1,0},{2,3},{3,2},{4,5},{5,4},{6,7},{7,6},{8,9},{9,8},{10,11... | collective-permute-start | bytes 786440 | tf_op jit(solution)/shard_map/ppermute | solution.py:740
  22.2 6.9 %collective-permute-start.9 = (bf16[8,16,512]{2,1,0:T(8,128)(2,1)S(1)}, bf16[8,16,512]{2,1,0:T(8,128)(2,1)S(1)}, u32[]{:S(2)}, u32[]{:S(2)}) collective-permute-start(bf16[8,16,512]{2,1,0:T(8,128)(2,1)S(1)} %get-tuple-element.145.refs_0_), channel_id=1, source_target_pairs={{0,8},{1,9},{2,10},{3,11},{4,12},{5,13},{6,14},{7,15},{8,0},{9,1},... | collective-permute-start | bytes 393224 | tf_op jit(solution)/shard_map/ppermute | solution.py:737
  26.4 6.8 %collective-permute-start.7 = (bf16[8,16,512]{2,1,0:T(8,128)(2,1)S(1)}, bf16[8,16,512]{2,1,0:T(8,128)(2,1)S(1)}, u32[]{:S(2)}, u32[]{:S(2)}) collective-permute-start(bf16[8,16,512]{2,1,0:T(8,128)(2,1)S(1)} %get-tuple-element.145.refs_0_), channel_id=1, source_target_pairs={{0,24},{1,25},{2,26},{3,27},{4,28},{5,29},{6,30},{7,31},{8,16},{9,... | collective-permute-start | bytes 393224 | tf_op jit(solution)/shard_map/ppermute | solution.py:737
  33.8 14.9 %collective-permute-start.12 = (bf16[4,8,16,512]{3,2,1,0:T(8,128)(2,1)S(1)}, bf16[4,8,16,512]{3,2,1,0:T(8,128)(2,1)S(1)}, u32[]{:S(2)}, u32[]{:S(2)}) collective-permute-start(bf16[4,8,16,512]{3,2,1,0:T(8,128)(2,1)S(1)} %shard_map.249.rest_1_), channel_id=1, source_target_pairs={{0,2},{1,3},{2,0},{3,1},{4,6},{5,7},{6,4},{7,5},{8,10},{9,11},{10,... | collective-permute-start | bytes 1572872 | tf_op jit(solution)/shard_map/ppermute | solution.py:737
  35.1 13.7 %collective-permute-start.11 = (bf16[4,8,16,512]{3,2,1,0:T(8,128)(2,1)S(1)}, bf16[4,8,16,512]{3,2,1,0:T(8,128)(2,1)S(1)}, u32[]{:S(2)}, u32[]{:S(2)}) collective-permute-start(bf16[4,8,16,512]{3,2,1,0:T(8,128)(2,1)S(1)} %shard_map.249.rest_1_), channel_id=1, source_target_pairs={{0,4},{1,5},{2,6},{3,7},{4,0},{5,1},{6,2},{7,3},{8,12},{9,13},{10,... | collective-permute-start | bytes 1572872 | tf_op jit(solution)/shard_map/ppermute | solution.py:737
  35.6 17.0 %collective-permute-start.8 = (bf16[4,5,16,512]{3,2,1,0:T(8,128)(2,1)S(1)}, bf16[4,5,16,512]{3,2,1,0:T(8,128)(2,1)S(1)}, u32[]{:S(2)}, u32[]{:S(2)}) collective-permute-start(bf16[4,5,16,512]{3,2,1,0:T(8,128)(2,1)S(1)} %collective-permute-done.6.rest_3_), channel_id=1, source_target_pairs={{0,2},{1,3},{2,0},{3,1},{4,6},{5,7},{6,4},{7,5},{8,10},{9,11},{10,... | collective-permute-start | bytes 983048 | tf_op jit(solution)/shard_map/ppermute | solution.py:737
  36.4 16.7 %collective-permute-start.13 = (bf16[4,5,16,512]{3,2,1,0:T(8,128)(2,1)S(1)}, bf16[4,5,16,512]{3,2,1,0:T(8,128)(2,1)S(1)}, u32[]{:S(2)}, u32[]{:S(2)}) collective-permute-start(bf16[4,5,16,512]{3,2,1,0:T(8,128)(2,1)S(1)} %shard_map.248.rest_1_), channel_id=1, source_target_pairs={{0,1},{1,0},{2,3},{3,2},{4,5},{5,4},{6,7},{7,6},{8,9},{9,8},{10,11... | collective-permute-start | bytes 983048 | tf_op jit(solution)/shard_map/ppermute | solution.py:737
  36.5 18.2 %collective-permute-start.15 = (bf16[4,5,16,512]{3,2,1,0:T(8,128)(2,1)S(1)}, bf16[4,5,16,512]{3,2,1,0:T(8,128)(2,1)S(1)}, u32[]{:S(2)}, u32[]{:S(2)}) collective-permute-start(bf16[4,5,16,512]{3,2,1,0:T(8,128)(2,1)S(1)} %collective-permute-done.6.rest_3_), channel_id=1, source_target_pairs={{0,1},{1,0},{2,3},{3,2},{4,5},{5,4},{6,7},{7,6},{8,9},{9,8},{10,11... | collective-permute-start | bytes 983048 | tf_op jit(solution)/shard_map/ppermute | solution.py:737
  48.8 6.3 %collective-permute-start.14 = (bf16[4,5,16,512]{3,2,1,0:T(8,128)(2,1)S(1)}, bf16[4,5,16,512]{3,2,1,0:T(8,128)(2,1)S(1)}, u32[]{:S(2)}, u32[]{:S(2)}) collective-permute-start(bf16[4,5,16,512]{3,2,1,0:T(8,128)(2,1)S(1)} %collective-permute-done.5.rest_2_), channel_id=1, source_target_pairs={{0,1},{1,0},{2,3},{3,2},{4,5},{5,4},{6,7},{7,6},{8,9},{9,8},{10,11... | collective-permute-start | bytes 983048 | tf_op jit(solution)/shard_map/ppermute | solution.py:737
  52.6 2.5 %collective-permute-start.16 = (bf16[4,5,16,512]{3,2,1,0:T(8,128)(2,1)S(1)}, bf16[4,5,16,512]{3,2,1,0:T(8,128)(2,1)S(1)}, u32[]{:S(2)}, u32[]{:S(2)}) collective-permute-start(bf16[4,5,16,512]{3,2,1,0:T(8,128)(2,1)S(1)} %collective-permute-done.8.rest_4_), channel_id=1, source_target_pairs={{0,1},{1,0},{2,3},{3,2},{4,5},{5,4},{6,7},{7,6},{8,9},{9,8},{10,11... | collective-permute-start | bytes 983048 | tf_op jit(solution)/shard_map/ppermute | solution.py:737
  52.6 10.5 %collective-permute-start.17 = (bf16[4,8,16,512]{3,2,1,0:T(8,128)(2,1)S(1)}, bf16[4,8,16,512]{3,2,1,0:T(8,128)(2,1)S(1)}, u32[]{:S(2)}, u32[]{:S(2)}) collective-permute-start(bf16[4,8,16,512]{3,2,1,0:T(8,128)(2,1)S(1)} %shard_map.249.rest_1_), channel_id=1, source_target_pairs={{0,1},{1,0},{2,3},{3,2},{4,5},{5,4},{6,7},{7,6},{8,9},{9,8},{10,11... | collective-permute-start | bytes 1572872 | tf_op jit(solution)/shard_map/ppermute | solution.py:737
  53.1 9.4 %collective-permute-start.20 = (bf16[2,8,16,512]{3,2,1,0:T(8,128)(2,1)S(1)}, bf16[2,8,16,512]{3,2,1,0:T(8,128)(2,1)S(1)}, u32[]{:S(2)}, u32[]{:S(2)}) collective-permute-start(bf16[2,8,16,512]{3,2,1,0:T(8,128)(2,1)S(1)} %get-tuple-element.148), channel_id=1, source_target_pairs={{0,2},{1,3},{2,0},{3,1},{4,6},{5,7},{6,4},{7,5},{8,10},{9,11},{10,... | collective-permute-start | bytes 786440 | tf_op jit(solution)/shard_map/ppermute | solution.py:737
  54.6 7.9 %collective-permute-start.21 = (bf16[2,8,16,512]{3,2,1,0:T(8,128)(2,1)S(1)}, bf16[2,8,16,512]{3,2,1,0:T(8,128)(2,1)S(1)}, u32[]{:S(2)}, u32[]{:S(2)}) collective-permute-start(bf16[2,8,16,512]{3,2,1,0:T(8,128)(2,1)S(1)} %get-tuple-element.156), channel_id=1, source_target_pairs={{0,4},{1,5},{2,6},{3,7},{4,0},{5,1},{6,2},{7,3},{8,12},{9,13},{10,... | collective-permute-start | bytes 786440 | tf_op jit(solution)/shard_map/ppermute | solution.py:737
  55.1 7.9 %collective-permute-start.18 = (bf16[4,8,16,512]{3,2,1,0:T(8,128)(2,1)S(1)}, bf16[4,8,16,512]{3,2,1,0:T(8,128)(2,1)S(1)}, u32[]{:S(2)}, u32[]{:S(2)}) collective-permute-start(bf16[4,8,16,512]{3,2,1,0:T(8,128)(2,1)S(1)} %collective-permute-done.12.by_x_ref.rest_2_), channel_id=1, source_target_pairs={{0,1},{1,0},{2,3},{3,2},{4,5},{5,4},{6,7},{7,6},{8,9},{9,8},{10,11... | collective-permute-start | bytes 1572872 | tf_op jit(solution)/shard_map/ppermute | solution.py:737
  55.1 7.9 %collective-permute-start.19 = (bf16[4,8,16,512]{3,2,1,0:T(8,128)(2,1)S(1)}, bf16[4,8,16,512]{3,2,1,0:T(8,128)(2,1)S(1)}, u32[]{:S(2)}, u32[]{:S(2)}) collective-permute-start(bf16[4,8,16,512]{3,2,1,0:T(8,128)(2,1)S(1)} %collective-permute-done.11.by_y_ref.rest_3_), channel_id=1, source_target_pairs={{0,1},{1,0},{2,3},{3,2},{4,5},{5,4},{6,7},{7,6},{8,9},{9,8},{10,11... | collective-permute-start | bytes 1572872 | tf_op jit(solution)/shard_map/ppermute | solution.py:737
  62.5 1.5 %collective-permute-start.22 = (bf16[2,8,16,512]{3,2,1,0:T(8,128)(2,1)S(1)}, bf16[2,8,16,512]{3,2,1,0:T(8,128)(2,1)S(1)}, u32[]{:S(2)}, u32[]{:S(2)}) collective-permute-start(bf16[2,8,16,512]{3,2,1,0:T(8,128)(2,1)S(1)} %collective-permute-done.20.rest_7_), channel_id=1, source_target_pairs={{0,1},{1,0},{2,3},{3,2},{4,5},{5,4},{6,7},{7,6},{8,9},{9,8},{10,11... | collective-permute-start | bytes 786440 | tf_op jit(solution)/shard_map/ppermute | solution.py:737
  62.5 1.9 %collective-permute-start.23 = (bf16[2,8,16,512]{3,2,1,0:T(8,128)(2,1)S(1)}, bf16[2,8,16,512]{3,2,1,0:T(8,128)(2,1)S(1)}, u32[]{:S(2)}, u32[]{:S(2)}) collective-permute-start(bf16[2,8,16,512]{3,2,1,0:T(8,128)(2,1)S(1)} %collective-permute-done.21.rest_8_), channel_id=1, source_target_pairs={{0,1},{1,0},{2,3},{3,2},{4,5},{5,4},{6,7},{7,6},{8,9},{9,8},{10,11... | collective-permute-start | bytes 786440 | tf_op jit(solution)/shard_map/ppermute | solution.py:737
  68.2 1.6 %collective-permute-start.24 = (bf16[1,256,512]{2,1,0:T(8,128)(2,1)S(1)}, bf16[1,256,512]{2,1,0:T(8,128)(2,1)S(1)}, u32[]{:S(2)}, u32[]{:S(2)}) collective-permute-start(bf16[1,256,512]{2,1,0:T(8,128)(2,1)S(1)} %bitcast.33), channel_id=1, source_target_pairs={{0,1},{1,0},{2,3},{3,2},{4,5},{5,4},{6,7},{7,6},{8,9},{9,8},{10,11... | collective-permute-start | bytes 786440 | tf_op jit(solution)/shard_map/ppermute | solution.py:740
  80.4 1.6 %collective-permute-start.25 = (bf16[256,512]{1,0:T(8,128)(2,1)S(1)}, bf16[256,512]{1,0:T(8,128)(2,1)S(1)}, u32[]{:S(2)}, u32[]{:S(2)}) collective-permute-start(bf16[256,512]{1,0:T(8,128)(2,1)S(1)} %get-tuple-element.166), channel_id=1, source_target_pairs={{0,1},{1,0},{2,3},{3,2},{4,5},{5,4},{6,7},{7,6},{8,9},{9,8},{10,11... | collective-permute-start | bytes 786440 | tf_op jit(solution)/shard_map/ppermute | solution.py:740
  84.6 2.7 %collective-permute-start.26 = (bf16[4,4,64,512]{3,2,1,0:T(8,128)(2,1)S(1)}, bf16[4,4,64,512]{3,2,1,0:T(8,128)(2,1)S(1)}, u32[]{:S(2)}, u32[]{:S(2)}) collective-permute-start(bf16[4,4,64,512]{3,2,1,0:T(8,128)(2,1)S(1)} %get-tuple-element.186), channel_id=1, source_target_pairs={{0,1},{1,0},{2,3},{3,2},{4,5},{5,4},{6,7},{7,6},{8,9},{9,8},{10,11... | collective-permute-start | bytes 3145736 | tf_op jit(solution)/shard_map/ppermute | solution.py:737
  89.8 3.2 %collective-permute-start.27 = (bf16[4,4,16,2688]{3,2,1,0:T(8,128)(2,1)S(1)}, bf16[4,4,16,2688]{3,2,1,0:T(8,128)(2,1)S(1)}, u32[]{:S(2)}, u32[]{:S(2)}) collective-permute-start(bf16[4,4,16,2688]{3,2,1,0:T(8,128)(2,1)S(1)} %get-tuple-element.198), channel_id=1, source_target_pairs={{0,1},{1,0},{2,3},{3,2},{4,5},{5,4},{6,7},{7,6},{8,9},{9,8},{10,11... | collective-permute-start | bytes 4128776 | tf_op jit(solution)/shard_map/ppermute | solution.py:737
  90.0 6.7 %collective-permute-start.28 = (bf16[2,64,512]{2,1,0:T(8,128)(2,1)S(1)}, bf16[2,64,512]{2,1,0:T(8,128)(2,1)S(1)}, u32[]{:S(2)}, u32[]{:S(2)}) collective-permute-start(bf16[2,64,512]{2,1,0:T(8,128)(2,1)S(1)} %get-tuple-element.187), channel_id=1, source_target_pairs={{0,2},{1,3},{2,0},{3,1},{4,6},{5,7},{6,4},{7,5},{8,10},{9,11},{10,... | collective-permute-start | bytes 393224 | tf_op jit(solution)/shard_map/ppermute | solution.py:737
  90.6 6.1 %collective-permute-start.29 = (bf16[2,64,512]{2,1,0:T(8,128)(2,1)S(1)}, bf16[2,64,512]{2,1,0:T(8,128)(2,1)S(1)}, u32[]{:S(2)}, u32[]{:S(2)}) collective-permute-start(bf16[2,64,512]{2,1,0:T(8,128)(2,1)S(1)} %get-tuple-element.209), channel_id=1, source_target_pairs={{0,4},{1,5},{2,6},{3,7},{4,0},{5,1},{6,2},{7,3},{8,12},{9,13},{10,... | collective-permute-start | bytes 393224 | tf_op jit(solution)/shard_map/ppermute | solution.py:737
  93.3 6.8 %collective-permute-start.30 = (bf16[2,16,2688]{2,1,0:T(8,128)(2,1)S(1)}, bf16[2,16,2688]{2,1,0:T(8,128)(2,1)S(1)}, u32[]{:S(2)}, u32[]{:S(2)}) collective-permute-start(bf16[2,16,2688]{2,1,0:T(8,128)(2,1)S(1)} %get-tuple-element.199), channel_id=1, source_target_pairs={{0,2},{1,3},{2,0},{3,1},{4,6},{5,7},{6,4},{7,5},{8,10},{9,11},{10,... | collective-permute-start | bytes 516104 | tf_op jit(solution)/shard_map/ppermute | solution.py:737
  93.9 6.1 %collective-permute-start.31 = (bf16[2,16,2688]{2,1,0:T(8,128)(2,1)S(1)}, bf16[2,16,2688]{2,1,0:T(8,128)(2,1)S(1)}, u32[]{:S(2)}, u32[]{:S(2)}) collective-permute-start(bf16[2,16,2688]{2,1,0:T(8,128)(2,1)S(1)} %get-tuple-element.212), channel_id=1, source_target_pairs={{0,4},{1,5},{2,6},{3,7},{4,0},{5,1},{6,2},{7,3},{8,12},{9,13},{10,... | collective-permute-start | bytes 516104 | tf_op jit(solution)/shard_map/ppermute | solution.py:737
  103.4 3.7 %collective-permute-start.33 = (bf16[4,4,16,1536]{3,2,1,0:T(8,128)(2,1)S(1)}, bf16[4,4,16,1536]{3,2,1,0:T(8,128)(2,1)S(1)}, u32[]{:S(2)}, u32[]{:S(2)}) collective-permute-start(bf16[4,4,16,1536]{3,2,1,0:T(8,128)(2,1)S(1)} %get-tuple-element.223), channel_id=1, source_target_pairs={{0,1},{1,0},{2,3},{3,2},{4,5},{5,4},{6,7},{7,6},{8,9},{9,8},{10,11... | collective-permute-start | bytes 2359304 | tf_op jit(solution)/shard_map/ppermute | solution.py:737
  103.5 16.6 %collective-permute-start.35 = (bf16[4,16,4736]{2,1,0:T(8,128)(2,1)S(1)}, bf16[4,16,4736]{2,1,0:T(8,128)(2,1)S(1)}, u32[]{:S(2)}, u32[]{:S(2)}) collective-permute-start(bf16[4,16,4736]{2,1,0:T(8,128)(2,1)S(1)} %get-tuple-element.227), channel_id=1, source_target_pairs={{0,4},{1,5},{2,6},{3,7},{4,0},{5,1},{6,2},{7,3},{8,12},{9,13},{10,... | collective-permute-start | bytes 1818632 | tf_op jit(solution)/shard_map/ppermute | solution.py:737
  104.1 16.5 %collective-permute-start.34 = (bf16[4,16,4736]{2,1,0:T(8,128)(2,1)S(1)}, bf16[4,16,4736]{2,1,0:T(8,128)(2,1)S(1)}, u32[]{:S(2)}, u32[]{:S(2)}) collective-permute-start(bf16[4,16,4736]{2,1,0:T(8,128)(2,1)S(1)} %get-tuple-element.213), channel_id=1, source_target_pairs={{0,2},{1,3},{2,0},{3,1},{4,6},{5,7},{6,4},{7,5},{8,10},{9,11},{10,... | collective-permute-start | bytes 1818632 | tf_op jit(solution)/shard_map/ppermute | solution.py:737
  105.6 1.5 %collective-permute-start.32 = (bf16[256,512]{1,0:T(8,128)(2,1)S(1)}, bf16[256,512]{1,0:T(8,128)(2,1)S(1)}, u32[]{:S(2)}, u32[]{:S(2)}) collective-permute-start(bf16[256,512]{1,0:T(8,128)(2,1)S(1)} %get-tuple-element.217), channel_id=1, source_target_pairs={{0,1},{1,0},{2,3},{3,2},{4,5},{5,4},{6,7},{7,6},{8,9},{9,8},{10,11... | collective-permute-start | bytes 786440 | tf_op jit(solution)/shard_map/ppermute | solution.py:740
  107.4 18.5 %collective-permute-start.37 = (bf16[4,16,1536]{2,1,0:T(8,128)(2,1)S(1)}, bf16[4,16,1536]{2,1,0:T(8,128)(2,1)S(1)}, u32[]{:S(2)}, u32[]{:S(2)}) collective-permute-start(bf16[4,16,1536]{2,1,0:T(8,128)(2,1)S(1)} %get-tuple-element.233), channel_id=1, source_target_pairs={{0,6},{1,7},{2,4},{3,5},{4,2},{5,3},{6,0},{7,1},{8,14},{9,15},{10,... | collective-permute-start | bytes 589832 | tf_op jit(solution)/shard_map/ppermute | solution.py:737
  108.9 20.1 %collective-permute-start.38 = (bf16[4,16,1536]{2,1,0:T(8,128)(2,1)S(1)}, bf16[4,16,1536]{2,1,0:T(8,128)(2,1)S(1)}, u32[]{:S(2)}, u32[]{:S(2)}) collective-permute-start(bf16[4,16,1536]{2,1,0:T(8,128)(2,1)S(1)} %get-tuple-element.234), channel_id=1, source_target_pairs={{0,2},{1,3},{2,0},{3,1},{4,6},{5,7},{6,4},{7,5},{8,10},{9,11},{10,... | collective-permute-start | bytes 589832 | tf_op jit(solution)/shard_map/ppermute | solution.py:737
  110.4 18.6 %collective-permute-start.39 = (bf16[4,16,1536]{2,1,0:T(8,128)(2,1)S(1)}, bf16[4,16,1536]{2,1,0:T(8,128)(2,1)S(1)}, u32[]{:S(2)}, u32[]{:S(2)}) collective-permute-start(bf16[4,16,1536]{2,1,0:T(8,128)(2,1)S(1)} %get-tuple-element.235), channel_id=1, source_target_pairs={{0,4},{1,5},{2,6},{3,7},{4,0},{5,1},{6,2},{7,3},{8,12},{9,13},{10,... | collective-permute-start | bytes 589832 | tf_op jit(solution)/shard_map/ppermute | solution.py:737
  121.4 8.4 %collective-permute-start.40 = (bf16[16,4736]{1,0:T(8,128)(2,1)S(1)}, bf16[16,4736]{1,0:T(8,128)(2,1)S(1)}, u32[]{:S(2)}, u32[]{:S(2)}) collective-permute-start(bf16[16,4736]{1,0:T(8,128)(2,1)S(1)} %get-tuple-element.238), channel_id=1, source_target_pairs={{0,8},{1,9},{2,10},{3,11},{4,12},{5,13},{6,14},{7,15},{8,0},{9,1},... | collective-permute-start | bytes 454664 | tf_op jit(solution)/shard_map/ppermute | solution.py:737
  121.5 8.3 %collective-permute-start.41 = (bf16[16,4736]{1,0:T(8,128)(2,1)S(1)}, bf16[16,4736]{1,0:T(8,128)(2,1)S(1)}, u32[]{:S(2)}, u32[]{:S(2)}) collective-permute-start(bf16[16,4736]{1,0:T(8,128)(2,1)S(1)} %get-tuple-element.242), channel_id=1, source_target_pairs={{0,8},{1,9},{2,10},{3,11},{4,12},{5,13},{6,14},{7,15},{8,0},{9,1},... | collective-permute-start | bytes 454664 | tf_op jit(solution)/shard_map/ppermute | solution.py:737
  125.8 13.3 %collective-permute-start.36 = (bf16[128,1024]{1,0:T(8,128)(2,1)S(1)}, bf16[128,1024]{1,0:T(8,128)(2,1)S(1)}, u32[]{:S(2)}, u32[]{:S(2)}) collective-permute-start(bf16[128,1024]{1,0:T(8,128)(2,1)S(1)} %get-tuple-element.229), channel_id=1, source_target_pairs={{0,2},{1,3},{2,0},{3,1},{4,6},{5,7},{6,4},{7,5},{8,10},{9,11},{10,... | collective-permute-start | bytes 786440 | tf_op jit(solution)/shard_map/ppermute | solution.py:740
  129.8 10.9 %collective-permute-start.42 = (bf16[16,4736]{1,0:T(8,128)(2,1)S(1)}, bf16[16,4736]{1,0:T(8,128)(2,1)S(1)}, u32[]{:S(2)}, u32[]{:S(2)}) collective-permute-start(bf16[16,4736]{1,0:T(8,128)(2,1)S(1)} %shard_map.267), channel_id=1, source_target_pairs={{0,24},{1,25},{2,26},{3,27},{4,28},{5,29},{6,30},{7,31},{8,16},{9,... | collective-permute-start | bytes 454664 | tf_op jit(solution)/shard_map/ppermute | solution.py:737
  132.9 4.9 %collective-permute-start.43 = (bf16[16,1536]{1,0:T(8,128)(2,1)S(1)}, bf16[16,1536]{1,0:T(8,128)(2,1)S(1)}, u32[]{:S(2)}, u32[]{:S(2)}) collective-permute-start(bf16[16,1536]{1,0:T(8,128)(2,1)S(1)} %get-tuple-element.245), channel_id=1, source_target_pairs={{0,8},{1,9},{2,10},{3,11},{4,12},{5,13},{6,14},{7,15},{8,0},{9,1},... | collective-permute-start | bytes 147464 | tf_op jit(solution)/shard_map/ppermute | solution.py:737
  132.9 5.4 %collective-permute-start.44 = (bf16[16,1536]{1,0:T(8,128)(2,1)S(1)}, bf16[16,1536]{1,0:T(8,128)(2,1)S(1)}, u32[]{:S(2)}, u32[]{:S(2)}) collective-permute-start(bf16[16,1536]{1,0:T(8,128)(2,1)S(1)} %get-tuple-element.248), channel_id=1, source_target_pairs={{0,8},{1,9},{2,10},{3,11},{4,12},{5,13},{6,14},{7,15},{8,0},{9,1},... | collective-permute-start | bytes 147464 | tf_op jit(solution)/shard_map/ppermute | solution.py:737
  138.4 6.0 %collective-permute-start.45 = (bf16[16,1536]{1,0:T(8,128)(2,1)S(1)}, bf16[16,1536]{1,0:T(8,128)(2,1)S(1)}, u32[]{:S(2)}, u32[]{:S(2)}) collective-permute-start(bf16[16,1536]{1,0:T(8,128)(2,1)S(1)} %shard_map.269), channel_id=1, source_target_pairs={{0,24},{1,25},{2,26},{3,27},{4,28},{5,29},{6,30},{7,31},{8,16},{9,... | collective-permute-start | bytes 147464 | tf_op jit(solution)/shard_map/ppermute | solution.py:737
where the time goes:
time: 145 us
  waiting for transfers between devices  63.3 us (44%)
  Pallas kernels  40.8 us (28%)
  starting transfers between devices  39.2 us (27%)
    ppermute x40, waiting for transfers between devices, flip(): return lax.ppermute(value, AXES, [(i, i ^ bit) for i in range(self.count)])  59 us
    pallas_call x25, Pallas kernels, run(): pl.pallas_call(kernel, out_shape=[jax.ShapeDtypeStruct(s, t) for s, t in...  40.8 us
    ppermute x40, starting transfers between devices, flip(): return lax.ppermute(value, AXES, [(i, i ^ bit) for i in range(self.count)])  34.2 us
    ppermute x6, starting transfers between devices, flip_head(): lax.ppermute(value, 'head', [(i, i ^ bit) for i in range(self.heads)])  4.97 us
    ppermute x6, waiting for transfers between devices, flip_head(): lax.ppermute(value, 'head', [(i, i ^ bit) for i in range(self.heads)])  4.34 us
  transfers between devices with their start and end apart: 46, of which 23 were waited for; matrix products, arithmetic and copies ran while one was open for 0% of the time, Pallas kernels for 10%

commit v1 on v0

--- a/solution.py
+++ b/solution.py
@@ -332,20 +332,23 @@
     sorted_refs, (block_ref, tall_ref, flip_ref, flags_ref, turn_ref, low_ref, sems) = rest[:2], rest[2:]
     rows, width = q_ref.shape
     moves = [(vector, low_ref.at[index]) for index, vector in enumerate(vectors)]
+    lanes = width // LANES
     for index, source in enumerate((q_ref, k_ref, v_ref, o_ref)):
-        moves.append((source, block_ref.at[index]))
+        for part in range(lanes):
+            cols = slice(part * LANES, (part + 1) * LANES)
+            moves.append((source.at[:, cols], block_ref.at[index * lanes + part]))
     for index in range(4):
         moves.append((win_ref.at[:, index * BLOCK : (index + 1) * BLOCK], tall_ref.at[index]))
         moves.append((whid_ref.at[index * rows : (index + 1) * rows, :], tall_ref.at[4 + index]))
-    copies = pull(moves, sems.at[:17])
-    sort_rows(place_ref, tok_ref, cot_ref, halt_ref, [*sorted_refs, flip_ref, flags_ref], sems.at[17:])
+    count = len(moves)
+    copies = pull(moves, sems.at[:count])
+    sort_rows(place_ref, tok_ref, cot_ref, halt_ref, [*sorted_refs, flip_ref, flags_ref], sems.at[count:])
     turn_ref[...] = jnp.zeros_like(turn_ref)
     for copy in copies:
         copy.wait()
     for index in range(VECS):
         turn_ref[index : index + 1, :rows] = low_ref[index].astype(F32)
-    block_ref[4, :, :LANES] = turn_ref[...].T[:rows, :].astype(BF16)
-    block_ref[4, :, LANES:] = jnp.zeros((rows, width - LANES), BF16)
+    block_ref[4 * lanes] = turn_ref[...].T[:rows, :].astype(BF16)
 
 
 def attend_kernel(
@@ -356,8 +359,10 @@
         wa_ref, vec_ref, q2_ref, k_ref, v_ref, p_ref, ctx_ref, q_ref, bias_ref, o_ref = rest
 
         def store(piece, z, line, place):
-            for chunk in range(5):
-                wa_ref[chunk, line, place] = piece[z, chunk]
+            lanes = wa_ref.shape[4] // LANES
+            for chunk in range(piece.shape[1]):
+                cols = slice(chunk % lanes * LANES, (chunk % lanes + 1) * LANES)
+                wa_ref[chunk // lanes, line, place, :, cols] = piece[z, chunk]
 
         fetch(plane, (0, 0, 0, 0, 1, 1, 1, 1), (0, 2, 4, 6) * 2, 0, store, me_ref)
         vec_ref[...] = matrix(wa_ref, 4)[:, :LANES].astype(F32).T[0:8, :]
@@ -368,17 +373,19 @@
     attend(q2_ref, k_ref, v_ref, bias_ref, p_ref, ctx_ref, o_ref)
 
 
-def ffn_kernel(
-    fast, x_ref, ctx_ref, tok_ref, sig_ref, vec_ref, wa_ref, *rest,
-):
+def norm_kernel(x_ref, ctx_ref, vec_ref, wa_ref, n1_ref, r1_ref, nlow_ref, acc_ref):
+    first_norm(x_ref, ctx_ref, wa_ref, vec_ref, acc_ref, n1_ref, r1_ref, nlow_ref)
+
+
+def ffn_kernel(fast, n1_ref, nlow_ref, tok_ref, sig_ref, vec_ref, *rest):
     if fast:
         me_ref, near, far, rest = rest[0], rest[1:7], rest[7:11], rest[11:]
         (win_ref, full_ref), rest = rest[:2], rest[2:]
     else:
         (win_ref, whid_ref), rest = rest[:2], rest[2:]
     (
-        n1_ref, r1_ref, nlow_ref, hid_ref, dg_ref, n2_ref, r2_ref, rate_ref, state_ref,
-        pooled_ref, next_ref, rown_ref, inner_ref, acc_ref,
+        hid_ref, dg_ref, n2_ref, r2_ref, rate_ref, state_ref, pooled_ref, next_ref, rown_ref,
+        inner_ref, acc_ref,
     ) = rest
     if fast:
 
@@ -391,8 +398,7 @@
         fetch((far[0], far[2]), (0, 1), (6, 6), 0, store, me_ref)
         fetch((far[1], far[3]), (0, 1), (6, 6), 2, store, me_ref)
         whid_ref = Flat(full_ref)
-    width = x_ref.shape[1]
-    first_norm(x_ref, ctx_ref, wa_ref, vec_ref, acc_ref, n1_ref, r1_ref, nlow_ref)
+    width = n1_ref.shape[1]
     feed_forward(nlow_ref, win_ref, whid_ref, inner_ref, hid_ref, dg_ref, acc_ref)
     for part in chunks(tok_ref.shape[0], ROWS):
         unit, inverse, updated, rate = second_norm(part, vec_ref, n1_ref, acc_ref)
@@ -454,9 +460,10 @@
     if not fast:
         outs[0][:, cols] = value
         return
-    scratch_ref[:, :, :, : value.shape[1]] = value.reshape(scratch_ref.shape[:3] + value.shape[1:])
+    low = value.astype(BF16)
+    scratch_ref[:, :, :, : value.shape[1]] = low.reshape(scratch_ref.shape[:3] + value.shape[1:])
     for relative in range(8):
-        block = scratch_ref[:, relative ^ (me_ref[0] % 8), :, : value.shape[1]].astype(BF16)
+        block = scratch_ref[:, relative ^ (me_ref[0] % 8), :, : value.shape[1]]
         outs[relative % 2][relative // 2, :, :, cols] = block
 
 
@@ -480,10 +487,9 @@
         span = slice(z * hidden_rows, (z + 1) * hidden_rows)
         value = dot(hid_ref[:, span], b2_ref[...], 0, 0) + dot(hid1_ref[:, span], b21_ref[...], 0, 0)
         if fast:
-            tall_ref[...] = value.reshape(tall_ref.shape)
+            tall_ref[...] = value.astype(BF16).reshape(tall_ref.shape)
             for relative in range(8):
-                block = tall_ref[relative ^ (me_ref[0] % 8)].astype(BF16)
-                outs[relative % 2][relative // 2, z] = block
+                outs[relative % 2][relative // 2, z] = tall_ref[relative ^ (me_ref[0] % 8)]
         else:
             outs[0][span, :] = value
 
@@ -675,11 +681,12 @@
         vector[...] = turned[index : index + 1, :rows]
 
 
-def end_kernel(own_ref, got_ref, far_ref, *outs):
+def end_kernel(a_ref, b_ref, c_ref, d_ref, *outs):
     at = 0
     for out in outs:
         cols = slice(at, at + out.shape[1])
-        out[...] = own_ref[:, cols].astype(F32) + got_ref[:, cols].astype(F32) + far_ref[:, cols].astype(F32)
+        total = a_ref[:, cols].astype(F32) + b_ref[:, cols].astype(F32)
+        out[...] = total + c_ref[:, cols].astype(F32) + d_ref[:, cols].astype(F32)
         at = at + out.shape[1]
 
 
@@ -753,8 +760,11 @@
         whole, half = ((4, *block), BF16), ((2, *block), BF16)
         return run(add_core_kernel, [keep, got], [half, half, whole, whole, whole])
 
+    def line_parts(self, kernel, parts, shape):
+        return run(kernel, [self.info, *parts], [(shape, BF16)] * 4, scalars=(0,))
+
     def line_first(self, kernel, parts, shape):
-        own, near, following, far = run(kernel, [self.info, *parts], [(shape, BF16)] * 4, scalars=(0,))
+        own, near, following, far = self.line_parts(kernel, parts, shape)
         return own, far, self.flip(near, 8), self.flip(following, 8)
 
     def line_last(self, own, far, got, got_far):
@@ -825,11 +835,11 @@
         send_tok, own_tok, block_a, block_b = run(
             pack_kernel,
             [*sort_in, *matrices, *(vector[None] for vector in vectors)],
-            [*sort_out, ((5, fine, BLOCK), BF16), ((8, fine, BLOCK), BF16)],
+            [*sort_out, ((4 * pairs + 1, fine, LANES), BF16), ((8, fine, BLOCK), BF16)],
             [*sort_tmp, ((LANES, LANES), F32), ((VECS, 1, fine), BF16)],
             scalars=(0,),
             pinned=range(1, 15),
-            sems=22,
+            sems=18 + 4 * pairs,
         )
         got_tok = links.flip_head(send_tok, group)
         line_a = links.along_z(block_a)
@@ -892,8 +902,9 @@
             [row_b, bias_t, o_t],
             micros=8,
         )
-    ffn_out = [row_f, stat, row_b, ff_b, ff_b, row_f, stat, stat, row_f, row_f, row_f, row_b]
-    ffn_in = [x0, ctx, tok, sig1, vec, full_a]
+    n1, r1, nlow = run(norm_kernel, [x0, ctx, vec, full_a], [row_f, stat, row_b], [row_f], micros=1)
+    ffn_out = [ff_b, ff_b, row_f, stat, stat, row_f, row_f, row_f, row_b]
+    ffn_in = [n1, nlow, tok, sig1, vec]
     if fast:
         far_b = [after(piece, ctx) for piece in far_b]
         far_b = far_b + [links.flip(piece, 1) for piece in far_b]
@@ -902,7 +913,7 @@
             [*ffn_in, links.info, *near, *far_b],
             [((4, 4, 8, fine, BLOCK), BF16), ((4, 8, 4, fine, BLOCK), BF16), *ffn_out],
             [inner_t, row_f],
-            scalars=(6,),
+            scalars=(5,),
             micros=5.5,
         )
         full_in = full_in.reshape(4, width, BLOCK)
@@ -915,7 +926,7 @@
             [inner_t, row_f],
             micros=5.5,
         )
-    n1, r1, nlow, hid, dg, n2, r2, rate, state, pooled, x1, rown1 = got
+    hid, dg, n2, r2, rate, state, pooled, x1, rown1 = got
     roth1 = links.spread(rown1, group)
     out, gs, goth, nlow1, hid1, b11, b21, ctx1, b01, dqkv1, doth1, vg1 = run(
         turn_kernel,
@@ -936,13 +947,13 @@
     hid_out = parts_of((4 * fine, width), (wide_ff, width))
     in_out = parts_of((fine, b_cols), (width, b_cols))
     attend_outs = parts_of((fine, 3 * width), (width, 3 * width))
-    whole_shape = (4, 8, fine, BLOCK) if fast else (8, LANES)
-    tall_shape = (8, 4 * fine, width) if fast else (8, LANES)
+    whole_shape = (4, 8, fine, BLOCK) if fast else (16, LANES)
+    tall_shape = (8, 4 * fine, width) if fast else (16, LANES)
     b2, gsec, base, sums, *hid_parts = run(
         functools.partial(hidden_back_kernel, fast),
         [links.info, gs, more, tok, vec, n2, r2, rate, hid, hid1, b21],
         [row_b, row_f, row_f, sums_t, *hid_out],
-        [(tall_shape, F32)],
+        [(tall_shape, BF16)],
         scalars=(0,),
         micros=2,
     )
@@ -960,7 +971,7 @@
         functools.partial(weights_back_kernel, fast),
         [links.info, b1, b0, sums, nlow, ctx, nlow1, b11, ctx1, b01, vg1],
         in_out,
-        [(whole_shape, F32), ((LANES, width), F32)],
+        [(whole_shape, BF16), ((LANES, width), F32)],
         scalars=(0,),
         micros=2,
     )
@@ -974,31 +985,30 @@
         [q2_t, ds_t, o_t],
         micros=3,
     )
+    g0, goth0, *attend_parts = run(
+        functools.partial(project_back_kernel, fast),
+        [links.info, base, full_a, rown0, roth0, rown1, roth1, dqkv1, doth1, dqkv0, doth0],
+        [row_f, ((others, width), BF16), *attend_outs],
+        [(whole_shape, BF16)],
+        scalars=(0,),
+    )
     if fast:
         c11a, c11b, c10, c01, c00 = c_sums
         b11a, b11b, b10, b01, b00 = b_sums
         halves = [
-            after(c10, dqkv0), links.flip(c11a, 2), c01, links.flip(c11b, 4),
+            after(c10, g0), links.flip(c11a, 2), c01, links.flip(c11b, 4),
             b10, links.flip(b11a, 2), b01, links.flip(b11b, 4),
         ]
         both_t = ((4, fine, 4 * width + b_cols), BF16)
         both10, both01 = run(add_half_kernel, halves, [both_t] * 2)
-        dqkv0 = after(dqkv0, both01)
-    g0, goth0, *attend_parts = run(
-        functools.partial(project_back_kernel, fast),
-        [links.info, base, full_a, rown0, roth0, rown1, roth1, dqkv1, doth1, dqkv0, doth0],
-        [row_f, ((others, width), BF16), *attend_outs],
-        [(whole_shape, F32)],
-        scalars=(0,),
-        micros=4,
-    )
+        goth0, send_a = after(goth0, both01), after(attend_parts[1], both01)
     inputs, back = run(
         send_kernel,
         [g0, links.collapse(goth0, group, rows), out],
         [row_f, ((local, 2 * width), BF16)],
     )
     if fast:
-        keep, got = after(attend_parts[0], back), links.flip(attend_parts[1], 1)
+        keep, got = after(attend_parts[0], back), links.flip(send_a, 1)
         a00, a01, a10, a11 = run(add_core_all_kernel, [keep, got], [(keep.shape[1:], BF16)] * 4)
         by_plane = [a00, links.flip(a11, 6), links.flip(a01, 2), links.flip(a10, 4)]
         both = links.line_first(
@@ -1006,9 +1016,9 @@
         )
         first_sums = both[0]
         by_plane[0] = after(by_plane[0], both[0])
-        attend_sums = links.line_first(add_four_kernel, by_plane, a00.shape[1:])
+        attend_sums = links.line_parts(add_four_kernel, by_plane, a00.shape[1:])
         both = links.line_last(both[0], after(both[1], attend_sums[0]), *both[2:])
-        attend_sums = links.line_last(*attend_sums)
+        attend_sums = [attend_sums[0], *(links.flip(attend_sums[k], 8 * k) for k in (1, 2, 3))]
         back = after(back, first_sums)
         output, input_grad = run(
             return_kernel,

time: 145 us -> 137 us (0.945)
  waiting for transfers between devices: 63.3 us -> 52.9 us
  starting transfers between devices: 39.2 us -> 41.4 us
    ppermute x40, waiting for transfers between devices: 59 us -> 48.5 us  [flip(): return lax.ppermute(value, AXES, [(i, i ^ bit) for i in range(self.count)])]
    ppermute x40, starting transfers between devices: 34.2 us -> 36.5 us  [flip(): return lax.ppermute(value, AXES, [(i, i ^ bit) for i in range(self.count)])]
  transfers between devices with their start and end apart: 46 -> 46, of which waited for: 23 -> 22; matrix products, arithmetic and copies ran while one was open for 0% -> 0% of each run, Pallas kernels for 10% -> 14%
where the time goes in v1:
time: 137 us
  waiting for transfers between devices  52.9 us (39%)
  starting transfers between devices  41.4 us (30%)
  Pallas kernels  40.9 us (30%)
    ppermute x40, waiting for transfers between devices, flip(): return lax.ppermute(value, AXES, [(i, i ^ bit) for i in range(self.count)])  48.5 us
    pallas_call x25, Pallas kernels, run(): pl.pallas_call(kernel, out_shape=[jax.ShapeDtypeStruct(s, t) for s, t in...  40.9 us
    ppermute x40, starting transfers between devices, flip(): return lax.ppermute(value, AXES, [(i, i ^ bit) for i in range(self.count)])  36.5 us
    ppermute x6, starting transfers between devices, flip_head(): lax.ppermute(value, 'head', [(i, i ^ bit) for i in range(self.heads)])  4.94 us
    ppermute x6, waiting for transfers between devices, flip_head(): lax.ppermute(value, 'head', [(i, i ^ bit) for i in range(self.heads)])  4.33 us
  transfers between devices with their start and end apart: 46, of which 22 were waited for; matrix products, arithmetic and copies ran while one was open for 0% of the time, Pallas kernels for 14%

profile of v1, /device:TPU:0, one launch (start us, length us, event | category | flops | bytes accessed | tf_op | source)
XLA Modules:
  0.0 136.9 jit_solution(45365792281811734)
XLA Ops:
  0.7 2.4 %shard_map.246 = (bf16[128,1152]{1,0:T(8,128)(2,1)S(1)}, bf16[128,1152]{1,0:T(8,128)(2,1)S(1)}, bf16[17,16,128]{2,1,0:T(8,128)(2,1)S(1)}, bf16[8,16,512]{2,1,0:T(8,128)(2,1)S(1)}) custom-call(s32[4]{0:T(128)S(1)} %pad_add_fusion.place_ref.rest_0_.me_ref.info_ref, bf16[2,128,512]{2,1,0:T(8,128)(2,1)} %tok_ref.1, bf16[2,128,512]{2,1,0:T(8,128)(2,1)} %cot_ref.1, ...), custom_call_target="tpu_custom_call" | custom-call | flops 57500000 | bytes 1513648 | tf_op jit(solution)/shard_map/pallas_call | solution.py:714
  3.2 3.0 %collective-permute-start = (bf16[128,1152]{1,0:T(8,128)(2,1)S(1)}, bf16[128,1152]{1,0:T(8,128)(2,1)S(1)}, u32[]{:S(2)}, u32[]{:S(2)}) collective-permute-start(bf16[128,1152]{1,0:T(8,128)(2,1)S(1)} %get-tuple-element.137), channel_id=1, source_target_pairs={{0,2},{1,3},{2,0},{3,1},{4,6},{5,7},{6,4},{7,5},{8,10},{9,11},{10,... | collective-permute-start | bytes 884744 | tf_op jit(solution)/shard_map/ppermute | solution.py:747
  6.2 3.6 %collective-permute-start.4 = (bf16[17,16,128]{2,1,0:T(8,128)(2,1)S(1)}, bf16[17,16,128]{2,1,0:T(8,128)(2,1)S(1)}, u32[]{:S(2)}, u32[]{:S(2)}) collective-permute-start(bf16[17,16,128]{2,1,0:T(8,128)(2,1)S(1)} %get-tuple-element.142.refs_0_), channel_id=1, source_target_pairs={{0,24},{1,25},{2,26},{3,27},{4,28},{5,29},{6,30},{7,31},{8,16},{9,... | collective-permute-start | bytes 208904 | tf_op jit(solution)/shard_map/ppermute | solution.py:744
  9.8 0.8 collective-permute-start.2
  10.6 2.6 %collective-permute-done.4.refs_3_ = bf16[17,16,128]{2,1,0:T(8,128)(2,1)S(1)} collective-permute-done((bf16[17,16,128]{2,1,0:T(8,128)(2,1)S(1)}, bf16[17,16,128]{2,1,0:T(8,128)(2,1)S(1)}, u32[]{:S(2)}, u32[]{:S(2)}) %collective-permute-start.4) | collective-permute-done | bytes 69664 | tf_op jit(solution)/shard_map/ppermute | solution.py:744
  13.1 2.3 %collective-permute-done.3.refs_2_ = bf16[17,16,128]{2,1,0:T(8,128)(2,1)S(1)} collective-permute-done((bf16[17,16,128]{2,1,0:T(8,128)(2,1)S(1)}, bf16[17,16,128]{2,1,0:T(8,128)(2,1)S(1)}, u32[]{:S(2)}, u32[]{:S(2)}) %collective-permute-start.3) | collective-permute-done | bytes 69664 | tf_op jit(solution)/shard_map/ppermute | solution.py:744
  15.9 1.6 %collective-permute-start.6 = (bf16[4,17,16,128]{3,2,1,0:T(8,128)(2,1)S(1)}, bf16[4,17,16,128]{3,2,1,0:T(8,128)(2,1)S(1)}, u32[]{:S(2)}, u32[]{:S(2)}) collective-permute-start(bf16[4,17,16,128]{3,2,1,0:T(8,128)(2,1)S(1)} %shard_map.248.rest_1_), channel_id=1, source_target_pairs={{0,4},{1,5},{2,6},{3,7},{4,0},{5,1},{6,2},{7,3},{8,12},{9,13},{10,... | collective-permute-start | bytes 835592 | tf_op jit(solution)/shard_map/ppermute | solution.py:744
  17.5 0.5 collective-permute-start.5
  18.0 1.5 %collective-permute-start.10 = (bf16[8,16,512]{2,1,0:T(8,128)(2,1)S(1)}, bf16[8,16,512]{2,1,0:T(8,128)(2,1)S(1)}, u32[]{:S(2)}, u32[]{:S(2)}) collective-permute-start(bf16[8,16,512]{2,1,0:T(8,128)(2,1)S(1)} %get-tuple-element.145.refs_0_), channel_id=1, source_target_pairs={{0,16},{1,17},{2,18},{3,19},{4,20},{5,21},{6,22},{7,23},{8,24},{9,... | collective-permute-start | bytes 393224 | tf_op jit(solution)/shard_map/ppermute | solution.py:744
  19.5 0.7 copy-done
  20.2 1.8 %shard_map.247 = (bf16[256,1152]{1,0:T(8,128)(2,1)S(1)}, f32[256,512]{1,0:T(8,128)S(1)}, bf16[256,512]{1,0:T(8,128)(2,1)S(1)}, f32[256,512]{1,0:T(8,128)S(1)}, s...) custom-call(s32[4]{0:T(128)S(1)} %pad_add_fusion.place_ref.rest_0_.me_ref.info_ref, s32[2,8]{1,0:T(2,128)S(1)} %bitcast.35, ...), custom_call_target="tpu_custom_call" | custom-call | flops 57500000 | bytes 2637904 | tf_op jit(solution)/shard_map/pallas_call | solution.py:714
  22.1 1.7 %collective-permute-start.9 = (bf16[8,16,512]{2,1,0:T(8,128)(2,1)S(1)}, bf16[8,16,512]{2,1,0:T(8,128)(2,1)S(1)}, u32[]{:S(2)}, u32[]{:S(2)}) collective-permute-start(bf16[8,16,512]{2,1,0:T(8,128)(2,1)S(1)} %get-tuple-element.145.refs_0_), channel_id=1, source_target_pairs={{0,8},{1,9},{2,10},{3,11},{4,12},{5,13},{6,14},{7,15},{8,0},{9,1},... | collective-permute-start | bytes 393224 | tf_op jit(solution)/shard_map/ppermute | solution.py:744
  23.8 1.9 %collective-permute-done.10.refs_2_ = bf16[8,16,512]{2,1,0:T(8,128)(2,1)S(1)} collective-permute-done((bf16[8,16,512]{2,1,0:T(8,128)(2,1)S(1)}, bf16[8,16,512]{2,1,0:T(8,128)(2,1)S(1)}, u32[]{:S(2)}, u32[]{:S(2)}) %collective-permute-start.10) | collective-permute-done | bytes 131104 | tf_op jit(solution)/shard_map/ppermute | solution.py:744
  25.7 2.1 %collective-permute-start.7 = (bf16[8,16,512]{2,1,0:T(8,128)(2,1)S(1)}, bf16[8,16,512]{2,1,0:T(8,128)(2,1)S(1)}, u32[]{:S(2)}, u32[]{:S(2)}) collective-permute-start(bf16[8,16,512]{2,1,0:T(8,128)(2,1)S(1)} %get-tuple-element.145.refs_0_), channel_id=1, source_target_pairs={{0,24},{1,25},{2,26},{3,27},{4,28},{5,29},{6,30},{7,31},{8,16},{9,... | collective-permute-start | bytes 393224 | tf_op jit(solution)/shard_map/ppermute | solution.py:744
  27.8 0.7 collective-permute-done.9.refs_1_
  28.4 4.0 %collective-permute-done.7.refs_3_ = bf16[8,16,512]{2,1,0:T(8,128)(2,1)S(1)} collective-permute-done((bf16[8,16,512]{2,1,0:T(8,128)(2,1)S(1)}, bf16[8,16,512]{2,1,0:T(8,128)(2,1)S(1)}, u32[]{:S(2)}, u32[]{:S(2)}) %collective-permute-start.7) | collective-permute-done | bytes 131104 | tf_op jit(solution)/shard_map/ppermute | solution.py:744
  32.4 0.7 shard_map.249.rest_1_
  33.2 1.5 %collective-permute-start.12 = (bf16[4,8,16,512]{3,2,1,0:T(8,128)(2,1)S(1)}, bf16[4,8,16,512]{3,2,1,0:T(8,128)(2,1)S(1)}, u32[]{:S(2)}, u32[]{:S(2)}) collective-permute-start(bf16[4,8,16,512]{3,2,1,0:T(8,128)(2,1)S(1)} %shard_map.249.rest_1_), channel_id=1, source_target_pairs={{0,2},{1,3},{2,0},{3,1},{4,6},{5,7},{6,4},{7,5},{8,10},{9,11},{10,... | collective-permute-start | bytes 1572872 | tf_op jit(solution)/shard_map/ppermute | solution.py:744
  35.2 0.5 collective-permute-start.8
  35.8 0.5 collective-permute-start.15
  36.3 11.7 %collective-permute-done.12.by_x_ref.rest_2_ = bf16[4,8,16,512]{3,2,1,0:T(8,128)(2,1)S(1)} collective-permute-done((bf16[4,8,16,512]{3,2,1,0:T(8,128)(2,1)S(1)}, bf16[4,8,16,512]{3,2,1,0:T(8,128)(2,1)S(1)}, u32[]{:S(2)}, u32[]{:S(2)}) %collective-permute-start.12) | collective-permute-done | bytes 524320 | tf_op jit(solution)/shard_map/ppermute | solution.py:744
  48.2 2.7 %collective-permute-done.8.rest_4_ = bf16[4,17,16,128]{3,2,1,0:T(8,128)(2,1)S(1)} collective-permute-done((bf16[4,17,16,128]{3,2,1,0:T(8,128)(2,1)S(1)}, bf16[4,17,16,128]{3,2,1,0:T(8,128)(2,1)S(1)}, u32[]{:S(2)}, u32[]{:S(2)}) %collective-permute-start.8) | collective-permute-done | bytes 278560 | tf_op jit(solution)/shard_map/ppermute | solution.py:744
  50.9 0.5 collective-permute-start.17
  51.4 1.5 %collective-permute-start.20 = (bf16[2,8,16,512]{3,2,1,0:T(8,128)(2,1)S(1)}, bf16[2,8,16,512]{3,2,1,0:T(8,128)(2,1)S(1)}, u32[]{:S(2)}, u32[]{:S(2)}) collective-permute-start(bf16[2,8,16,512]{3,2,1,0:T(8,128)(2,1)S(1)} %get-tuple-element.148), channel_id=1, source_target_pairs={{0,2},{1,3},{2,0},{3,1},{4,6},{5,7},{6,4},{7,5},{8,10},{9,11},{10,... | collective-permute-start | bytes 786440 | tf_op jit(solution)/shard_map/ppermute | solution.py:744
  52.9 0.5 collective-permute-start.21
  53.9 3.9 %shard_map.251 = (bf16[5,4,8,16,512]{4,3,2,1,0:T(8,128)(2,1)S(1)}, f32[8,512]{1,0:T(8,128)S(1)}, bf16[4,512,128]{2,1,0:T(8,128)(2,1)S(1)}, bf16[512,512]{1,0:T(8...) custom-call(bf16[256,512]{1,0:T(8,128)(2,1)S(1)} %get-tuple-element.139, ...), custom_call_target="tpu_custom_call" | custom-call | flops 9200000000 | bytes 9469968 | tf_op jit(solution)/shard_map/pallas_call | solution.py:714
  57.8 3.0 %collective-permute-done.21.rest_8_ = bf16[2,8,16,512]{3,2,1,0:T(8,128)(2,1)S(1)} collective-permute-done((bf16[2,8,16,512]{3,2,1,0:T(8,128)(2,1)S(1)}, bf16[2,8,16,512]{3,2,1,0:T(8,128)(2,1)S(1)}, u32[]{:S(2)}, u32[]{:S(2)}) %collective-permute-start.21) | collective-permute-done | bytes 262176 | tf_op jit(solution)/shard_map/ppermute | solution.py:744
  60.8 0.5 collective-permute-start.23
  62.7 3.3 %shard_map.253 = (bf16[4,4,8,16,512]{4,3,2,1,0:T(8,128)(2,1)S(1)}, bf16[4,8,4,16,512]{4,3,2,1,0:T(8,128)(2,1)S(1)}, bf16[256,2048]{1,0:T(8,128)(2,1)S(1)}, bf16[...) custom-call(f32[256,512]{1,0:T(8,128)S(1)} %get-tuple-element.153.n1, ...), custom_call_target="tpu_custom_call" | custom-call | flops 6325000192 | bytes 15024144 | tf_op jit(solution)/shard_map/pallas_call | solution.py:714
  66.3 1.4 %collective-permute-done.24 = bf16[1,256,512]{2,1,0:T(8,128)(2,1)S(1)} collective-permute-done((bf16[1,256,512]{2,1,0:T(8,128)(2,1)S(1)}, bf16[1,256,512]{2,1,0:T(8,128)(2,1)S(1)}, u32[]{:S(2)}, u32[]{:S(2)}) %collective-permute-start.24) | collective-permute-done | bytes 262176 | tf_op jit(solution)/shard_map/ppermute | solution.py:747
  67.7 10.4 %shard_map.254 = (f32[256,512]{1,0:T(8,128)S(1)}, f32[256,512]{1,0:T(8,128)S(1)}, bf16[256,512]{1,0:T(8,128)(2,1)S(1)}, bf16[256,512]{1,0:T(8,128)(2,1)S(1)}, bf...) custom-call(f32[256,512]{1,0:T(8,128)S(1)} %get-tuple-element.160.x_, ...), custom_call_target="tpu_custom_call" | custom-call | flops 18055000064 | bytes 15450112 | tf_op jit(solution)/shard_map/pallas_call | solution.py:714
  78.3 1.4 %collective-permute-done.25.more_ref = bf16[256,512]{1,0:T(8,128)(2,1)S(1)} collective-permute-done((bf16[256,512]{1,0:T(8,128)(2,1)S(1)}, bf16[256,512]{1,0:T(8,128)(2,1)S(1)}, u32[]{:S(2)}, u32[]{:S(2)}) %collective-permute-start.25) | collective-permute-done | bytes 262176 | tf_op jit(solution)/shard_map/ppermute | solution.py:747
  79.7 2.5 %shard_map.255 = (bf16[256,512]{1,0:T(8,128)(2,1)S(1)}, f32[256,512]{1,0:T(8,128)S(1)}, f32[256,512]{1,0:T(8,128)S(1)}, f32[5,8,512]{2,1,0:T(8,128)S(1)}, bf16[4...) custom-call(s32[4]{0:T(128)S(1)} %pad_add_fusion.place_ref.rest_0_.me_ref.info_ref, ...), custom_call_target="tpu_custom_call" | custom-call | flops 2300000000 | bytes 8028176 | tf_op jit(solution)/shard_map/pallas_call | solution.py:714
  82.4 1.8 %shard_map.256 = (bf16[256,2048]{1,0:T(8,128)(2,1)S(1)}, bf16[256,512]{1,0:T(8,128)(2,1)S(1)}, f32[256,512]{1,0:T(8,128)S(1)}, bf16[256,512]{1,0:T(8,128)(2,1)S(1)}, f32[5,8,512]{2,1,0:T(8,128)S(1)}) custom-call(bf16[256,512]{1,0:T(8,128)(2,1)S(1)} %get-tuple-element.175.b2_ref, f32[256,512]{1,0:T(8,128)S(1)} %get-tuple-element.176.gsec_ref, ...), custom_call_target="tpu_custom_call" | custom-call | flops 2529999872 | bytes 12107776 | tf_op jit(solution)/shard_map/pallas_call | solution.py:714
  84.2 0.7 collective-permute-done.26.got_ref
  85.2 2.2 %shard_map.258 = (bf16[4,4,16,2688]{3,2,1,0:T(8,128)(2,1)S(1)}, bf16[4,4,16,2688]{3,2,1,0:T(8,128)(2,1)S(1)}) custom-call(s32[4]{0:T(128)S(1)} %pad_add_fusion.place_ref.rest_0_.me_ref.info_ref, bf16[256,2048]{1,0:T(8,128)(2,1)S(1)} %get-tuple-element.189.b1_ref, bf16[256,512]{1,0:T(8,128)(2,1)S(1)} %get-tuple-element.190.b0_ref, ...), custom_call_target="tpu_custom_call" | custom-call | flops 2300000000 | bytes 6520848 | tf_op jit(solution)/shard_map/pallas_call | solution.py:714
  87.6 0.6 collective-permute-start.28
  88.2 0.6 collective-permute-start.29
  88.8 1.8 %collective-permute-done.27.got_ref = bf16[4,4,16,2688]{3,2,1,0:T(8,128)(2,1)S(1)} collective-permute-done((bf16[4,4,16,2688]{3,2,1,0:T(8,128)(2,1)S(1)}, bf16[4,4,16,2688]{3,2,1,0:T(8,128)(2,1)S(1)}, u32[]{:S(2)}, u32[]{:S(2)}) %collective-permute-start.27) | collective-permute-done | bytes 1376288 | tf_op jit(solution)/shard_map/ppermute | solution.py:744
  90.9 0.6 collective-permute-start.30
  91.5 0.6 collective-permute-start.31
  92.1 2.2 %shard_map.260 = (bf16[256,1536]{1,0:T(8,128)(2,1)S(1)}, bf16[256,1024]{1,0:T(8,128)(2,1)S(1)}) custom-call(bf16[256,512]{1,0:T(8,128)(2,1)S(1)} %get-tuple-element.200.gctx_ref, bf16[4,512,128]{2,1,0:T(8,128)(2,1)S(1)} %get-tuple-element.201.q2_ref, bf16[512,512]{1,0:T(8,128)(2,1)S(1)} %get-tuple-element.202.k_ref, ...), custom_call_target="tpu_custom_call" | custom-call | flops 3449999872 | bytes 5505024 | tf_op jit(solution)/shard_map/pallas_call | solution.py:714
  94.4 3.2 %shard_map.261 = (f32[256,512]{1,0:T(8,128)S(1)}, bf16[256,512]{1,0:T(8,128)(2,1)S(1)}, bf16[4,4,16,1536]{3,2,1,0:T(8,128)(2,1)S(1)}, bf16[4,4,16,1536]{3,2,1,0:T(8,128)(2,1)S(1)}) custom-call(s32[4]{0:T(128)S(1)} %pad_add_fusion.place_ref.rest_0_.me_ref.info_ref, f32[256,512]{1,0:T(8,128)S(1)} %get-tuple-element.181.base_ref, ...), custom_call_target="tpu_custom_call" | custom-call | flops 57500000 | bytes 9175056 | tf_op jit(solution)/shard_map/pallas_call | solution.py:714
  97.9 1.4 %collective-permute-start.35 = (bf16[4,16,4736]{2,1,0:T(8,128)(2,1)S(1)}, bf16[4,16,4736]{2,1,0:T(8,128)(2,1)S(1)}, u32[]{:S(2)}, u32[]{:S(2)}) collective-permute-start(bf16[4,16,4736]{2,1,0:T(8,128)(2,1)S(1)} %get-tuple-element.228), channel_id=1, source_target_pairs={{0,4},{1,5},{2,6},{3,7},{4,0},{5,1},{6,2},{7,3},{8,12},{9,13},{10,... | collective-permute-start | bytes 1818632 | tf_op jit(solution)/shard_map/ppermute | solution.py:744
  99.3 1.5 %collective-permute-start.34 = (bf16[4,16,4736]{2,1,0:T(8,128)(2,1)S(1)}, bf16[4,16,4736]{2,1,0:T(8,128)(2,1)S(1)}, u32[]{:S(2)}, u32[]{:S(2)}) collective-permute-start(bf16[4,16,4736]{2,1,0:T(8,128)(2,1)S(1)} %get-tuple-element.216), channel_id=1, source_target_pairs={{0,2},{1,3},{2,0},{3,1},{4,6},{5,7},{6,4},{7,5},{8,10},{9,11},{10,... | collective-permute-start | bytes 1818632 | tf_op jit(solution)/shard_map/ppermute | solution.py:744
  100.8 1.5 %collective-permute-done.32.more_ref = bf16[256,512]{1,0:T(8,128)(2,1)S(1)} collective-permute-done((bf16[256,512]{1,0:T(8,128)(2,1)S(1)}, bf16[256,512]{1,0:T(8,128)(2,1)S(1)}, u32[]{:S(2)}, u32[]{:S(2)}) %collective-permute-start.32) | collective-permute-done | bytes 262176 | tf_op jit(solution)/shard_map/ppermute | solution.py:747
  102.6 0.8 collective-permute-start.37
  103.4 1.5 %collective-permute-start.38 = (bf16[4,16,1536]{2,1,0:T(8,128)(2,1)S(1)}, bf16[4,16,1536]{2,1,0:T(8,128)(2,1)S(1)}, u32[]{:S(2)}, u32[]{:S(2)}) collective-permute-start(bf16[4,16,1536]{2,1,0:T(8,128)(2,1)S(1)} %get-tuple-element.235), channel_id=1, source_target_pairs={{0,2},{1,3},{2,0},{3,1},{4,6},{5,7},{6,4},{7,5},{8,10},{9,11},{10,... | collective-permute-start | bytes 589832 | tf_op jit(solution)/shard_map/ppermute | solution.py:744
  104.8 1.3 collective-permute-start.39
  106.2 8.4 %collective-permute-done.35.got_y_ref = bf16[4,16,4736]{2,1,0:T(8,128)(2,1)S(1)} collective-permute-done((bf16[4,16,4736]{2,1,0:T(8,128)(2,1)S(1)}, bf16[4,16,4736]{2,1,0:T(8,128)(2,1)S(1)}, u32[]{:S(2)}, u32[]{:S(2)}) %collective-permute-start.35) | collective-permute-done | bytes 606240 | tf_op jit(solution)/shard_map/ppermute | solution.py:744
  114.5 1.3 collective-permute-done.34.got_x_ref
  115.8 0.8 shard_map.265
  116.7 2.0 %collective-permute-start.41 = (bf16[16,4736]{1,0:T(8,128)(2,1)S(1)}, bf16[16,4736]{1,0:T(8,128)(2,1)S(1)}, u32[]{:S(2)}, u32[]{:S(2)}) collective-permute-start(bf16[16,4736]{1,0:T(8,128)(2,1)S(1)} %get-tuple-element.243), channel_id=1, source_target_pairs={{0,8},{1,9},{2,10},{3,11},{4,12},{5,13},{6,14},{7,15},{8,0},{9,1},... | collective-permute-start | bytes 454664 | tf_op jit(solution)/shard_map/ppermute | solution.py:744
  118.7 1.5 %collective-permute-done.37.b_ref = bf16[4,16,1536]{2,1,0:T(8,128)(2,1)S(1)} collective-permute-done((bf16[4,16,1536]{2,1,0:T(8,128)(2,1)S(1)}, bf16[4,16,1536]{2,1,0:T(8,128)(2,1)S(1)}, u32[]{:S(2)}, u32[]{:S(2)}) %collective-permute-start.37) | collective-permute-done | bytes 196640 | tf_op jit(solution)/shard_map/ppermute | solution.py:744
  120.2 1.5 %collective-permute-start.36 = (bf16[128,1024]{1,0:T(8,128)(2,1)S(1)}, bf16[128,1024]{1,0:T(8,128)(2,1)S(1)}, u32[]{:S(2)}, u32[]{:S(2)}) collective-permute-start(bf16[128,1024]{1,0:T(8,128)(2,1)S(1)} %get-tuple-element.230), channel_id=1, source_target_pairs={{0,2},{1,3},{2,0},{3,1},{4,6},{5,7},{6,4},{7,5},{8,10},{9,11},{10,... | collective-permute-start | bytes 786440 | tf_op jit(solution)/shard_map/ppermute | solution.py:747
  121.7 2.6 %collective-permute-done.38.c_ref = bf16[4,16,1536]{2,1,0:T(8,128)(2,1)S(1)} collective-permute-done((bf16[4,16,1536]{2,1,0:T(8,128)(2,1)S(1)}, bf16[4,16,1536]{2,1,0:T(8,128)(2,1)S(1)}, u32[]{:S(2)}, u32[]{:S(2)}) %collective-permute-start.38) | collective-permute-done | bytes 196640 | tf_op jit(solution)/shard_map/ppermute | solution.py:744
  124.3 0.7 shard_map.267
  125.0 2.4 %collective-permute-start.42 = (bf16[16,4736]{1,0:T(8,128)(2,1)S(1)}, bf16[16,4736]{1,0:T(8,128)(2,1)S(1)}, u32[]{:S(2)}, u32[]{:S(2)}) collective-permute-start(bf16[16,4736]{1,0:T(8,128)(2,1)S(1)} %shard_map.268), channel_id=1, source_target_pairs={{0,24},{1,25},{2,26},{3,27},{4,28},{5,29},{6,30},{7,31},{8,16},{9,... | collective-permute-start | bytes 454664 | tf_op jit(solution)/shard_map/ppermute | solution.py:744
  127.4 2.1 %collective-permute-start.44 = (bf16[16,1536]{1,0:T(8,128)(2,1)S(1)}, bf16[16,1536]{1,0:T(8,128)(2,1)S(1)}, u32[]{:S(2)}, u32[]{:S(2)}) collective-permute-start(bf16[16,1536]{1,0:T(8,128)(2,1)S(1)} %get-tuple-element.247), channel_id=1, source_target_pairs={{0,16},{1,17},{2,18},{3,19},{4,20},{5,21},{6,22},{7,23},{8,24},{9,... | collective-permute-start | bytes 147464 | tf_op jit(solution)/shard_map/ppermute | solution.py:744
  129.5 2.3 %collective-permute-start.45 = (bf16[16,1536]{1,0:T(8,128)(2,1)S(1)}, bf16[16,1536]{1,0:T(8,128)(2,1)S(1)}, u32[]{:S(2)}, u32[]{:S(2)}) collective-permute-start(bf16[16,1536]{1,0:T(8,128)(2,1)S(1)} %get-tuple-element.248), channel_id=1, source_target_pairs={{0,24},{1,25},{2,26},{3,27},{4,28},{5,29},{6,30},{7,31},{8,16},{9,... | collective-permute-start | bytes 147464 | tf_op jit(solution)/shard_map/ppermute | solution.py:744
  131.8 1.6 %shard_map.266 = (f32[2,128,512]{2,1,0:T(8,128)}, f32[2,128,512]{2,1,0:T(8,128)}) custom-call(s32[4]{0:T(128)S(1)} %pad_add_fusion.place_ref.rest_0_.me_ref.info_ref, f32[256,512]{1,0:T(8,128)S(1)} %get-tuple-element.166.out_ref, f32[256,512]{1,0:T(8,128)S(1)} %get-tuple-element.218.in_ref, bf16[128,1024]{1,0:T(8,128)(2,1)S(1)} %collective-permute-done.36.back_ref), custom_call_target="tpu_custom_call" | custom-call | flops 57500000 | bytes 2359312 | tf_op jit(solution)/shard_map/pallas_call | solution.py:714
  133.4 0.7 shard_map.269
  134.1 2.2 %collective-permute-done.44.c_ref = bf16[16,1536]{1,0:T(8,128)(2,1)S(1)} collective-permute-done((bf16[16,1536]{1,0:T(8,128)(2,1)S(1)}, bf16[16,1536]{1,0:T(8,128)(2,1)S(1)}, u32[]{:S(2)}, u32[]{:S(2)}) %collective-permute-start.44) | collective-permute-done | bytes 49184 | tf_op jit(solution)/shard_map/ppermute | solution.py:744
  136.3 0.6 shard_map.270
  (56 shorter events, 5.4 us)
Async XLA Ops:
  3.2 12.7 %collective-permute-start = (bf16[128,1152]{1,0:T(8,128)(2,1)S(1)}, bf16[128,1152]{1,0:T(8,128)(2,1)S(1)}, u32[]{:S(2)}, u32[]{:S(2)}) collective-permute-start(bf16[128,1152]{1,0:T(8,128)(2,1)S(1)} %get-tuple-element.137), channel_id=1, source_target_pairs={{0,2},{1,3},{2,0},{3,1},{4,6},{5,7},{6,4},{7,5},{8,10},{9,11},{10,... | collective-permute-start | bytes 884744 | tf_op jit(solution)/shard_map/ppermute | solution.py:747
  6.2 7.0 %collective-permute-start.4 = (bf16[17,16,128]{2,1,0:T(8,128)(2,1)S(1)}, bf16[17,16,128]{2,1,0:T(8,128)(2,1)S(1)}, u32[]{:S(2)}, u32[]{:S(2)}) collective-permute-start(bf16[17,16,128]{2,1,0:T(8,128)(2,1)S(1)} %get-tuple-element.142.refs_0_), channel_id=1, source_target_pairs={{0,24},{1,25},{2,26},{3,27},{4,28},{5,29},{6,30},{7,31},{8,16},{9,... | collective-permute-start | bytes 208904 | tf_op jit(solution)/shard_map/ppermute | solution.py:744
  9.8 5.7 %collective-permute-start.3 = (bf16[17,16,128]{2,1,0:T(8,128)(2,1)S(1)}, bf16[17,16,128]{2,1,0:T(8,128)(2,1)S(1)}, u32[]{:S(2)}, u32[]{:S(2)}) collective-permute-start(bf16[17,16,128]{2,1,0:T(8,128)(2,1)S(1)} %get-tuple-element.142.refs_0_), channel_id=1, source_target_pairs={{0,16},{1,17},{2,18},{3,19},{4,20},{5,21},{6,22},{7,23},{8,24},{9,... | collective-permute-start | bytes 208904 | tf_op jit(solution)/shard_map/ppermute | solution.py:744
  9.8 5.7 %collective-permute-start.2 = (bf16[17,16,128]{2,1,0:T(8,128)(2,1)S(1)}, bf16[17,16,128]{2,1,0:T(8,128)(2,1)S(1)}, u32[]{:S(2)}, u32[]{:S(2)}) collective-permute-start(bf16[17,16,128]{2,1,0:T(8,128)(2,1)S(1)} %get-tuple-element.142.refs_0_), channel_id=1, source_target_pairs={{0,8},{1,9},{2,10},{3,11},{4,12},{5,13},{6,14},{7,15},{8,0},{9,1},... | collective-permute-start | bytes 208904 | tf_op jit(solution)/shard_map/ppermute | solution.py:744
  15.9 17.2 %collective-permute-start.6 = (bf16[4,17,16,128]{3,2,1,0:T(8,128)(2,1)S(1)}, bf16[4,17,16,128]{3,2,1,0:T(8,128)(2,1)S(1)}, u32[]{:S(2)}, u32[]{:S(2)}) collective-permute-start(bf16[4,17,16,128]{3,2,1,0:T(8,128)(2,1)S(1)} %shard_map.248.rest_1_), channel_id=1, source_target_pairs={{0,4},{1,5},{2,6},{3,7},{4,0},{5,1},{6,2},{7,3},{8,12},{9,13},{10,... | collective-permute-start | bytes 835592 | tf_op jit(solution)/shard_map/ppermute | solution.py:744
  17.5 15.7 %collective-permute-start.5 = (bf16[4,17,16,128]{3,2,1,0:T(8,128)(2,1)S(1)}, bf16[4,17,16,128]{3,2,1,0:T(8,128)(2,1)S(1)}, u32[]{:S(2)}, u32[]{:S(2)}) collective-permute-start(bf16[4,17,16,128]{3,2,1,0:T(8,128)(2,1)S(1)} %shard_map.248.rest_1_), channel_id=1, source_target_pairs={{0,2},{1,3},{2,0},{3,1},{4,6},{5,7},{6,4},{7,5},{8,10},{9,11},{10,... | collective-permute-start | bytes 835592 | tf_op jit(solution)/shard_map/ppermute | solution.py:744
  18.0 7.7 %collective-permute-start.10 = (bf16[8,16,512]{2,1,0:T(8,128)(2,1)S(1)}, bf16[8,16,512]{2,1,0:T(8,128)(2,1)S(1)}, u32[]{:S(2)}, u32[]{:S(2)}) collective-permute-start(bf16[8,16,512]{2,1,0:T(8,128)(2,1)S(1)} %get-tuple-element.145.refs_0_), channel_id=1, source_target_pairs={{0,16},{1,17},{2,18},{3,19},{4,20},{5,21},{6,22},{7,23},{8,24},{9,... | collective-permute-start | bytes 393224 | tf_op jit(solution)/shard_map/ppermute | solution.py:744
  19.5 0.7 copy-start
  22.0 11.1 %collective-permute-start.1 = (bf16[1,256,512]{2,1,0:T(8,128)(2,1)S(1)}, bf16[1,256,512]{2,1,0:T(8,128)(2,1)S(1)}, u32[]{:S(2)}, u32[]{:S(2)}) collective-permute-start(bf16[1,256,512]{2,1,0:T(8,128)(2,1)S(1)} %bitcast.29), channel_id=1, source_target_pairs={{0,1},{1,0},{2,3},{3,2},{4,5},{5,4},{6,7},{7,6},{8,9},{9,8},{10,11... | collective-permute-start | bytes 786440 | tf_op jit(solution)/shard_map/ppermute | solution.py:747
  22.1 6.3 %collective-permute-start.9 = (bf16[8,16,512]{2,1,0:T(8,128)(2,1)S(1)}, bf16[8,16,512]{2,1,0:T(8,128)(2,1)S(1)}, u32[]{:S(2)}, u32[]{:S(2)}) collective-permute-start(bf16[8,16,512]{2,1,0:T(8,128)(2,1)S(1)} %get-tuple-element.145.refs_0_), channel_id=1, source_target_pairs={{0,8},{1,9},{2,10},{3,11},{4,12},{5,13},{6,14},{7,15},{8,0},{9,1},... | collective-permute-start | bytes 393224 | tf_op jit(solution)/shard_map/ppermute | solution.py:744
  25.7 6.8 %collective-permute-start.7 = (bf16[8,16,512]{2,1,0:T(8,128)(2,1)S(1)}, bf16[8,16,512]{2,1,0:T(8,128)(2,1)S(1)}, u32[]{:S(2)}, u32[]{:S(2)}) collective-permute-start(bf16[8,16,512]{2,1,0:T(8,128)(2,1)S(1)} %get-tuple-element.145.refs_0_), channel_id=1, source_target_pairs={{0,24},{1,25},{2,26},{3,27},{4,28},{5,29},{6,30},{7,31},{8,16},{9,... | collective-permute-start | bytes 393224 | tf_op jit(solution)/shard_map/ppermute | solution.py:744
  33.2 14.8 %collective-permute-start.12 = (bf16[4,8,16,512]{3,2,1,0:T(8,128)(2,1)S(1)}, bf16[4,8,16,512]{3,2,1,0:T(8,128)(2,1)S(1)}, u32[]{:S(2)}, u32[]{:S(2)}) collective-permute-start(bf16[4,8,16,512]{3,2,1,0:T(8,128)(2,1)S(1)} %shard_map.249.rest_1_), channel_id=1, source_target_pairs={{0,2},{1,3},{2,0},{3,1},{4,6},{5,7},{6,4},{7,5},{8,10},{9,11},{10,... | collective-permute-start | bytes 1572872 | tf_op jit(solution)/shard_map/ppermute | solution.py:744
  34.7 13.2 %collective-permute-start.11 = (bf16[4,8,16,512]{3,2,1,0:T(8,128)(2,1)S(1)}, bf16[4,8,16,512]{3,2,1,0:T(8,128)(2,1)S(1)}, u32[]{:S(2)}, u32[]{:S(2)}) collective-permute-start(bf16[4,8,16,512]{3,2,1,0:T(8,128)(2,1)S(1)} %shard_map.249.rest_1_), channel_id=1, source_target_pairs={{0,4},{1,5},{2,6},{3,7},{4,0},{5,1},{6,2},{7,3},{8,12},{9,13},{10,... | collective-permute-start | bytes 1572872 | tf_op jit(solution)/shard_map/ppermute | solution.py:744
  35.2 15.7 %collective-permute-start.8 = (bf16[4,17,16,128]{3,2,1,0:T(8,128)(2,1)S(1)}, bf16[4,17,16,128]{3,2,1,0:T(8,128)(2,1)S(1)}, u32[]{:S(2)}, u32[]{:S(2)}) collective-permute-start(bf16[4,17,16,128]{3,2,1,0:T(8,128)(2,1)S(1)} %collective-permute-done.6.rest_3_), channel_id=1, source_target_pairs={{0,2},{1,3},{2,0},{3,1},{4,6},{5,7},{6,4},{7,5},{8,10},{9,11},{10,... | collective-permute-start | bytes 835592 | tf_op jit(solution)/shard_map/ppermute | solution.py:744
  35.8 15.7 %collective-permute-start.13 = (bf16[4,17,16,128]{3,2,1,0:T(8,128)(2,1)S(1)}, bf16[4,17,16,128]{3,2,1,0:T(8,128)(2,1)S(1)}, u32[]{:S(2)}, u32[]{:S(2)}) collective-permute-start(bf16[4,17,16,128]{3,2,1,0:T(8,128)(2,1)S(1)} %shard_map.248.rest_1_), channel_id=1, source_target_pairs={{0,1},{1,0},{2,3},{3,2},{4,5},{5,4},{6,7},{7,6},{8,9},{9,8},{10,11... | collective-permute-start | bytes 835592 | tf_op jit(solution)/shard_map/ppermute | solution.py:744
  35.8 17.1 %collective-permute-start.15 = (bf16[4,17,16,128]{3,2,1,0:T(8,128)(2,1)S(1)}, bf16[4,17,16,128]{3,2,1,0:T(8,128)(2,1)S(1)}, u32[]{:S(2)}, u32[]{:S(2)}) collective-permute-start(bf16[4,17,16,128]{3,2,1,0:T(8,128)(2,1)S(1)} %collective-permute-done.6.rest_3_), channel_id=1, source_target_pairs={{0,1},{1,0},{2,3},{3,2},{4,5},{5,4},{6,7},{7,6},{8,9},{9,8},{10,11... | collective-permute-start | bytes 835592 | tf_op jit(solution)/shard_map/ppermute | solution.py:744
  47.9 5.5 %collective-permute-start.14 = (bf16[4,17,16,128]{3,2,1,0:T(8,128)(2,1)S(1)}, bf16[4,17,16,128]{3,2,1,0:T(8,128)(2,1)S(1)}, u32[]{:S(2)}, u32[]{:S(2)}) collective-permute-start(bf16[4,17,16,128]{3,2,1,0:T(8,128)(2,1)S(1)} %collective-permute-done.5.rest_2_), channel_id=1, source_target_pairs={{0,1},{1,0},{2,3},{3,2},{4,5},{5,4},{6,7},{7,6},{8,9},{9,8},{10,11... | collective-permute-start | bytes 835592 | tf_op jit(solution)/shard_map/ppermute | solution.py:744
  50.9 2.5 %collective-permute-start.16 = (bf16[4,17,16,128]{3,2,1,0:T(8,128)(2,1)S(1)}, bf16[4,17,16,128]{3,2,1,0:T(8,128)(2,1)S(1)}, u32[]{:S(2)}, u32[]{:S(2)}) collective-permute-start(bf16[4,17,16,128]{3,2,1,0:T(8,128)(2,1)S(1)} %collective-permute-done.8.rest_4_), channel_id=1, source_target_pairs={{0,1},{1,0},{2,3},{3,2},{4,5},{5,4},{6,7},{7,6},{8,9},{9,8},{10,11... | collective-permute-start | bytes 835592 | tf_op jit(solution)/shard_map/ppermute | solution.py:744
  50.9 10.9 %collective-permute-start.17 = (bf16[4,8,16,512]{3,2,1,0:T(8,128)(2,1)S(1)}, bf16[4,8,16,512]{3,2,1,0:T(8,128)(2,1)S(1)}, u32[]{:S(2)}, u32[]{:S(2)}) collective-permute-start(bf16[4,8,16,512]{3,2,1,0:T(8,128)(2,1)S(1)} %shard_map.249.rest_1_), channel_id=1, source_target_pairs={{0,1},{1,0},{2,3},{3,2},{4,5},{5,4},{6,7},{7,6},{8,9},{9,8},{10,11... | collective-permute-start | bytes 1572872 | tf_op jit(solution)/shard_map/ppermute | solution.py:744
  51.4 9.4 %collective-permute-start.20 = (bf16[2,8,16,512]{3,2,1,0:T(8,128)(2,1)S(1)}, bf16[2,8,16,512]{3,2,1,0:T(8,128)(2,1)S(1)}, u32[]{:S(2)}, u32[]{:S(2)}) collective-permute-start(bf16[2,8,16,512]{3,2,1,0:T(8,128)(2,1)S(1)} %get-tuple-element.148), channel_id=1, source_target_pairs={{0,2},{1,3},{2,0},{3,1},{4,6},{5,7},{6,4},{7,5},{8,10},{9,11},{10,... | collective-permute-start | bytes 786440 | tf_op jit(solution)/shard_map/ppermute | solution.py:744
  52.9 7.9 %collective-permute-start.21 = (bf16[2,8,16,512]{3,2,1,0:T(8,128)(2,1)S(1)}, bf16[2,8,16,512]{3,2,1,0:T(8,128)(2,1)S(1)}, u32[]{:S(2)}, u32[]{:S(2)}) collective-permute-start(bf16[2,8,16,512]{3,2,1,0:T(8,128)(2,1)S(1)} %get-tuple-element.158), channel_id=1, source_target_pairs={{0,4},{1,5},{2,6},{3,7},{4,0},{5,1},{6,2},{7,3},{8,12},{9,13},{10,... | collective-permute-start | bytes 786440 | tf_op jit(solution)/shard_map/ppermute | solution.py:744
  53.4 8.4 %collective-permute-start.18 = (bf16[4,8,16,512]{3,2,1,0:T(8,128)(2,1)S(1)}, bf16[4,8,16,512]{3,2,1,0:T(8,128)(2,1)S(1)}, u32[]{:S(2)}, u32[]{:S(2)}) collective-permute-start(bf16[4,8,16,512]{3,2,1,0:T(8,128)(2,1)S(1)} %collective-permute-done.12.by_x_ref.rest_2_), channel_id=1, source_target_pairs={{0,1},{1,0},{2,3},{3,2},{4,5},{5,4},{6,7},{7,6},{8,9},{9,8},{10,11... | collective-permute-start | bytes 1572872 | tf_op jit(solution)/shard_map/ppermute | solution.py:744
  53.4 8.4 %collective-permute-start.19 = (bf16[4,8,16,512]{3,2,1,0:T(8,128)(2,1)S(1)}, bf16[4,8,16,512]{3,2,1,0:T(8,128)(2,1)S(1)}, u32[]{:S(2)}, u32[]{:S(2)}) collective-permute-start(bf16[4,8,16,512]{3,2,1,0:T(8,128)(2,1)S(1)} %collective-permute-done.11.by_y_ref.rest_3_), channel_id=1, source_target_pairs={{0,1},{1,0},{2,3},{3,2},{4,5},{5,4},{6,7},{7,6},{8,9},{9,8},{10,11... | collective-permute-start | bytes 1572872 | tf_op jit(solution)/shard_map/ppermute | solution.py:744
  60.8 1.5 %collective-permute-start.22 = (bf16[2,8,16,512]{3,2,1,0:T(8,128)(2,1)S(1)}, bf16[2,8,16,512]{3,2,1,0:T(8,128)(2,1)S(1)}, u32[]{:S(2)}, u32[]{:S(2)}) collective-permute-start(bf16[2,8,16,512]{3,2,1,0:T(8,128)(2,1)S(1)} %collective-permute-done.20.rest_7_), channel_id=1, source_target_pairs={{0,1},{1,0},{2,3},{3,2},{4,5},{5,4},{6,7},{7,6},{8,9},{9,8},{10,11... | collective-permute-start | bytes 786440 | tf_op jit(solution)/shard_map/ppermute | solution.py:744
  60.8 1.9 %collective-permute-start.23 = (bf16[2,8,16,512]{3,2,1,0:T(8,128)(2,1)S(1)}, bf16[2,8,16,512]{3,2,1,0:T(8,128)(2,1)S(1)}, u32[]{:S(2)}, u32[]{:S(2)}) collective-permute-start(bf16[2,8,16,512]{3,2,1,0:T(8,128)(2,1)S(1)} %collective-permute-done.21.rest_8_), channel_id=1, source_target_pairs={{0,1},{1,0},{2,3},{3,2},{4,5},{5,4},{6,7},{7,6},{8,9},{9,8},{10,11... | collective-permute-start | bytes 786440 | tf_op jit(solution)/shard_map/ppermute | solution.py:744
  66.1 1.6 %collective-permute-start.24 = (bf16[1,256,512]{2,1,0:T(8,128)(2,1)S(1)}, bf16[1,256,512]{2,1,0:T(8,128)(2,1)S(1)}, u32[]{:S(2)}, u32[]{:S(2)}) collective-permute-start(bf16[1,256,512]{2,1,0:T(8,128)(2,1)S(1)} %bitcast.32), channel_id=1, source_target_pairs={{0,1},{1,0},{2,3},{3,2},{4,5},{5,4},{6,7},{7,6},{8,9},{9,8},{10,11... | collective-permute-start | bytes 786440 | tf_op jit(solution)/shard_map/ppermute | solution.py:747
  78.1 1.6 %collective-permute-start.25 = (bf16[256,512]{1,0:T(8,128)(2,1)S(1)}, bf16[256,512]{1,0:T(8,128)(2,1)S(1)}, u32[]{:S(2)}, u32[]{:S(2)}) collective-permute-start(bf16[256,512]{1,0:T(8,128)(2,1)S(1)} %get-tuple-element.168), channel_id=1, source_target_pairs={{0,1},{1,0},{2,3},{3,2},{4,5},{5,4},{6,7},{7,6},{8,9},{9,8},{10,11... | collective-permute-start | bytes 786440 | tf_op jit(solution)/shard_map/ppermute | solution.py:747
  82.2 2.7 %collective-permute-start.26 = (bf16[4,4,64,512]{3,2,1,0:T(8,128)(2,1)S(1)}, bf16[4,4,64,512]{3,2,1,0:T(8,128)(2,1)S(1)}, u32[]{:S(2)}, u32[]{:S(2)}) collective-permute-start(bf16[4,4,64,512]{3,2,1,0:T(8,128)(2,1)S(1)} %get-tuple-element.187), channel_id=1, source_target_pairs={{0,1},{1,0},{2,3},{3,2},{4,5},{5,4},{6,7},{7,6},{8,9},{9,8},{10,11... | collective-permute-start | bytes 3145736 | tf_op jit(solution)/shard_map/ppermute | solution.py:744
  87.4 3.2 %collective-permute-start.27 = (bf16[4,4,16,2688]{3,2,1,0:T(8,128)(2,1)S(1)}, bf16[4,4,16,2688]{3,2,1,0:T(8,128)(2,1)S(1)}, u32[]{:S(2)}, u32[]{:S(2)}) collective-permute-start(bf16[4,4,16,2688]{3,2,1,0:T(8,128)(2,1)S(1)} %get-tuple-element.198), channel_id=1, source_target_pairs={{0,1},{1,0},{2,3},{3,2},{4,5},{5,4},{6,7},{7,6},{8,9},{9,8},{10,11... | collective-permute-start | bytes 4128776 | tf_op jit(solution)/shard_map/ppermute | solution.py:744
  87.6 10.0 %collective-permute-start.28 = (bf16[2,64,512]{2,1,0:T(8,128)(2,1)S(1)}, bf16[2,64,512]{2,1,0:T(8,128)(2,1)S(1)}, u32[]{:S(2)}, u32[]{:S(2)}) collective-permute-start(bf16[2,64,512]{2,1,0:T(8,128)(2,1)S(1)} %get-tuple-element.188), channel_id=1, source_target_pairs={{0,2},{1,3},{2,0},{3,1},{4,6},{5,7},{6,4},{7,5},{8,10},{9,11},{10,... | collective-permute-start | bytes 393224 | tf_op jit(solution)/shard_map/ppermute | solution.py:744
  88.2 9.4 %collective-permute-start.29 = (bf16[2,64,512]{2,1,0:T(8,128)(2,1)S(1)}, bf16[2,64,512]{2,1,0:T(8,128)(2,1)S(1)}, u32[]{:S(2)}, u32[]{:S(2)}) collective-permute-start(bf16[2,64,512]{2,1,0:T(8,128)(2,1)S(1)} %get-tuple-element.212), channel_id=1, source_target_pairs={{0,4},{1,5},{2,6},{3,7},{4,0},{5,1},{6,2},{7,3},{8,12},{9,13},{10,... | collective-permute-start | bytes 393224 | tf_op jit(solution)/shard_map/ppermute | solution.py:744
  90.9 6.8 %collective-permute-start.30 = (bf16[2,16,2688]{2,1,0:T(8,128)(2,1)S(1)}, bf16[2,16,2688]{2,1,0:T(8,128)(2,1)S(1)}, u32[]{:S(2)}, u32[]{:S(2)}) collective-permute-start(bf16[2,16,2688]{2,1,0:T(8,128)(2,1)S(1)} %get-tuple-element.199), channel_id=1, source_target_pairs={{0,2},{1,3},{2,0},{3,1},{4,6},{5,7},{6,4},{7,5},{8,10},{9,11},{10,... | collective-permute-start | bytes 516104 | tf_op jit(solution)/shard_map/ppermute | solution.py:744
  91.5 6.1 %collective-permute-start.31 = (bf16[2,16,2688]{2,1,0:T(8,128)(2,1)S(1)}, bf16[2,16,2688]{2,1,0:T(8,128)(2,1)S(1)}, u32[]{:S(2)}, u32[]{:S(2)}) collective-permute-start(bf16[2,16,2688]{2,1,0:T(8,128)(2,1)S(1)} %get-tuple-element.215), channel_id=1, source_target_pairs={{0,4},{1,5},{2,6},{3,7},{4,0},{5,1},{6,2},{7,3},{8,12},{9,13},{10,... | collective-permute-start | bytes 516104 | tf_op jit(solution)/shard_map/ppermute | solution.py:744
  97.8 4.6 %collective-permute-start.33 = (bf16[4,4,16,1536]{3,2,1,0:T(8,128)(2,1)S(1)}, bf16[4,4,16,1536]{3,2,1,0:T(8,128)(2,1)S(1)}, u32[]{:S(2)}, u32[]{:S(2)}) collective-permute-start(bf16[4,4,16,1536]{3,2,1,0:T(8,128)(2,1)S(1)} %get-tuple-element.224), channel_id=1, source_target_pairs={{0,1},{1,0},{2,3},{3,2},{4,5},{5,4},{6,7},{7,6},{8,9},{9,8},{10,11... | collective-permute-start | bytes 2359304 | tf_op jit(solution)/shard_map/ppermute | solution.py:744
  97.9 16.6 %collective-permute-start.35 = (bf16[4,16,4736]{2,1,0:T(8,128)(2,1)S(1)}, bf16[4,16,4736]{2,1,0:T(8,128)(2,1)S(1)}, u32[]{:S(2)}, u32[]{:S(2)}) collective-permute-start(bf16[4,16,4736]{2,1,0:T(8,128)(2,1)S(1)} %get-tuple-element.228), channel_id=1, source_target_pairs={{0,4},{1,5},{2,6},{3,7},{4,0},{5,1},{6,2},{7,3},{8,12},{9,13},{10,... | collective-permute-start | bytes 1818632 | tf_op jit(solution)/shard_map/ppermute | solution.py:744
  99.3 16.5 %collective-permute-start.34 = (bf16[4,16,4736]{2,1,0:T(8,128)(2,1)S(1)}, bf16[4,16,4736]{2,1,0:T(8,128)(2,1)S(1)}, u32[]{:S(2)}, u32[]{:S(2)}) collective-permute-start(bf16[4,16,4736]{2,1,0:T(8,128)(2,1)S(1)} %get-tuple-element.216), channel_id=1, source_target_pairs={{0,2},{1,3},{2,0},{3,1},{4,6},{5,7},{6,4},{7,5},{8,10},{9,11},{10,... | collective-permute-start | bytes 1818632 | tf_op jit(solution)/shard_map/ppermute | solution.py:744
  100.8 1.5 %collective-permute-start.32 = (bf16[256,512]{1,0:T(8,128)(2,1)S(1)}, bf16[256,512]{1,0:T(8,128)(2,1)S(1)}, u32[]{:S(2)}, u32[]{:S(2)}) collective-permute-start(bf16[256,512]{1,0:T(8,128)(2,1)S(1)} %get-tuple-element.217), channel_id=1, source_target_pairs={{0,1},{1,0},{2,3},{3,2},{4,5},{5,4},{6,7},{7,6},{8,9},{9,8},{10,11... | collective-permute-start | bytes 786440 | tf_op jit(solution)/shard_map/ppermute | solution.py:747
  102.6 17.6 %collective-permute-start.37 = (bf16[4,16,1536]{2,1,0:T(8,128)(2,1)S(1)}, bf16[4,16,1536]{2,1,0:T(8,128)(2,1)S(1)}, u32[]{:S(2)}, u32[]{:S(2)}) collective-permute-start(bf16[4,16,1536]{2,1,0:T(8,128)(2,1)S(1)} %get-tuple-element.234), channel_id=1, source_target_pairs={{0,6},{1,7},{2,4},{3,5},{4,2},{5,3},{6,0},{7,1},{8,14},{9,15},{10,... | collective-permute-start | bytes 589832 | tf_op jit(solution)/shard_map/ppermute | solution.py:744
  103.4 21.0 %collective-permute-start.38 = (bf16[4,16,1536]{2,1,0:T(8,128)(2,1)S(1)}, bf16[4,16,1536]{2,1,0:T(8,128)(2,1)S(1)}, u32[]{:S(2)}, u32[]{:S(2)}) collective-permute-start(bf16[4,16,1536]{2,1,0:T(8,128)(2,1)S(1)} %get-tuple-element.235), channel_id=1, source_target_pairs={{0,2},{1,3},{2,0},{3,1},{4,6},{5,7},{6,4},{7,5},{8,10},{9,11},{10,... | collective-permute-start | bytes 589832 | tf_op jit(solution)/shard_map/ppermute | solution.py:744
  104.8 19.5 %collective-permute-start.39 = (bf16[4,16,1536]{2,1,0:T(8,128)(2,1)S(1)}, bf16[4,16,1536]{2,1,0:T(8,128)(2,1)S(1)}, u32[]{:S(2)}, u32[]{:S(2)}) collective-permute-start(bf16[4,16,1536]{2,1,0:T(8,128)(2,1)S(1)} %get-tuple-element.236), channel_id=1, source_target_pairs={{0,4},{1,5},{2,6},{3,7},{4,0},{5,1},{6,2},{7,3},{8,12},{9,13},{10,... | collective-permute-start | bytes 589832 | tf_op jit(solution)/shard_map/ppermute | solution.py:744
  116.6 8.4 %collective-permute-start.40 = (bf16[16,4736]{1,0:T(8,128)(2,1)S(1)}, bf16[16,4736]{1,0:T(8,128)(2,1)S(1)}, u32[]{:S(2)}, u32[]{:S(2)}) collective-permute-start(bf16[16,4736]{1,0:T(8,128)(2,1)S(1)} %get-tuple-element.239), channel_id=1, source_target_pairs={{0,8},{1,9},{2,10},{3,11},{4,12},{5,13},{6,14},{7,15},{8,0},{9,1},... | collective-permute-start | bytes 454664 | tf_op jit(solution)/shard_map/ppermute | solution.py:744
  116.7 8.3 %collective-permute-start.41 = (bf16[16,4736]{1,0:T(8,128)(2,1)S(1)}, bf16[16,4736]{1,0:T(8,128)(2,1)S(1)}, u32[]{:S(2)}, u32[]{:S(2)}) collective-permute-start(bf16[16,4736]{1,0:T(8,128)(2,1)S(1)} %get-tuple-element.243), channel_id=1, source_target_pairs={{0,8},{1,9},{2,10},{3,11},{4,12},{5,13},{6,14},{7,15},{8,0},{9,1},... | collective-permute-start | bytes 454664 | tf_op jit(solution)/shard_map/ppermute | solution.py:744
  120.2 11.6 %collective-permute-start.36 = (bf16[128,1024]{1,0:T(8,128)(2,1)S(1)}, bf16[128,1024]{1,0:T(8,128)(2,1)S(1)}, u32[]{:S(2)}, u32[]{:S(2)}) collective-permute-start(bf16[128,1024]{1,0:T(8,128)(2,1)S(1)} %get-tuple-element.230), channel_id=1, source_target_pairs={{0,2},{1,3},{2,0},{3,1},{4,6},{5,7},{6,4},{7,5},{8,10},{9,11},{10,... | collective-permute-start | bytes 786440 | tf_op jit(solution)/shard_map/ppermute | solution.py:747
  125.0 8.3 %collective-permute-start.42 = (bf16[16,4736]{1,0:T(8,128)(2,1)S(1)}, bf16[16,4736]{1,0:T(8,128)(2,1)S(1)}, u32[]{:S(2)}, u32[]{:S(2)}) collective-permute-start(bf16[16,4736]{1,0:T(8,128)(2,1)S(1)} %shard_map.268), channel_id=1, source_target_pairs={{0,24},{1,25},{2,26},{3,27},{4,28},{5,29},{6,30},{7,31},{8,16},{9,... | collective-permute-start | bytes 454664 | tf_op jit(solution)/shard_map/ppermute | solution.py:744
  127.4 6.7 %collective-permute-start.43 = (bf16[16,1536]{1,0:T(8,128)(2,1)S(1)}, bf16[16,1536]{1,0:T(8,128)(2,1)S(1)}, u32[]{:S(2)}, u32[]{:S(2)}) collective-permute-start(bf16[16,1536]{1,0:T(8,128)(2,1)S(1)} %get-tuple-element.246), channel_id=1, source_target_pairs={{0,8},{1,9},{2,10},{3,11},{4,12},{5,13},{6,14},{7,15},{8,0},{9,1},... | collective-permute-start | bytes 147464 | tf_op jit(solution)/shard_map/ppermute | solution.py:744
  127.4 8.9 %collective-permute-start.44 = (bf16[16,1536]{1,0:T(8,128)(2,1)S(1)}, bf16[16,1536]{1,0:T(8,128)(2,1)S(1)}, u32[]{:S(2)}, u32[]{:S(2)}) collective-permute-start(bf16[16,1536]{1,0:T(8,128)(2,1)S(1)} %get-tuple-element.247), channel_id=1, source_target_pairs={{0,16},{1,17},{2,18},{3,19},{4,20},{5,21},{6,22},{7,23},{8,24},{9,... | collective-permute-start | bytes 147464 | tf_op jit(solution)/shard_map/ppermute | solution.py:744
  129.5 6.8 %collective-permute-start.45 = (bf16[16,1536]{1,0:T(8,128)(2,1)S(1)}, bf16[16,1536]{1,0:T(8,128)(2,1)S(1)}, u32[]{:S(2)}, u32[]{:S(2)}) collective-permute-start(bf16[16,1536]{1,0:T(8,128)(2,1)S(1)} %get-tuple-element.248), channel_id=1, source_target_pairs={{0,24},{1,25},{2,26},{3,27},{4,28},{5,29},{6,30},{7,31},{8,16},{9,... | collective-permute-start | bytes 147464 | tf_op jit(solution)/shard_map/ppermute | solution.py:744

commit v2 on v1

--- a/solution.py
+++ b/solution.py
@@ -328,10 +328,10 @@
 
 
 def pack_kernel(place_ref, tok_ref, cot_ref, halt_ref, q_ref, k_ref, v_ref, o_ref, win_ref, whid_ref, *rest):
-    vectors, rest = rest[:VECS], rest[VECS:]
+    vectors_ref, rest = rest[0], rest[1:]
     sorted_refs, (block_ref, tall_ref, flip_ref, flags_ref, turn_ref, low_ref, sems) = rest[:2], rest[2:]
     rows, width = q_ref.shape
-    moves = [(vector, low_ref.at[index]) for index, vector in enumerate(vectors)]
+    moves = [(vectors_ref, low_ref)]
     lanes = width // LANES
     for index, source in enumerate((q_ref, k_ref, v_ref, o_ref)):
         for part in range(lanes):
@@ -346,8 +346,7 @@
     turn_ref[...] = jnp.zeros_like(turn_ref)
     for copy in copies:
         copy.wait()
-    for index in range(VECS):
-        turn_ref[index : index + 1, :rows] = low_ref[index].astype(F32)
+    turn_ref[:rows, :] = low_ref[...].astype(F32)
     block_ref[4 * lanes] = turn_ref[...].T[:rows, :].astype(BF16)
 
 
@@ -834,12 +833,12 @@
     if fast:
         send_tok, own_tok, block_a, block_b = run(
             pack_kernel,
-            [*sort_in, *matrices, *(vector[None] for vector in vectors)],
+            [*sort_in, *matrices, jnp.pad(jnp.stack(vectors), ((0, fine - VECS), (0, LANES - fine)))],
             [*sort_out, ((4 * pairs + 1, fine, LANES), BF16), ((8, fine, BLOCK), BF16)],
-            [*sort_tmp, ((LANES, LANES), F32), ((VECS, 1, fine), BF16)],
+            [*sort_tmp, ((LANES, LANES), F32), ((fine, LANES), BF16)],
             scalars=(0,),
-            pinned=range(1, 15),
-            sems=18 + 4 * pairs,
+            pinned=range(1, 11),
+            sems=14 + 4 * pairs,
         )
         got_tok = links.flip_head(send_tok, group)
         line_a = links.along_z(block_a)

time: 137 us -> 138 us (level)
  no operation moved by 1% of the time
where the time goes in v2:
time: 138 us
  waiting for transfers between devices  52.9 us (38%)
  starting transfers between devices  41.4 us (30%)
  Pallas kernels  40.8 us (30%)
  local copies, waits for them, and re-layouts  2.02 us (1%)
    ppermute x40, waiting for transfers between devices, flip(): return lax.ppermute(value, AXES, [(i, i ^ bit) for i in range(self.count)])  48.6 us
    pallas_call x25, Pallas kernels, run(): pl.pallas_call(kernel, out_shape=[jax.ShapeDtypeStruct(s, t) for s, t in...  40.8 us
    ppermute x40, starting transfers between devices, flip(): return lax.ppermute(value, AXES, [(i, i ^ bit) for i in range(self.count)])  36.5 us
    ppermute x6, starting transfers between devices, flip_head(): lax.ppermute(value, 'head', [(i, i ^ bit) for i in range(self.heads)])  4.93 us
    ppermute x6, waiting for transfers between devices, flip_head(): lax.ppermute(value, 'head', [(i, i ^ bit) for i in range(self.heads)])  4.34 us
  transfers between devices with their start and end apart: 46, of which 22 were waited for; matrix products, arithmetic and copies ran while one was open for 0% of the time, Pallas kernels for 14%

profile of v2, /device:TPU:0, one launch (start us, length us, event | category | flops | bytes accessed | tf_op | source)
XLA Modules:
  0.0 138.2 jit_solution(12043838557695210135)
XLA Ops:
  0.7 0.7 stack.39
  1.4 0.6 pad.4.rest_0_
  2.1 2.3 %shard_map.246 = (bf16[128,1152]{1,0:T(8,128)(2,1)S(1)}, bf16[128,1152]{1,0:T(8,128)(2,1)S(1)}, bf16[17,16,128]{2,1,0:T(8,128)(2,1)S(1)}, bf16[8,16,512]{2,1,0:T(8,128)(2,1)S(1)}) custom-call(s32[4]{0:T(128)S(1)} %pad_add_fusion.place_ref.rest_0_.me_ref.info_ref, bf16[2,128,512]{2,1,0:T(8,128)(2,1)} %tok_ref.1, bf16[2,128,512]{2,1,0:T(8,128)(2,1)} %cot_ref.1, ...), custom_call_target="tpu_custom_call" | custom-call | flops 57500000 | bytes 1517584 | tf_op jit(solution)/shard_map/pallas_call | solution.py:713
  4.4 3.0 %collective-permute-start = (bf16[128,1152]{1,0:T(8,128)(2,1)S(1)}, bf16[128,1152]{1,0:T(8,128)(2,1)S(1)}, u32[]{:S(2)}, u32[]{:S(2)}) collective-permute-start(bf16[128,1152]{1,0:T(8,128)(2,1)S(1)} %get-tuple-element.137), channel_id=1, source_target_pairs={{0,2},{1,3},{2,0},{3,1},{4,6},{5,7},{6,4},{7,5},{8,10},{9,11},{10,... | collective-permute-start | bytes 884744 | tf_op jit(solution)/shard_map/ppermute | solution.py:746
  7.4 3.6 %collective-permute-start.4 = (bf16[17,16,128]{2,1,0:T(8,128)(2,1)S(1)}, bf16[17,16,128]{2,1,0:T(8,128)(2,1)S(1)}, u32[]{:S(2)}, u32[]{:S(2)}) collective-permute-start(bf16[17,16,128]{2,1,0:T(8,128)(2,1)S(1)} %get-tuple-element.142.refs_0_), channel_id=1, source_target_pairs={{0,24},{1,25},{2,26},{3,27},{4,28},{5,29},{6,30},{7,31},{8,16},{9,... | collective-permute-start | bytes 208904 | tf_op jit(solution)/shard_map/ppermute | solution.py:743
  11.1 0.8 collective-permute-start.2
  11.8 2.6 %collective-permute-done.4.refs_3_ = bf16[17,16,128]{2,1,0:T(8,128)(2,1)S(1)} collective-permute-done((bf16[17,16,128]{2,1,0:T(8,128)(2,1)S(1)}, bf16[17,16,128]{2,1,0:T(8,128)(2,1)S(1)}, u32[]{:S(2)}, u32[]{:S(2)}) %collective-permute-start.4) | collective-permute-done | bytes 69664 | tf_op jit(solution)/shard_map/ppermute | solution.py:743
  14.4 2.3 %collective-permute-done.3.refs_2_ = bf16[17,16,128]{2,1,0:T(8,128)(2,1)S(1)} collective-permute-done((bf16[17,16,128]{2,1,0:T(8,128)(2,1)S(1)}, bf16[17,16,128]{2,1,0:T(8,128)(2,1)S(1)}, u32[]{:S(2)}, u32[]{:S(2)}) %collective-permute-start.3) | collective-permute-done | bytes 69664 | tf_op jit(solution)/shard_map/ppermute | solution.py:743
  17.2 1.6 %collective-permute-start.6 = (bf16[4,17,16,128]{3,2,1,0:T(8,128)(2,1)S(1)}, bf16[4,17,16,128]{3,2,1,0:T(8,128)(2,1)S(1)}, u32[]{:S(2)}, u32[]{:S(2)}) collective-permute-start(bf16[4,17,16,128]{3,2,1,0:T(8,128)(2,1)S(1)} %shard_map.248.rest_1_), channel_id=1, source_target_pairs={{0,4},{1,5},{2,6},{3,7},{4,0},{5,1},{6,2},{7,3},{8,12},{9,13},{10,... | collective-permute-start | bytes 835592 | tf_op jit(solution)/shard_map/ppermute | solution.py:743
  18.8 0.5 collective-permute-start.5
  19.3 1.5 %collective-permute-start.10 = (bf16[8,16,512]{2,1,0:T(8,128)(2,1)S(1)}, bf16[8,16,512]{2,1,0:T(8,128)(2,1)S(1)}, u32[]{:S(2)}, u32[]{:S(2)}) collective-permute-start(bf16[8,16,512]{2,1,0:T(8,128)(2,1)S(1)} %get-tuple-element.145.refs_0_), channel_id=1, source_target_pairs={{0,16},{1,17},{2,18},{3,19},{4,20},{5,21},{6,22},{7,23},{8,24},{9,... | collective-permute-start | bytes 393224 | tf_op jit(solution)/shard_map/ppermute | solution.py:743
  20.8 0.7 copy-done
  21.5 1.8 %shard_map.247 = (bf16[256,1152]{1,0:T(8,128)(2,1)S(1)}, f32[256,512]{1,0:T(8,128)S(1)}, bf16[256,512]{1,0:T(8,128)(2,1)S(1)}, f32[256,512]{1,0:T(8,128)S(1)}, s...) custom-call(s32[4]{0:T(128)S(1)} %pad_add_fusion.place_ref.rest_0_.me_ref.info_ref, s32[2,8]{1,0:T(2,128)S(1)} %bitcast.35, ...), custom_call_target="tpu_custom_call" | custom-call | flops 57500000 | bytes 2637904 | tf_op jit(solution)/shard_map/pallas_call | solution.py:713
  23.4 1.7 %collective-permute-start.9 = (bf16[8,16,512]{2,1,0:T(8,128)(2,1)S(1)}, bf16[8,16,512]{2,1,0:T(8,128)(2,1)S(1)}, u32[]{:S(2)}, u32[]{:S(2)}) collective-permute-start(bf16[8,16,512]{2,1,0:T(8,128)(2,1)S(1)} %get-tuple-element.145.refs_0_), channel_id=1, source_target_pairs={{0,8},{1,9},{2,10},{3,11},{4,12},{5,13},{6,14},{7,15},{8,0},{9,1},... | collective-permute-start | bytes 393224 | tf_op jit(solution)/shard_map/ppermute | solution.py:743
  25.1 1.9 %collective-permute-done.10.refs_2_ = bf16[8,16,512]{2,1,0:T(8,128)(2,1)S(1)} collective-permute-done((bf16[8,16,512]{2,1,0:T(8,128)(2,1)S(1)}, bf16[8,16,512]{2,1,0:T(8,128)(2,1)S(1)}, u32[]{:S(2)}, u32[]{:S(2)}) %collective-permute-start.10) | collective-permute-done | bytes 131104 | tf_op jit(solution)/shard_map/ppermute | solution.py:743
  27.0 2.1 %collective-permute-start.7 = (bf16[8,16,512]{2,1,0:T(8,128)(2,1)S(1)}, bf16[8,16,512]{2,1,0:T(8,128)(2,1)S(1)}, u32[]{:S(2)}, u32[]{:S(2)}) collective-permute-start(bf16[8,16,512]{2,1,0:T(8,128)(2,1)S(1)} %get-tuple-element.145.refs_0_), channel_id=1, source_target_pairs={{0,24},{1,25},{2,26},{3,27},{4,28},{5,29},{6,30},{7,31},{8,16},{9,... | collective-permute-start | bytes 393224 | tf_op jit(solution)/shard_map/ppermute | solution.py:743
  29.0 0.7 collective-permute-done.9.refs_1_
  29.7 4.0 %collective-permute-done.7.refs_3_ = bf16[8,16,512]{2,1,0:T(8,128)(2,1)S(1)} collective-permute-done((bf16[8,16,512]{2,1,0:T(8,128)(2,1)S(1)}, bf16[8,16,512]{2,1,0:T(8,128)(2,1)S(1)}, u32[]{:S(2)}, u32[]{:S(2)}) %collective-permute-start.7) | collective-permute-done | bytes 131104 | tf_op jit(solution)/shard_map/ppermute | solution.py:743
  33.7 0.7 shard_map.249.rest_1_
  34.4 1.5 %collective-permute-start.12 = (bf16[4,8,16,512]{3,2,1,0:T(8,128)(2,1)S(1)}, bf16[4,8,16,512]{3,2,1,0:T(8,128)(2,1)S(1)}, u32[]{:S(2)}, u32[]{:S(2)}) collective-permute-start(bf16[4,8,16,512]{3,2,1,0:T(8,128)(2,1)S(1)} %shard_map.249.rest_1_), channel_id=1, source_target_pairs={{0,2},{1,3},{2,0},{3,1},{4,6},{5,7},{6,4},{7,5},{8,10},{9,11},{10,... | collective-permute-start | bytes 1572872 | tf_op jit(solution)/shard_map/ppermute | solution.py:743
  36.5 0.5 collective-permute-start.8
  37.0 0.5 collective-permute-start.15
  37.6 11.7 %collective-permute-done.12.by_x_ref.rest_2_ = bf16[4,8,16,512]{3,2,1,0:T(8,128)(2,1)S(1)} collective-permute-done((bf16[4,8,16,512]{3,2,1,0:T(8,128)(2,1)S(1)}, bf16[4,8,16,512]{3,2,1,0:T(8,128)(2,1)S(1)}, u32[]{:S(2)}, u32[]{:S(2)}) %collective-permute-start.12) | collective-permute-done | bytes 524320 | tf_op jit(solution)/shard_map/ppermute | solution.py:743
  49.5 2.7 %collective-permute-done.8.rest_4_ = bf16[4,17,16,128]{3,2,1,0:T(8,128)(2,1)S(1)} collective-permute-done((bf16[4,17,16,128]{3,2,1,0:T(8,128)(2,1)S(1)}, bf16[4,17,16,128]{3,2,1,0:T(8,128)(2,1)S(1)}, u32[]{:S(2)}, u32[]{:S(2)}) %collective-permute-start.8) | collective-permute-done | bytes 278560 | tf_op jit(solution)/shard_map/ppermute | solution.py:743
  52.7 1.5 %collective-permute-start.20 = (bf16[2,8,16,512]{3,2,1,0:T(8,128)(2,1)S(1)}, bf16[2,8,16,512]{3,2,1,0:T(8,128)(2,1)S(1)}, u32[]{:S(2)}, u32[]{:S(2)}) collective-permute-start(bf16[2,8,16,512]{3,2,1,0:T(8,128)(2,1)S(1)} %get-tuple-element.148), channel_id=1, source_target_pairs={{0,2},{1,3},{2,0},{3,1},{4,6},{5,7},{6,4},{7,5},{8,10},{9,11},{10,... | collective-permute-start | bytes 786440 | tf_op jit(solution)/shard_map/ppermute | solution.py:743
  55.2 3.9 %shard_map.251 = (bf16[5,4,8,16,512]{4,3,2,1,0:T(8,128)(2,1)S(1)}, f32[8,512]{1,0:T(8,128)S(1)}, bf16[4,512,128]{2,1,0:T(8,128)(2,1)S(1)}, bf16[512,512]{1,0:T(8...) custom-call(bf16[256,512]{1,0:T(8,128)(2,1)S(1)} %get-tuple-element.139, ...), custom_call_target="tpu_custom_call" | custom-call | flops 9200000000 | bytes 9469968 | tf_op jit(solution)/shard_map/pallas_call | solution.py:713
  59.1 3.0 %collective-permute-done.21.rest_8_ = bf16[2,8,16,512]{3,2,1,0:T(8,128)(2,1)S(1)} collective-permute-done((bf16[2,8,16,512]{3,2,1,0:T(8,128)(2,1)S(1)}, bf16[2,8,16,512]{3,2,1,0:T(8,128)(2,1)S(1)}, u32[]{:S(2)}, u32[]{:S(2)}) %collective-permute-start.21) | collective-permute-done | bytes 262176 | tf_op jit(solution)/shard_map/ppermute | solution.py:743
  62.1 0.5 collective-permute-start.23
  64.0 3.3 %shard_map.253 = (bf16[4,4,8,16,512]{4,3,2,1,0:T(8,128)(2,1)S(1)}, bf16[4,8,4,16,512]{4,3,2,1,0:T(8,128)(2,1)S(1)}, bf16[256,2048]{1,0:T(8,128)(2,1)S(1)}, bf16[...) custom-call(f32[256,512]{1,0:T(8,128)S(1)} %get-tuple-element.153.n1, ...), custom_call_target="tpu_custom_call" | custom-call | flops 6325000192 | bytes 15024144 | tf_op jit(solution)/shard_map/pallas_call | solution.py:713
  67.5 1.4 %collective-permute-done.24 = bf16[1,256,512]{2,1,0:T(8,128)(2,1)S(1)} collective-permute-done((bf16[1,256,512]{2,1,0:T(8,128)(2,1)S(1)}, bf16[1,256,512]{2,1,0:T(8,128)(2,1)S(1)}, u32[]{:S(2)}, u32[]{:S(2)}) %collective-permute-start.24) | collective-permute-done | bytes 262176 | tf_op jit(solution)/shard_map/ppermute | solution.py:746
  68.9 10.4 %shard_map.254 = (f32[256,512]{1,0:T(8,128)S(1)}, f32[256,512]{1,0:T(8,128)S(1)}, bf16[256,512]{1,0:T(8,128)(2,1)S(1)}, bf16[256,512]{1,0:T(8,128)(2,1)S(1)}, bf...) custom-call(f32[256,512]{1,0:T(8,128)S(1)} %get-tuple-element.160.x_, ...), custom_call_target="tpu_custom_call" | custom-call | flops 18055000064 | bytes 15450112 | tf_op jit(solution)/shard_map/pallas_call | solution.py:713
  79.5 1.4 %collective-permute-done.25.more_ref = bf16[256,512]{1,0:T(8,128)(2,1)S(1)} collective-permute-done((bf16[256,512]{1,0:T(8,128)(2,1)S(1)}, bf16[256,512]{1,0:T(8,128)(2,1)S(1)}, u32[]{:S(2)}, u32[]{:S(2)}) %collective-permute-start.25) | collective-permute-done | bytes 262176 | tf_op jit(solution)/shard_map/ppermute | solution.py:746
  80.9 2.5 %shard_map.255 = (bf16[256,512]{1,0:T(8,128)(2,1)S(1)}, f32[256,512]{1,0:T(8,128)S(1)}, f32[256,512]{1,0:T(8,128)S(1)}, f32[5,8,512]{2,1,0:T(8,128)S(1)}, bf16[4...) custom-call(s32[4]{0:T(128)S(1)} %pad_add_fusion.place_ref.rest_0_.me_ref.info_ref, ...), custom_call_target="tpu_custom_call" | custom-call | flops 2300000000 | bytes 8028176 | tf_op jit(solution)/shard_map/pallas_call | solution.py:713
  83.7 1.8 %shard_map.256 = (bf16[256,2048]{1,0:T(8,128)(2,1)S(1)}, bf16[256,512]{1,0:T(8,128)(2,1)S(1)}, f32[256,512]{1,0:T(8,128)S(1)}, bf16[256,512]{1,0:T(8,128)(2,1)S(1)}, f32[5,8,512]{2,1,0:T(8,128)S(1)}) custom-call(bf16[256,512]{1,0:T(8,128)(2,1)S(1)} %get-tuple-element.175.b2_ref, f32[256,512]{1,0:T(8,128)S(1)} %get-tuple-element.176.gsec_ref, ...), custom_call_target="tpu_custom_call" | custom-call | flops 2529999872 | bytes 12107776 | tf_op jit(solution)/shard_map/pallas_call | solution.py:713
  85.5 0.7 collective-permute-done.26.got_ref
  86.4 2.2 %shard_map.258 = (bf16[4,4,16,2688]{3,2,1,0:T(8,128)(2,1)S(1)}, bf16[4,4,16,2688]{3,2,1,0:T(8,128)(2,1)S(1)}) custom-call(s32[4]{0:T(128)S(1)} %pad_add_fusion.place_ref.rest_0_.me_ref.info_ref, bf16[256,2048]{1,0:T(8,128)(2,1)S(1)} %get-tuple-element.189.b1_ref, bf16[256,512]{1,0:T(8,128)(2,1)S(1)} %get-tuple-element.190.b0_ref, ...), custom_call_target="tpu_custom_call" | custom-call | flops 2300000000 | bytes 6520848 | tf_op jit(solution)/shard_map/pallas_call | solution.py:713
  88.9 0.6 collective-permute-start.28
  89.5 0.6 collective-permute-start.29
  90.0 1.8 %collective-permute-done.27.got_ref = bf16[4,4,16,2688]{3,2,1,0:T(8,128)(2,1)S(1)} collective-permute-done((bf16[4,4,16,2688]{3,2,1,0:T(8,128)(2,1)S(1)}, bf16[4,4,16,2688]{3,2,1,0:T(8,128)(2,1)S(1)}, u32[]{:S(2)}, u32[]{:S(2)}) %collective-permute-start.27) | collective-permute-done | bytes 1376288 | tf_op jit(solution)/shard_map/ppermute | solution.py:743
  92.2 0.6 collective-permute-start.30
  92.8 0.6 collective-permute-start.31
  93.4 2.2 %shard_map.260 = (bf16[256,1536]{1,0:T(8,128)(2,1)S(1)}, bf16[256,1024]{1,0:T(8,128)(2,1)S(1)}) custom-call(bf16[256,512]{1,0:T(8,128)(2,1)S(1)} %get-tuple-element.200.gctx_ref, bf16[4,512,128]{2,1,0:T(8,128)(2,1)S(1)} %get-tuple-element.201.q2_ref, bf16[512,512]{1,0:T(8,128)(2,1)S(1)} %get-tuple-element.202.k_ref, ...), custom_call_target="tpu_custom_call" | custom-call | flops 3449999872 | bytes 5505024 | tf_op jit(solution)/shard_map/pallas_call | solution.py:713
  95.6 3.2 %shard_map.261 = (f32[256,512]{1,0:T(8,128)S(1)}, bf16[256,512]{1,0:T(8,128)(2,1)S(1)}, bf16[4,4,16,1536]{3,2,1,0:T(8,128)(2,1)S(1)}, bf16[4,4,16,1536]{3,2,1,0:T(8,128)(2,1)S(1)}) custom-call(s32[4]{0:T(128)S(1)} %pad_add_fusion.place_ref.rest_0_.me_ref.info_ref, f32[256,512]{1,0:T(8,128)S(1)} %get-tuple-element.181.base_ref, ...), custom_call_target="tpu_custom_call" | custom-call | flops 57500000 | bytes 9175056 | tf_op jit(solution)/shard_map/pallas_call | solution.py:713
  99.2 1.4 %collective-permute-start.35 = (bf16[4,16,4736]{2,1,0:T(8,128)(2,1)S(1)}, bf16[4,16,4736]{2,1,0:T(8,128)(2,1)S(1)}, u32[]{:S(2)}, u32[]{:S(2)}) collective-permute-start(bf16[4,16,4736]{2,1,0:T(8,128)(2,1)S(1)} %get-tuple-element.228), channel_id=1, source_target_pairs={{0,4},{1,5},{2,6},{3,7},{4,0},{5,1},{6,2},{7,3},{8,12},{9,13},{10,... | collective-permute-start | bytes 1818632 | tf_op jit(solution)/shard_map/ppermute | solution.py:743
  100.6 1.4 %collective-permute-start.34 = (bf16[4,16,4736]{2,1,0:T(8,128)(2,1)S(1)}, bf16[4,16,4736]{2,1,0:T(8,128)(2,1)S(1)}, u32[]{:S(2)}, u32[]{:S(2)}) collective-permute-start(bf16[4,16,4736]{2,1,0:T(8,128)(2,1)S(1)} %get-tuple-element.216), channel_id=1, source_target_pairs={{0,2},{1,3},{2,0},{3,1},{4,6},{5,7},{6,4},{7,5},{8,10},{9,11},{10,... | collective-permute-start | bytes 1818632 | tf_op jit(solution)/shard_map/ppermute | solution.py:743
  102.1 1.5 %collective-permute-done.32.more_ref = bf16[256,512]{1,0:T(8,128)(2,1)S(1)} collective-permute-done((bf16[256,512]{1,0:T(8,128)(2,1)S(1)}, bf16[256,512]{1,0:T(8,128)(2,1)S(1)}, u32[]{:S(2)}, u32[]{:S(2)}) %collective-permute-start.32) | collective-permute-done | bytes 262176 | tf_op jit(solution)/shard_map/ppermute | solution.py:746
  103.9 0.8 collective-permute-start.37
  104.6 1.4 %collective-permute-start.38 = (bf16[4,16,1536]{2,1,0:T(8,128)(2,1)S(1)}, bf16[4,16,1536]{2,1,0:T(8,128)(2,1)S(1)}, u32[]{:S(2)}, u32[]{:S(2)}) collective-permute-start(bf16[4,16,1536]{2,1,0:T(8,128)(2,1)S(1)} %get-tuple-element.235), channel_id=1, source_target_pairs={{0,2},{1,3},{2,0},{3,1},{4,6},{5,7},{6,4},{7,5},{8,10},{9,11},{10,... | collective-permute-start | bytes 589832 | tf_op jit(solution)/shard_map/ppermute | solution.py:743
  106.1 1.3 collective-permute-start.39
  107.4 8.4 %collective-permute-done.35.got_y_ref = bf16[4,16,4736]{2,1,0:T(8,128)(2,1)S(1)} collective-permute-done((bf16[4,16,4736]{2,1,0:T(8,128)(2,1)S(1)}, bf16[4,16,4736]{2,1,0:T(8,128)(2,1)S(1)}, u32[]{:S(2)}, u32[]{:S(2)}) %collective-permute-start.35) | collective-permute-done | bytes 606240 | tf_op jit(solution)/shard_map/ppermute | solution.py:743
  115.8 1.3 collective-permute-done.34.got_x_ref
  117.1 0.8 shard_map.265
  118.0 2.0 %collective-permute-start.41 = (bf16[16,4736]{1,0:T(8,128)(2,1)S(1)}, bf16[16,4736]{1,0:T(8,128)(2,1)S(1)}, u32[]{:S(2)}, u32[]{:S(2)}) collective-permute-start(bf16[16,4736]{1,0:T(8,128)(2,1)S(1)} %get-tuple-element.243), channel_id=1, source_target_pairs={{0,8},{1,9},{2,10},{3,11},{4,12},{5,13},{6,14},{7,15},{8,0},{9,1},... | collective-permute-start | bytes 454664 | tf_op jit(solution)/shard_map/ppermute | solution.py:743
  120.0 1.5 %collective-permute-done.37.b_ref = bf16[4,16,1536]{2,1,0:T(8,128)(2,1)S(1)} collective-permute-done((bf16[4,16,1536]{2,1,0:T(8,128)(2,1)S(1)}, bf16[4,16,1536]{2,1,0:T(8,128)(2,1)S(1)}, u32[]{:S(2)}, u32[]{:S(2)}) %collective-permute-start.37) | collective-permute-done | bytes 196640 | tf_op jit(solution)/shard_map/ppermute | solution.py:743
  121.5 1.4 %collective-permute-start.36 = (bf16[128,1024]{1,0:T(8,128)(2,1)S(1)}, bf16[128,1024]{1,0:T(8,128)(2,1)S(1)}, u32[]{:S(2)}, u32[]{:S(2)}) collective-permute-start(bf16[128,1024]{1,0:T(8,128)(2,1)S(1)} %get-tuple-element.230), channel_id=1, source_target_pairs={{0,2},{1,3},{2,0},{3,1},{4,6},{5,7},{6,4},{7,5},{8,10},{9,11},{10,... | collective-permute-start | bytes 786440 | tf_op jit(solution)/shard_map/ppermute | solution.py:746
  123.0 2.6 %collective-permute-done.38.c_ref = bf16[4,16,1536]{2,1,0:T(8,128)(2,1)S(1)} collective-permute-done((bf16[4,16,1536]{2,1,0:T(8,128)(2,1)S(1)}, bf16[4,16,1536]{2,1,0:T(8,128)(2,1)S(1)}, u32[]{:S(2)}, u32[]{:S(2)}) %collective-permute-start.38) | collective-permute-done | bytes 196640 | tf_op jit(solution)/shard_map/ppermute | solution.py:743
  125.6 0.7 shard_map.267
  126.3 2.4 %collective-permute-start.42 = (bf16[16,4736]{1,0:T(8,128)(2,1)S(1)}, bf16[16,4736]{1,0:T(8,128)(2,1)S(1)}, u32[]{:S(2)}, u32[]{:S(2)}) collective-permute-start(bf16[16,4736]{1,0:T(8,128)(2,1)S(1)} %shard_map.268), channel_id=1, source_target_pairs={{0,24},{1,25},{2,26},{3,27},{4,28},{5,29},{6,30},{7,31},{8,16},{9,... | collective-permute-start | bytes 454664 | tf_op jit(solution)/shard_map/ppermute | solution.py:743
  128.7 2.1 %collective-permute-start.44 = (bf16[16,1536]{1,0:T(8,128)(2,1)S(1)}, bf16[16,1536]{1,0:T(8,128)(2,1)S(1)}, u32[]{:S(2)}, u32[]{:S(2)}) collective-permute-start(bf16[16,1536]{1,0:T(8,128)(2,1)S(1)} %get-tuple-element.247), channel_id=1, source_target_pairs={{0,16},{1,17},{2,18},{3,19},{4,20},{5,21},{6,22},{7,23},{8,24},{9,... | collective-permute-start | bytes 147464 | tf_op jit(solution)/shard_map/ppermute | solution.py:743
  130.8 2.3 %collective-permute-start.45 = (bf16[16,1536]{1,0:T(8,128)(2,1)S(1)}, bf16[16,1536]{1,0:T(8,128)(2,1)S(1)}, u32[]{:S(2)}, u32[]{:S(2)}) collective-permute-start(bf16[16,1536]{1,0:T(8,128)(2,1)S(1)} %get-tuple-element.248), channel_id=1, source_target_pairs={{0,24},{1,25},{2,26},{3,27},{4,28},{5,29},{6,30},{7,31},{8,16},{9,... | collective-permute-start | bytes 147464 | tf_op jit(solution)/shard_map/ppermute | solution.py:743
  133.1 1.6 %shard_map.266 = (f32[2,128,512]{2,1,0:T(8,128)}, f32[2,128,512]{2,1,0:T(8,128)}) custom-call(s32[4]{0:T(128)S(1)} %pad_add_fusion.place_ref.rest_0_.me_ref.info_ref, f32[256,512]{1,0:T(8,128)S(1)} %get-tuple-element.166.out_ref, f32[256,512]{1,0:T(8,128)S(1)} %get-tuple-element.218.in_ref, bf16[128,1024]{1,0:T(8,128)(2,1)S(1)} %collective-permute-done.36.back_ref), custom_call_target="tpu_custom_call" | custom-call | flops 57500000 | bytes 2359312 | tf_op jit(solution)/shard_map/pallas_call | solution.py:713
  134.7 0.7 shard_map.269
  135.4 2.2 %collective-permute-done.44.c_ref = bf16[16,1536]{1,0:T(8,128)(2,1)S(1)} collective-permute-done((bf16[16,1536]{1,0:T(8,128)(2,1)S(1)}, bf16[16,1536]{1,0:T(8,128)(2,1)S(1)}, u32[]{:S(2)}, u32[]{:S(2)}) %collective-permute-start.44) | collective-permute-done | bytes 49184 | tf_op jit(solution)/shard_map/ppermute | solution.py:743
  137.6 0.6 shard_map.270
  (58 shorter events, 6.4 us)
Async XLA Ops:
  4.4 12.7 %collective-permute-start = (bf16[128,1152]{1,0:T(8,128)(2,1)S(1)}, bf16[128,1152]{1,0:T(8,128)(2,1)S(1)}, u32[]{:S(2)}, u32[]{:S(2)}) collective-permute-start(bf16[128,1152]{1,0:T(8,128)(2,1)S(1)} %get-tuple-element.137), channel_id=1, source_target_pairs={{0,2},{1,3},{2,0},{3,1},{4,6},{5,7},{6,4},{7,5},{8,10},{9,11},{10,... | collective-permute-start | bytes 884744 | tf_op jit(solution)/shard_map/ppermute | solution.py:746
  7.4 7.0 %collective-permute-start.4 = (bf16[17,16,128]{2,1,0:T(8,128)(2,1)S(1)}, bf16[17,16,128]{2,1,0:T(8,128)(2,1)S(1)}, u32[]{:S(2)}, u32[]{:S(2)}) collective-permute-start(bf16[17,16,128]{2,1,0:T(8,128)(2,1)S(1)} %get-tuple-element.142.refs_0_), channel_id=1, source_target_pairs={{0,24},{1,25},{2,26},{3,27},{4,28},{5,29},{6,30},{7,31},{8,16},{9,... | collective-permute-start | bytes 208904 | tf_op jit(solution)/shard_map/ppermute | solution.py:743
  11.0 5.7 %collective-permute-start.3 = (bf16[17,16,128]{2,1,0:T(8,128)(2,1)S(1)}, bf16[17,16,128]{2,1,0:T(8,128)(2,1)S(1)}, u32[]{:S(2)}, u32[]{:S(2)}) collective-permute-start(bf16[17,16,128]{2,1,0:T(8,128)(2,1)S(1)} %get-tuple-element.142.refs_0_), channel_id=1, source_target_pairs={{0,16},{1,17},{2,18},{3,19},{4,20},{5,21},{6,22},{7,23},{8,24},{9,... | collective-permute-start | bytes 208904 | tf_op jit(solution)/shard_map/ppermute | solution.py:743
  11.1 5.7 %collective-permute-start.2 = (bf16[17,16,128]{2,1,0:T(8,128)(2,1)S(1)}, bf16[17,16,128]{2,1,0:T(8,128)(2,1)S(1)}, u32[]{:S(2)}, u32[]{:S(2)}) collective-permute-start(bf16[17,16,128]{2,1,0:T(8,128)(2,1)S(1)} %get-tuple-element.142.refs_0_), channel_id=1, source_target_pairs={{0,8},{1,9},{2,10},{3,11},{4,12},{5,13},{6,14},{7,15},{8,0},{9,1},... | collective-permute-start | bytes 208904 | tf_op jit(solution)/shard_map/ppermute | solution.py:743
  17.2 17.2 %collective-permute-start.6 = (bf16[4,17,16,128]{3,2,1,0:T(8,128)(2,1)S(1)}, bf16[4,17,16,128]{3,2,1,0:T(8,128)(2,1)S(1)}, u32[]{:S(2)}, u32[]{:S(2)}) collective-permute-start(bf16[4,17,16,128]{3,2,1,0:T(8,128)(2,1)S(1)} %shard_map.248.rest_1_), channel_id=1, source_target_pairs={{0,4},{1,5},{2,6},{3,7},{4,0},{5,1},{6,2},{7,3},{8,12},{9,13},{10,... | collective-permute-start | bytes 835592 | tf_op jit(solution)/shard_map/ppermute | solution.py:743
  18.8 15.7 %collective-permute-start.5 = (bf16[4,17,16,128]{3,2,1,0:T(8,128)(2,1)S(1)}, bf16[4,17,16,128]{3,2,1,0:T(8,128)(2,1)S(1)}, u32[]{:S(2)}, u32[]{:S(2)}) collective-permute-start(bf16[4,17,16,128]{3,2,1,0:T(8,128)(2,1)S(1)} %shard_map.248.rest_1_), channel_id=1, source_target_pairs={{0,2},{1,3},{2,0},{3,1},{4,6},{5,7},{6,4},{7,5},{8,10},{9,11},{10,... | collective-permute-start | bytes 835592 | tf_op jit(solution)/shard_map/ppermute | solution.py:743
  19.3 7.7 %collective-permute-start.10 = (bf16[8,16,512]{2,1,0:T(8,128)(2,1)S(1)}, bf16[8,16,512]{2,1,0:T(8,128)(2,1)S(1)}, u32[]{:S(2)}, u32[]{:S(2)}) collective-permute-start(bf16[8,16,512]{2,1,0:T(8,128)(2,1)S(1)} %get-tuple-element.145.refs_0_), channel_id=1, source_target_pairs={{0,16},{1,17},{2,18},{3,19},{4,20},{5,21},{6,22},{7,23},{8,24},{9,... | collective-permute-start | bytes 393224 | tf_op jit(solution)/shard_map/ppermute | solution.py:743
  20.8 0.7 copy-start
  23.3 11.1 %collective-permute-start.1 = (bf16[1,256,512]{2,1,0:T(8,128)(2,1)S(1)}, bf16[1,256,512]{2,1,0:T(8,128)(2,1)S(1)}, u32[]{:S(2)}, u32[]{:S(2)}) collective-permute-start(bf16[1,256,512]{2,1,0:T(8,128)(2,1)S(1)} %bitcast.29), channel_id=1, source_target_pairs={{0,1},{1,0},{2,3},{3,2},{4,5},{5,4},{6,7},{7,6},{8,9},{9,8},{10,11... | collective-permute-start | bytes 786440 | tf_op jit(solution)/shard_map/ppermute | solution.py:746
  23.4 6.3 %collective-permute-start.9 = (bf16[8,16,512]{2,1,0:T(8,128)(2,1)S(1)}, bf16[8,16,512]{2,1,0:T(8,128)(2,1)S(1)}, u32[]{:S(2)}, u32[]{:S(2)}) collective-permute-start(bf16[8,16,512]{2,1,0:T(8,128)(2,1)S(1)} %get-tuple-element.145.refs_0_), channel_id=1, source_target_pairs={{0,8},{1,9},{2,10},{3,11},{4,12},{5,13},{6,14},{7,15},{8,0},{9,1},... | collective-permute-start | bytes 393224 | tf_op jit(solution)/shard_map/ppermute | solution.py:743
  27.0 6.8 %collective-permute-start.7 = (bf16[8,16,512]{2,1,0:T(8,128)(2,1)S(1)}, bf16[8,16,512]{2,1,0:T(8,128)(2,1)S(1)}, u32[]{:S(2)}, u32[]{:S(2)}) collective-permute-start(bf16[8,16,512]{2,1,0:T(8,128)(2,1)S(1)} %get-tuple-element.145.refs_0_), channel_id=1, source_target_pairs={{0,24},{1,25},{2,26},{3,27},{4,28},{5,29},{6,30},{7,31},{8,16},{9,... | collective-permute-start | bytes 393224 | tf_op jit(solution)/shard_map/ppermute | solution.py:743
  34.4 14.8 %collective-permute-start.12 = (bf16[4,8,16,512]{3,2,1,0:T(8,128)(2,1)S(1)}, bf16[4,8,16,512]{3,2,1,0:T(8,128)(2,1)S(1)}, u32[]{:S(2)}, u32[]{:S(2)}) collective-permute-start(bf16[4,8,16,512]{3,2,1,0:T(8,128)(2,1)S(1)} %shard_map.249.rest_1_), channel_id=1, source_target_pairs={{0,2},{1,3},{2,0},{3,1},{4,6},{5,7},{6,4},{7,5},{8,10},{9,11},{10,... | collective-permute-start | bytes 1572872 | tf_op jit(solution)/shard_map/ppermute | solution.py:743
  36.0 13.2 %collective-permute-start.11 = (bf16[4,8,16,512]{3,2,1,0:T(8,128)(2,1)S(1)}, bf16[4,8,16,512]{3,2,1,0:T(8,128)(2,1)S(1)}, u32[]{:S(2)}, u32[]{:S(2)}) collective-permute-start(bf16[4,8,16,512]{3,2,1,0:T(8,128)(2,1)S(1)} %shard_map.249.rest_1_), channel_id=1, source_target_pairs={{0,4},{1,5},{2,6},{3,7},{4,0},{5,1},{6,2},{7,3},{8,12},{9,13},{10,... | collective-permute-start | bytes 1572872 | tf_op jit(solution)/shard_map/ppermute | solution.py:743
  36.5 15.7 %collective-permute-start.8 = (bf16[4,17,16,128]{3,2,1,0:T(8,128)(2,1)S(1)}, bf16[4,17,16,128]{3,2,1,0:T(8,128)(2,1)S(1)}, u32[]{:S(2)}, u32[]{:S(2)}) collective-permute-start(bf16[4,17,16,128]{3,2,1,0:T(8,128)(2,1)S(1)} %collective-permute-done.6.rest_3_), channel_id=1, source_target_pairs={{0,2},{1,3},{2,0},{3,1},{4,6},{5,7},{6,4},{7,5},{8,10},{9,11},{10,... | collective-permute-start | bytes 835592 | tf_op jit(solution)/shard_map/ppermute | solution.py:743
  37.0 15.7 %collective-permute-start.13 = (bf16[4,17,16,128]{3,2,1,0:T(8,128)(2,1)S(1)}, bf16[4,17,16,128]{3,2,1,0:T(8,128)(2,1)S(1)}, u32[]{:S(2)}, u32[]{:S(2)}) collective-permute-start(bf16[4,17,16,128]{3,2,1,0:T(8,128)(2,1)S(1)} %shard_map.248.rest_1_), channel_id=1, source_target_pairs={{0,1},{1,0},{2,3},{3,2},{4,5},{5,4},{6,7},{7,6},{8,9},{9,8},{10,11... | collective-permute-start | bytes 835592 | tf_op jit(solution)/shard_map/ppermute | solution.py:743
  37.0 17.1 %collective-permute-start.15 = (bf16[4,17,16,128]{3,2,1,0:T(8,128)(2,1)S(1)}, bf16[4,17,16,128]{3,2,1,0:T(8,128)(2,1)S(1)}, u32[]{:S(2)}, u32[]{:S(2)}) collective-permute-start(bf16[4,17,16,128]{3,2,1,0:T(8,128)(2,1)S(1)} %collective-permute-done.6.rest_3_), channel_id=1, source_target_pairs={{0,1},{1,0},{2,3},{3,2},{4,5},{5,4},{6,7},{7,6},{8,9},{9,8},{10,11... | collective-permute-start | bytes 835592 | tf_op jit(solution)/shard_map/ppermute | solution.py:743
  49.2 5.5 %collective-permute-start.14 = (bf16[4,17,16,128]{3,2,1,0:T(8,128)(2,1)S(1)}, bf16[4,17,16,128]{3,2,1,0:T(8,128)(2,1)S(1)}, u32[]{:S(2)}, u32[]{:S(2)}) collective-permute-start(bf16[4,17,16,128]{3,2,1,0:T(8,128)(2,1)S(1)} %collective-permute-done.5.rest_2_), channel_id=1, source_target_pairs={{0,1},{1,0},{2,3},{3,2},{4,5},{5,4},{6,7},{7,6},{8,9},{9,8},{10,11... | collective-permute-start | bytes 835592 | tf_op jit(solution)/shard_map/ppermute | solution.py:743
  52.2 2.5 %collective-permute-start.16 = (bf16[4,17,16,128]{3,2,1,0:T(8,128)(2,1)S(1)}, bf16[4,17,16,128]{3,2,1,0:T(8,128)(2,1)S(1)}, u32[]{:S(2)}, u32[]{:S(2)}) collective-permute-start(bf16[4,17,16,128]{3,2,1,0:T(8,128)(2,1)S(1)} %collective-permute-done.8.rest_4_), channel_id=1, source_target_pairs={{0,1},{1,0},{2,3},{3,2},{4,5},{5,4},{6,7},{7,6},{8,9},{9,8},{10,11... | collective-permute-start | bytes 835592 | tf_op jit(solution)/shard_map/ppermute | solution.py:743
  52.2 10.9 %collective-permute-start.17 = (bf16[4,8,16,512]{3,2,1,0:T(8,128)(2,1)S(1)}, bf16[4,8,16,512]{3,2,1,0:T(8,128)(2,1)S(1)}, u32[]{:S(2)}, u32[]{:S(2)}) collective-permute-start(bf16[4,8,16,512]{3,2,1,0:T(8,128)(2,1)S(1)} %shard_map.249.rest_1_), channel_id=1, source_target_pairs={{0,1},{1,0},{2,3},{3,2},{4,5},{5,4},{6,7},{7,6},{8,9},{9,8},{10,11... | collective-permute-start | bytes 1572872 | tf_op jit(solution)/shard_map/ppermute | solution.py:743
  52.7 9.4 %collective-permute-start.20 = (bf16[2,8,16,512]{3,2,1,0:T(8,128)(2,1)S(1)}, bf16[2,8,16,512]{3,2,1,0:T(8,128)(2,1)S(1)}, u32[]{:S(2)}, u32[]{:S(2)}) collective-permute-start(bf16[2,8,16,512]{3,2,1,0:T(8,128)(2,1)S(1)} %get-tuple-element.148), channel_id=1, source_target_pairs={{0,2},{1,3},{2,0},{3,1},{4,6},{5,7},{6,4},{7,5},{8,10},{9,11},{10,... | collective-permute-start | bytes 786440 | tf_op jit(solution)/shard_map/ppermute | solution.py:743
  54.2 7.9 %collective-permute-start.21 = (bf16[2,8,16,512]{3,2,1,0:T(8,128)(2,1)S(1)}, bf16[2,8,16,512]{3,2,1,0:T(8,128)(2,1)S(1)}, u32[]{:S(2)}, u32[]{:S(2)}) collective-permute-start(bf16[2,8,16,512]{3,2,1,0:T(8,128)(2,1)S(1)} %get-tuple-element.158), channel_id=1, source_target_pairs={{0,4},{1,5},{2,6},{3,7},{4,0},{5,1},{6,2},{7,3},{8,12},{9,13},{10,... | collective-permute-start | bytes 786440 | tf_op jit(solution)/shard_map/ppermute | solution.py:743
  54.7 8.4 %collective-permute-start.18 = (bf16[4,8,16,512]{3,2,1,0:T(8,128)(2,1)S(1)}, bf16[4,8,16,512]{3,2,1,0:T(8,128)(2,1)S(1)}, u32[]{:S(2)}, u32[]{:S(2)}) collective-permute-start(bf16[4,8,16,512]{3,2,1,0:T(8,128)(2,1)S(1)} %collective-permute-done.12.by_x_ref.rest_2_), channel_id=1, source_target_pairs={{0,1},{1,0},{2,3},{3,2},{4,5},{5,4},{6,7},{7,6},{8,9},{9,8},{10,11... | collective-permute-start | bytes 1572872 | tf_op jit(solution)/shard_map/ppermute | solution.py:743
  54.7 8.4 %collective-permute-start.19 = (bf16[4,8,16,512]{3,2,1,0:T(8,128)(2,1)S(1)}, bf16[4,8,16,512]{3,2,1,0:T(8,128)(2,1)S(1)}, u32[]{:S(2)}, u32[]{:S(2)}) collective-permute-start(bf16[4,8,16,512]{3,2,1,0:T(8,128)(2,1)S(1)} %collective-permute-done.11.by_y_ref.rest_3_), channel_id=1, source_target_pairs={{0,1},{1,0},{2,3},{3,2},{4,5},{5,4},{6,7},{7,6},{8,9},{9,8},{10,11... | collective-permute-start | bytes 1572872 | tf_op jit(solution)/shard_map/ppermute | solution.py:743
  62.1 1.5 %collective-permute-start.22 = (bf16[2,8,16,512]{3,2,1,0:T(8,128)(2,1)S(1)}, bf16[2,8,16,512]{3,2,1,0:T(8,128)(2,1)S(1)}, u32[]{:S(2)}, u32[]{:S(2)}) collective-permute-start(bf16[2,8,16,512]{3,2,1,0:T(8,128)(2,1)S(1)} %collective-permute-done.20.rest_7_), channel_id=1, source_target_pairs={{0,1},{1,0},{2,3},{3,2},{4,5},{5,4},{6,7},{7,6},{8,9},{9,8},{10,11... | collective-permute-start | bytes 786440 | tf_op jit(solution)/shard_map/ppermute | solution.py:743
  62.1 1.9 %collective-permute-start.23 = (bf16[2,8,16,512]{3,2,1,0:T(8,128)(2,1)S(1)}, bf16[2,8,16,512]{3,2,1,0:T(8,128)(2,1)S(1)}, u32[]{:S(2)}, u32[]{:S(2)}) collective-permute-start(bf16[2,8,16,512]{3,2,1,0:T(8,128)(2,1)S(1)} %collective-permute-done.21.rest_8_), channel_id=1, source_target_pairs={{0,1},{1,0},{2,3},{3,2},{4,5},{5,4},{6,7},{7,6},{8,9},{9,8},{10,11... | collective-permute-start | bytes 786440 | tf_op jit(solution)/shard_map/ppermute | solution.py:743
  67.3 1.6 %collective-permute-start.24 = (bf16[1,256,512]{2,1,0:T(8,128)(2,1)S(1)}, bf16[1,256,512]{2,1,0:T(8,128)(2,1)S(1)}, u32[]{:S(2)}, u32[]{:S(2)}) collective-permute-start(bf16[1,256,512]{2,1,0:T(8,128)(2,1)S(1)} %bitcast.32), channel_id=1, source_target_pairs={{0,1},{1,0},{2,3},{3,2},{4,5},{5,4},{6,7},{7,6},{8,9},{9,8},{10,11... | collective-permute-start | bytes 786440 | tf_op jit(solution)/shard_map/ppermute | solution.py:746
  79.3 1.6 %collective-permute-start.25 = (bf16[256,512]{1,0:T(8,128)(2,1)S(1)}, bf16[256,512]{1,0:T(8,128)(2,1)S(1)}, u32[]{:S(2)}, u32[]{:S(2)}) collective-permute-start(bf16[256,512]{1,0:T(8,128)(2,1)S(1)} %get-tuple-element.168), channel_id=1, source_target_pairs={{0,1},{1,0},{2,3},{3,2},{4,5},{5,4},{6,7},{7,6},{8,9},{9,8},{10,11... | collective-permute-start | bytes 786440 | tf_op jit(solution)/shard_map/ppermute | solution.py:746
  83.5 2.7 %collective-permute-start.26 = (bf16[4,4,64,512]{3,2,1,0:T(8,128)(2,1)S(1)}, bf16[4,4,64,512]{3,2,1,0:T(8,128)(2,1)S(1)}, u32[]{:S(2)}, u32[]{:S(2)}) collective-permute-start(bf16[4,4,64,512]{3,2,1,0:T(8,128)(2,1)S(1)} %get-tuple-element.187), channel_id=1, source_target_pairs={{0,1},{1,0},{2,3},{3,2},{4,5},{5,4},{6,7},{7,6},{8,9},{9,8},{10,11... | collective-permute-start | bytes 3145736 | tf_op jit(solution)/shard_map/ppermute | solution.py:743
  88.7 3.2 %collective-permute-start.27 = (bf16[4,4,16,2688]{3,2,1,0:T(8,128)(2,1)S(1)}, bf16[4,4,16,2688]{3,2,1,0:T(8,128)(2,1)S(1)}, u32[]{:S(2)}, u32[]{:S(2)}) collective-permute-start(bf16[4,4,16,2688]{3,2,1,0:T(8,128)(2,1)S(1)} %get-tuple-element.198), channel_id=1, source_target_pairs={{0,1},{1,0},{2,3},{3,2},{4,5},{5,4},{6,7},{7,6},{8,9},{9,8},{10,11... | collective-permute-start | bytes 4128776 | tf_op jit(solution)/shard_map/ppermute | solution.py:743
  88.9 9.9 %collective-permute-start.28 = (bf16[2,64,512]{2,1,0:T(8,128)(2,1)S(1)}, bf16[2,64,512]{2,1,0:T(8,128)(2,1)S(1)}, u32[]{:S(2)}, u32[]{:S(2)}) collective-permute-start(bf16[2,64,512]{2,1,0:T(8,128)(2,1)S(1)} %get-tuple-element.188), channel_id=1, source_target_pairs={{0,2},{1,3},{2,0},{3,1},{4,6},{5,7},{6,4},{7,5},{8,10},{9,11},{10,... | collective-permute-start | bytes 393224 | tf_op jit(solution)/shard_map/ppermute | solution.py:743
  89.5 9.3 %collective-permute-start.29 = (bf16[2,64,512]{2,1,0:T(8,128)(2,1)S(1)}, bf16[2,64,512]{2,1,0:T(8,128)(2,1)S(1)}, u32[]{:S(2)}, u32[]{:S(2)}) collective-permute-start(bf16[2,64,512]{2,1,0:T(8,128)(2,1)S(1)} %get-tuple-element.212), channel_id=1, source_target_pairs={{0,4},{1,5},{2,6},{3,7},{4,0},{5,1},{6,2},{7,3},{8,12},{9,13},{10,... | collective-permute-start | bytes 393224 | tf_op jit(solution)/shard_map/ppermute | solution.py:743
  92.2 6.8 %collective-permute-start.30 = (bf16[2,16,2688]{2,1,0:T(8,128)(2,1)S(1)}, bf16[2,16,2688]{2,1,0:T(8,128)(2,1)S(1)}, u32[]{:S(2)}, u32[]{:S(2)}) collective-permute-start(bf16[2,16,2688]{2,1,0:T(8,128)(2,1)S(1)} %get-tuple-element.199), channel_id=1, source_target_pairs={{0,2},{1,3},{2,0},{3,1},{4,6},{5,7},{6,4},{7,5},{8,10},{9,11},{10,... | collective-permute-start | bytes 516104 | tf_op jit(solution)/shard_map/ppermute | solution.py:743
  92.8 6.1 %collective-permute-start.31 = (bf16[2,16,2688]{2,1,0:T(8,128)(2,1)S(1)}, bf16[2,16,2688]{2,1,0:T(8,128)(2,1)S(1)}, u32[]{:S(2)}, u32[]{:S(2)}) collective-permute-start(bf16[2,16,2688]{2,1,0:T(8,128)(2,1)S(1)} %get-tuple-element.215), channel_id=1, source_target_pairs={{0,4},{1,5},{2,6},{3,7},{4,0},{5,1},{6,2},{7,3},{8,12},{9,13},{10,... | collective-permute-start | bytes 516104 | tf_op jit(solution)/shard_map/ppermute | solution.py:743
  99.1 4.5 %collective-permute-start.33 = (bf16[4,4,16,1536]{3,2,1,0:T(8,128)(2,1)S(1)}, bf16[4,4,16,1536]{3,2,1,0:T(8,128)(2,1)S(1)}, u32[]{:S(2)}, u32[]{:S(2)}) collective-permute-start(bf16[4,4,16,1536]{3,2,1,0:T(8,128)(2,1)S(1)} %get-tuple-element.224), channel_id=1, source_target_pairs={{0,1},{1,0},{2,3},{3,2},{4,5},{5,4},{6,7},{7,6},{8,9},{9,8},{10,11... | collective-permute-start | bytes 2359304 | tf_op jit(solution)/shard_map/ppermute | solution.py:743
  99.2 16.6 %collective-permute-start.35 = (bf16[4,16,4736]{2,1,0:T(8,128)(2,1)S(1)}, bf16[4,16,4736]{2,1,0:T(8,128)(2,1)S(1)}, u32[]{:S(2)}, u32[]{:S(2)}) collective-permute-start(bf16[4,16,4736]{2,1,0:T(8,128)(2,1)S(1)} %get-tuple-element.228), channel_id=1, source_target_pairs={{0,4},{1,5},{2,6},{3,7},{4,0},{5,1},{6,2},{7,3},{8,12},{9,13},{10,... | collective-permute-start | bytes 1818632 | tf_op jit(solution)/shard_map/ppermute | solution.py:743
  100.6 16.5 %collective-permute-start.34 = (bf16[4,16,4736]{2,1,0:T(8,128)(2,1)S(1)}, bf16[4,16,4736]{2,1,0:T(8,128)(2,1)S(1)}, u32[]{:S(2)}, u32[]{:S(2)}) collective-permute-start(bf16[4,16,4736]{2,1,0:T(8,128)(2,1)S(1)} %get-tuple-element.216), channel_id=1, source_target_pairs={{0,2},{1,3},{2,0},{3,1},{4,6},{5,7},{6,4},{7,5},{8,10},{9,11},{10,... | collective-permute-start | bytes 1818632 | tf_op jit(solution)/shard_map/ppermute | solution.py:743
  102.1 1.5 %collective-permute-start.32 = (bf16[256,512]{1,0:T(8,128)(2,1)S(1)}, bf16[256,512]{1,0:T(8,128)(2,1)S(1)}, u32[]{:S(2)}, u32[]{:S(2)}) collective-permute-start(bf16[256,512]{1,0:T(8,128)(2,1)S(1)} %get-tuple-element.217), channel_id=1, source_target_pairs={{0,1},{1,0},{2,3},{3,2},{4,5},{5,4},{6,7},{7,6},{8,9},{9,8},{10,11... | collective-permute-start | bytes 786440 | tf_op jit(solution)/shard_map/ppermute | solution.py:746
  103.9 17.6 %collective-permute-start.37 = (bf16[4,16,1536]{2,1,0:T(8,128)(2,1)S(1)}, bf16[4,16,1536]{2,1,0:T(8,128)(2,1)S(1)}, u32[]{:S(2)}, u32[]{:S(2)}) collective-permute-start(bf16[4,16,1536]{2,1,0:T(8,128)(2,1)S(1)} %get-tuple-element.234), channel_id=1, source_target_pairs={{0,6},{1,7},{2,4},{3,5},{4,2},{5,3},{6,0},{7,1},{8,14},{9,15},{10,... | collective-permute-start | bytes 589832 | tf_op jit(solution)/shard_map/ppermute | solution.py:743
  104.6 21.0 %collective-permute-start.38 = (bf16[4,16,1536]{2,1,0:T(8,128)(2,1)S(1)}, bf16[4,16,1536]{2,1,0:T(8,128)(2,1)S(1)}, u32[]{:S(2)}, u32[]{:S(2)}) collective-permute-start(bf16[4,16,1536]{2,1,0:T(8,128)(2,1)S(1)} %get-tuple-element.235), channel_id=1, source_target_pairs={{0,2},{1,3},{2,0},{3,1},{4,6},{5,7},{6,4},{7,5},{8,10},{9,11},{10,... | collective-permute-start | bytes 589832 | tf_op jit(solution)/shard_map/ppermute | solution.py:743
  106.1 19.5 %collective-permute-start.39 = (bf16[4,16,1536]{2,1,0:T(8,128)(2,1)S(1)}, bf16[4,16,1536]{2,1,0:T(8,128)(2,1)S(1)}, u32[]{:S(2)}, u32[]{:S(2)}) collective-permute-start(bf16[4,16,1536]{2,1,0:T(8,128)(2,1)S(1)} %get-tuple-element.236), channel_id=1, source_target_pairs={{0,4},{1,5},{2,6},{3,7},{4,0},{5,1},{6,2},{7,3},{8,12},{9,13},{10,... | collective-permute-start | bytes 589832 | tf_op jit(solution)/shard_map/ppermute | solution.py:743
  117.9 8.4 %collective-permute-start.40 = (bf16[16,4736]{1,0:T(8,128)(2,1)S(1)}, bf16[16,4736]{1,0:T(8,128)(2,1)S(1)}, u32[]{:S(2)}, u32[]{:S(2)}) collective-permute-start(bf16[16,4736]{1,0:T(8,128)(2,1)S(1)} %get-tuple-element.239), channel_id=1, source_target_pairs={{0,8},{1,9},{2,10},{3,11},{4,12},{5,13},{6,14},{7,15},{8,0},{9,1},... | collective-permute-start | bytes 454664 | tf_op jit(solution)/shard_map/ppermute | solution.py:743
  118.0 8.3 %collective-permute-start.41 = (bf16[16,4736]{1,0:T(8,128)(2,1)S(1)}, bf16[16,4736]{1,0:T(8,128)(2,1)S(1)}, u32[]{:S(2)}, u32[]{:S(2)}) collective-permute-start(bf16[16,4736]{1,0:T(8,128)(2,1)S(1)} %get-tuple-element.243), channel_id=1, source_target_pairs={{0,8},{1,9},{2,10},{3,11},{4,12},{5,13},{6,14},{7,15},{8,0},{9,1},... | collective-permute-start | bytes 454664 | tf_op jit(solution)/shard_map/ppermute | solution.py:743
  121.5 11.6 %collective-permute-start.36 = (bf16[128,1024]{1,0:T(8,128)(2,1)S(1)}, bf16[128,1024]{1,0:T(8,128)(2,1)S(1)}, u32[]{:S(2)}, u32[]{:S(2)}) collective-permute-start(bf16[128,1024]{1,0:T(8,128)(2,1)S(1)} %get-tuple-element.230), channel_id=1, source_target_pairs={{0,2},{1,3},{2,0},{3,1},{4,6},{5,7},{6,4},{7,5},{8,10},{9,11},{10,... | collective-permute-start | bytes 786440 | tf_op jit(solution)/shard_map/ppermute | solution.py:746
  126.3 8.3 %collective-permute-start.42 = (bf16[16,4736]{1,0:T(8,128)(2,1)S(1)}, bf16[16,4736]{1,0:T(8,128)(2,1)S(1)}, u32[]{:S(2)}, u32[]{:S(2)}) collective-permute-start(bf16[16,4736]{1,0:T(8,128)(2,1)S(1)} %shard_map.268), channel_id=1, source_target_pairs={{0,24},{1,25},{2,26},{3,27},{4,28},{5,29},{6,30},{7,31},{8,16},{9,... | collective-permute-start | bytes 454664 | tf_op jit(solution)/shard_map/ppermute | solution.py:743
  128.7 6.7 %collective-permute-start.43 = (bf16[16,1536]{1,0:T(8,128)(2,1)S(1)}, bf16[16,1536]{1,0:T(8,128)(2,1)S(1)}, u32[]{:S(2)}, u32[]{:S(2)}) collective-permute-start(bf16[16,1536]{1,0:T(8,128)(2,1)S(1)} %get-tuple-element.246), channel_id=1, source_target_pairs={{0,8},{1,9},{2,10},{3,11},{4,12},{5,13},{6,14},{7,15},{8,0},{9,1},... | collective-permute-start | bytes 147464 | tf_op jit(solution)/shard_map/ppermute | solution.py:743
  128.7 8.9 %collective-permute-start.44 = (bf16[16,1536]{1,0:T(8,128)(2,1)S(1)}, bf16[16,1536]{1,0:T(8,128)(2,1)S(1)}, u32[]{:S(2)}, u32[]{:S(2)}) collective-permute-start(bf16[16,1536]{1,0:T(8,128)(2,1)S(1)} %get-tuple-element.247), channel_id=1, source_target_pairs={{0,16},{1,17},{2,18},{3,19},{4,20},{5,21},{6,22},{7,23},{8,24},{9,... | collective-permute-start | bytes 147464 | tf_op jit(solution)/shard_map/ppermute | solution.py:743
  130.8 6.8 %collective-permute-start.45 = (bf16[16,1536]{1,0:T(8,128)(2,1)S(1)}, bf16[16,1536]{1,0:T(8,128)(2,1)S(1)}, u32[]{:S(2)}, u32[]{:S(2)}) collective-permute-start(bf16[16,1536]{1,0:T(8,128)(2,1)S(1)} %get-tuple-element.248), channel_id=1, source_target_pairs={{0,24},{1,25},{2,26},{3,27},{4,28},{5,29},{6,30},{7,31},{8,16},{9,... | collective-permute-start | bytes 147464 | tf_op jit(solution)/shard_map/ppermute | solution.py:743

commit v3 on v1

--- a/solution.py
+++ b/solution.py
@@ -643,8 +643,10 @@
             out_ref[:, cols] = total.astype(BF16)
 
 
-def add_pair_kernel(own_ref, got_ref, sum_ref):
-    sum_ref[...] = (own_ref[...].astype(F32) + got_ref[...].astype(F32)).astype(BF16)
+def add_pair_kernel(own_ref, got_ref, next_ref, sum_ref):
+    cols = own_ref.shape[1]
+    sum_ref[:, :cols] = (own_ref[...].astype(F32) + got_ref[...].astype(F32)).astype(BF16)
+    sum_ref[:, cols:] = next_ref[...]
 
 
 def add_core_all_kernel(keep_ref, got_ref, *outs):
@@ -663,7 +665,7 @@
 
 def end_both_kernel(own_ref, got_ref, far_ref, tall_ref, win_ref, wo_ref, *rest):
     vectors, flip_ref = rest[:-1], rest[-1]
-    rows, width = far_ref.shape[0], tall_ref.shape[1]
+    rows, width = own_ref.shape[0], tall_ref.shape[1]
 
     def total(cols):
         return own_ref[:, cols].astype(F32) + got_ref[:, cols].astype(F32) + far_ref[:, cols].astype(F32)
@@ -681,12 +683,14 @@
         vector[...] = turned[index : index + 1, :rows]
 
 
-def end_kernel(a_ref, b_ref, c_ref, d_ref, *outs):
+def end_kernel(a_ref, b_ref, c_ref, far_ref, *outs):
     at = 0
+    first = far_ref.shape[1] - a_ref.shape[1]
     for out in outs:
         cols = slice(at, at + out.shape[1])
         total = a_ref[:, cols].astype(F32) + b_ref[:, cols].astype(F32)
-        out[...] = total + c_ref[:, cols].astype(F32) + d_ref[:, cols].astype(F32)
+        total = total + c_ref[:, cols].astype(F32)
+        out[...] = total + far_ref[:, first + at : first + at + out.shape[1]].astype(F32)
         at = at + out.shape[1]
 
 
@@ -767,9 +771,10 @@
         own, near, following, far = self.line_parts(kernel, parts, shape)
         return own, far, self.flip(near, 8), self.flip(following, 8)
 
-    def line_last(self, own, far, got, got_far):
-        (far,) = run(add_pair_kernel, [after(far, got), got_far], [(far.shape, BF16)])
-        return own, got, self.flip(far, 24)
+    def line_last(self, far, got, got_far, beside):
+        shape = (far.shape[0], far.shape[1] + beside.shape[1])
+        (far,) = run(add_pair_kernel, [after(far, got), got_far, beside], [(shape, BF16)])
+        return self.flip(far, 24)
 
     def spread(self, own, group):
         held, bit = own[None], 1
@@ -867,12 +872,12 @@
     )
     roth0 = links.spread(rown0, group)
     if fast:
-        own_b = after(links.stack(line_b), by_x, by_y, roth0)
+        own_b = after(links.stack(line_b), by_x, by_y)
         near = [own_b, links.flip(own_b, 2), links.flip(own_b, 4)]
         near = near + [links.flip(piece, 1) for piece in near]
         halves = run(
             halves_kernel,
-            [near[2], near[1]],
+            [after(near[2], roth0), near[1]],
             [((2, 8, fine, BLOCK), BF16)] * 2,
             loose=(0, 1),
             far=(0, 1),
@@ -1017,8 +1022,9 @@
         first_sums = both[0]
         by_plane[0] = after(by_plane[0], both[0])
         attend_sums = links.line_parts(add_four_kernel, by_plane, a00.shape[1:])
-        both = links.line_last(both[0], after(both[1], attend_sums[0]), *both[2:])
-        attend_sums = [attend_sums[0], *(links.flip(attend_sums[k], 8 * k) for k in (1, 2, 3))]
+        far = links.line_last(after(both[1], attend_sums[0]), *both[2:], attend_sums[3])
+        both = [both[0], both[2], far]
+        attend_sums = [attend_sums[0], *(links.flip(attend_sums[k], 8 * k) for k in (1, 2)), far]
         back = after(back, first_sums)
         output, input_grad = run(
             return_kernel,

time: 137 us -> 137 us (level)
  starting transfers between devices: 41.4 us -> 43.3 us
    ppermute x40 -> x39, waiting for transfers between devices: 48.5 us -> 46.6 us  [flip(): return lax.ppermute(value, AXES, [(i, i ^ bit) for i in range(self.count)])]
    ppermute x40 -> x39, starting transfers between devices: 36.5 us -> 38.4 us  [flip(): return lax.ppermute(value, AXES, [(i, i ^ bit) for i in range(self.count)])]
  transfers between devices with their start and end apart: 46 -> 45, of which waited for: 22 -> 23; matrix products, arithmetic and copies ran while one was open for 0% -> 0% of each run, Pallas kernels for 14% -> 14%
where the time goes in v3:
time: 137 us
  waiting for transfers between devices  52 us (38%)
  starting transfers between devices  43.3 us (32%)
  Pallas kernels  40.8 us (30%)
    ppermute x39, waiting for transfers between devices, flip(): return lax.ppermute(value, AXES, [(i, i ^ bit) for i in range(self.count)])  46.6 us
    pallas_call x25, Pallas kernels, run(): pl.pallas_call(kernel, out_shape=[jax.ShapeDtypeStruct(s, t) for s, t in...  40.8 us
    ppermute x39, starting transfers between devices, flip(): return lax.ppermute(value, AXES, [(i, i ^ bit) for i in range(self.count)])  38.4 us
    ppermute x6, waiting for transfers between devices, flip_head(): lax.ppermute(value, 'head', [(i, i ^ bit) for i in range(self.heads)])  5.38 us
    ppermute x6, starting transfers between devices, flip_head(): lax.ppermute(value, 'head', [(i, i ^ bit) for i in range(self.heads)])  4.92 us
  transfers between devices with their start and end apart: 45, of which 23 were waited for; matrix products, arithmetic and copies ran while one was open for 0% of the time, Pallas kernels for 14%

profile of v3, /device:TPU:0, one launch (start us, length us, event | category | flops | bytes accessed | tf_op | source)
XLA Modules:
  0.0 137.2 jit_solution(7245384787654790682)
XLA Ops:
  0.8 2.4 %shard_map.246 = (bf16[128,1152]{1,0:T(8,128)(2,1)S(1)}, bf16[128,1152]{1,0:T(8,128)(2,1)S(1)}, bf16[17,16,128]{2,1,0:T(8,128)(2,1)S(1)}, bf16[8,16,512]{2,1,0:T(8,128)(2,1)S(1)}) custom-call(s32[4]{0:T(128)S(1)} %pad_add_fusion.place_ref.rest_0_.me_ref.info_ref, bf16[2,128,512]{2,1,0:T(8,128)(2,1)} %tok_ref.1, bf16[2,128,512]{2,1,0:T(8,128)(2,1)} %cot_ref.1, ...), custom_call_target="tpu_custom_call" | custom-call | flops 57500000 | bytes 1513648 | tf_op jit(solution)/shard_map/pallas_call | solution.py:718
  3.2 3.0 %collective-permute-start = (bf16[128,1152]{1,0:T(8,128)(2,1)S(1)}, bf16[128,1152]{1,0:T(8,128)(2,1)S(1)}, u32[]{:S(2)}, u32[]{:S(2)}) collective-permute-start(bf16[128,1152]{1,0:T(8,128)(2,1)S(1)} %get-tuple-element.138), channel_id=1, source_target_pairs={{0,2},{1,3},{2,0},{3,1},{4,6},{5,7},{6,4},{7,5},{8,10},{9,11},{10,... | collective-permute-start | bytes 884744 | tf_op jit(solution)/shard_map/ppermute | solution.py:751
  6.2 3.6 %collective-permute-start.4 = (bf16[17,16,128]{2,1,0:T(8,128)(2,1)S(1)}, bf16[17,16,128]{2,1,0:T(8,128)(2,1)S(1)}, u32[]{:S(2)}, u32[]{:S(2)}) collective-permute-start(bf16[17,16,128]{2,1,0:T(8,128)(2,1)S(1)} %get-tuple-element.143.refs_0_), channel_id=1, source_target_pairs={{0,24},{1,25},{2,26},{3,27},{4,28},{5,29},{6,30},{7,31},{8,16},{9,... | collective-permute-start | bytes 208904 | tf_op jit(solution)/shard_map/ppermute | solution.py:748
  9.8 0.8 collective-permute-start.2
  10.6 2.6 %collective-permute-done.4.refs_3_ = bf16[17,16,128]{2,1,0:T(8,128)(2,1)S(1)} collective-permute-done((bf16[17,16,128]{2,1,0:T(8,128)(2,1)S(1)}, bf16[17,16,128]{2,1,0:T(8,128)(2,1)S(1)}, u32[]{:S(2)}, u32[]{:S(2)}) %collective-permute-start.4) | collective-permute-done | bytes 69664 | tf_op jit(solution)/shard_map/ppermute | solution.py:748
  13.1 2.3 %collective-permute-done.3.refs_2_ = bf16[17,16,128]{2,1,0:T(8,128)(2,1)S(1)} collective-permute-done((bf16[17,16,128]{2,1,0:T(8,128)(2,1)S(1)}, bf16[17,16,128]{2,1,0:T(8,128)(2,1)S(1)}, u32[]{:S(2)}, u32[]{:S(2)}) %collective-permute-start.3) | collective-permute-done | bytes 69664 | tf_op jit(solution)/shard_map/ppermute | solution.py:748
  15.9 1.6 %collective-permute-start.6 = (bf16[4,17,16,128]{3,2,1,0:T(8,128)(2,1)S(1)}, bf16[4,17,16,128]{3,2,1,0:T(8,128)(2,1)S(1)}, u32[]{:S(2)}, u32[]{:S(2)}) collective-permute-start(bf16[4,17,16,128]{3,2,1,0:T(8,128)(2,1)S(1)} %shard_map.248.rest_1_), channel_id=1, source_target_pairs={{0,4},{1,5},{2,6},{3,7},{4,0},{5,1},{6,2},{7,3},{8,12},{9,13},{10,... | collective-permute-start | bytes 835592 | tf_op jit(solution)/shard_map/ppermute | solution.py:748
  17.5 0.5 collective-permute-start.5
  18.0 1.5 %collective-permute-start.10 = (bf16[8,16,512]{2,1,0:T(8,128)(2,1)S(1)}, bf16[8,16,512]{2,1,0:T(8,128)(2,1)S(1)}, u32[]{:S(2)}, u32[]{:S(2)}) collective-permute-start(bf16[8,16,512]{2,1,0:T(8,128)(2,1)S(1)} %get-tuple-element.146.refs_0_), channel_id=1, source_target_pairs={{0,16},{1,17},{2,18},{3,19},{4,20},{5,21},{6,22},{7,23},{8,24},{9,... | collective-permute-start | bytes 393224 | tf_op jit(solution)/shard_map/ppermute | solution.py:748
  19.5 1.6 %collective-permute-start.9 = (bf16[8,16,512]{2,1,0:T(8,128)(2,1)S(1)}, bf16[8,16,512]{2,1,0:T(8,128)(2,1)S(1)}, u32[]{:S(2)}, u32[]{:S(2)}) collective-permute-start(bf16[8,16,512]{2,1,0:T(8,128)(2,1)S(1)} %get-tuple-element.146.refs_0_), channel_id=1, source_target_pairs={{0,8},{1,9},{2,10},{3,11},{4,12},{5,13},{6,14},{7,15},{8,0},{9,1},... | collective-permute-start | bytes 393224 | tf_op jit(solution)/shard_map/ppermute | solution.py:748
  21.1 1.3 collective-permute-start.7
  22.4 7.2 %collective-permute-done.10.refs_2_ = bf16[8,16,512]{2,1,0:T(8,128)(2,1)S(1)} collective-permute-done((bf16[8,16,512]{2,1,0:T(8,128)(2,1)S(1)}, bf16[8,16,512]{2,1,0:T(8,128)(2,1)S(1)}, u32[]{:S(2)}, u32[]{:S(2)}) %collective-permute-start.10) | collective-permute-done | bytes 131104 | tf_op jit(solution)/shard_map/ppermute | solution.py:748
  29.6 0.7 shard_map.249.rest_1_
  30.8 1.6 %collective-permute-start.12 = (bf16[4,8,16,512]{3,2,1,0:T(8,128)(2,1)S(1)}, bf16[4,8,16,512]{3,2,1,0:T(8,128)(2,1)S(1)}, u32[]{:S(2)}, u32[]{:S(2)}) collective-permute-start(bf16[4,8,16,512]{3,2,1,0:T(8,128)(2,1)S(1)} %shard_map.249.rest_1_), channel_id=1, source_target_pairs={{0,2},{1,3},{2,0},{3,1},{4,6},{5,7},{6,4},{7,5},{8,10},{9,11},{10,... | collective-permute-start | bytes 1572872 | tf_op jit(solution)/shard_map/ppermute | solution.py:748
  32.9 1.8 %shard_map.247 = (bf16[256,1152]{1,0:T(8,128)(2,1)S(1)}, f32[256,512]{1,0:T(8,128)S(1)}, bf16[256,512]{1,0:T(8,128)(2,1)S(1)}, f32[256,512]{1,0:T(8,128)S(1)}, s...) custom-call(s32[4]{0:T(128)S(1)} %pad_add_fusion.place_ref.rest_0_.me_ref.info_ref, s32[2,8]{1,0:T(2,128)S(1)} %bitcast.35, ...), custom_call_target="tpu_custom_call" | custom-call | flops 57500000 | bytes 2637904 | tf_op jit(solution)/shard_map/pallas_call | solution.py:718
  35.2 1.0 collective-permute-done.1
  36.4 4.3 %collective-permute-done.11.by_y_ref.rest_3_ = bf16[4,8,16,512]{3,2,1,0:T(8,128)(2,1)S(1)} collective-permute-done((bf16[4,8,16,512]{3,2,1,0:T(8,128)(2,1)S(1)}, bf16[4,8,16,512]{3,2,1,0:T(8,128)(2,1)S(1)}, u32[]{:S(2)}, u32[]{:S(2)}) %collective-permute-start.11) | collective-permute-done | bytes 524320 | tf_op jit(solution)/shard_map/ppermute | solution.py:748
  40.7 3.2 %collective-permute-done.12.by_x_ref.rest_2_ = bf16[4,8,16,512]{3,2,1,0:T(8,128)(2,1)S(1)} collective-permute-done((bf16[4,8,16,512]{3,2,1,0:T(8,128)(2,1)S(1)}, bf16[4,8,16,512]{3,2,1,0:T(8,128)(2,1)S(1)}, u32[]{:S(2)}, u32[]{:S(2)}) %collective-permute-start.12) | collective-permute-done | bytes 524320 | tf_op jit(solution)/shard_map/ppermute | solution.py:748
  44.1 2.7 %collective-permute-done.8.rest_4_ = bf16[4,17,16,128]{3,2,1,0:T(8,128)(2,1)S(1)} collective-permute-done((bf16[4,17,16,128]{3,2,1,0:T(8,128)(2,1)S(1)}, bf16[4,17,16,128]{3,2,1,0:T(8,128)(2,1)S(1)}, u32[]{:S(2)}, u32[]{:S(2)}) %collective-permute-start.8) | collective-permute-done | bytes 278560 | tf_op jit(solution)/shard_map/ppermute | solution.py:748
  46.9 0.5 collective-permute-start.17
  47.4 1.5 %collective-permute-start.20 = (bf16[2,8,16,512]{3,2,1,0:T(8,128)(2,1)S(1)}, bf16[2,8,16,512]{3,2,1,0:T(8,128)(2,1)S(1)}, u32[]{:S(2)}, u32[]{:S(2)}) collective-permute-start(bf16[2,8,16,512]{3,2,1,0:T(8,128)(2,1)S(1)} %get-tuple-element.150), channel_id=1, source_target_pairs={{0,2},{1,3},{2,0},{3,1},{4,6},{5,7},{6,4},{7,5},{8,10},{9,11},{10,... | collective-permute-start | bytes 786440 | tf_op jit(solution)/shard_map/ppermute | solution.py:748
  48.9 1.5 %collective-permute-start.21 = (bf16[2,8,16,512]{3,2,1,0:T(8,128)(2,1)S(1)}, bf16[2,8,16,512]{3,2,1,0:T(8,128)(2,1)S(1)}, u32[]{:S(2)}, u32[]{:S(2)}) collective-permute-start(bf16[2,8,16,512]{3,2,1,0:T(8,128)(2,1)S(1)} %get-tuple-element.160), channel_id=1, source_target_pairs={{0,4},{1,5},{2,6},{3,7},{4,0},{5,1},{6,2},{7,3},{8,12},{9,13},{10,... | collective-permute-start | bytes 786440 | tf_op jit(solution)/shard_map/ppermute | solution.py:748
  50.4 0.5 collective-permute-start.19
  50.9 3.9 %shard_map.251 = (bf16[5,4,8,16,512]{4,3,2,1,0:T(8,128)(2,1)S(1)}, f32[8,512]{1,0:T(8,128)S(1)}, bf16[4,512,128]{2,1,0:T(8,128)(2,1)S(1)}, bf16[512,512]{1,0:T(8...) custom-call(bf16[256,512]{1,0:T(8,128)(2,1)S(1)} %get-tuple-element.140, ...), custom_call_target="tpu_custom_call" | custom-call | flops 9200000000 | bytes 9469968 | tf_op jit(solution)/shard_map/pallas_call | solution.py:718
  54.8 2.0 %collective-permute-done.21.rest_8_ = bf16[2,8,16,512]{3,2,1,0:T(8,128)(2,1)S(1)} collective-permute-done((bf16[2,8,16,512]{3,2,1,0:T(8,128)(2,1)S(1)}, bf16[2,8,16,512]{3,2,1,0:T(8,128)(2,1)S(1)}, u32[]{:S(2)}, u32[]{:S(2)}) %collective-permute-start.21) | collective-permute-done | bytes 262176 | tf_op jit(solution)/shard_map/ppermute | solution.py:748
  56.8 0.5 collective-permute-start.23
  58.8 3.3 %shard_map.253 = (bf16[4,4,8,16,512]{4,3,2,1,0:T(8,128)(2,1)S(1)}, bf16[4,8,4,16,512]{4,3,2,1,0:T(8,128)(2,1)S(1)}, bf16[256,2048]{1,0:T(8,128)(2,1)S(1)}, bf16[...) custom-call(f32[256,512]{1,0:T(8,128)S(1)} %get-tuple-element.155.n1, ...), custom_call_target="tpu_custom_call" | custom-call | flops 6325000192 | bytes 15024144 | tf_op jit(solution)/shard_map/pallas_call | solution.py:718
  62.3 1.4 %collective-permute-done.24 = bf16[1,256,512]{2,1,0:T(8,128)(2,1)S(1)} collective-permute-done((bf16[1,256,512]{2,1,0:T(8,128)(2,1)S(1)}, bf16[1,256,512]{2,1,0:T(8,128)(2,1)S(1)}, u32[]{:S(2)}, u32[]{:S(2)}) %collective-permute-start.24) | collective-permute-done | bytes 262176 | tf_op jit(solution)/shard_map/ppermute | solution.py:751
  63.7 10.3 %shard_map.254 = (f32[256,512]{1,0:T(8,128)S(1)}, f32[256,512]{1,0:T(8,128)S(1)}, bf16[256,512]{1,0:T(8,128)(2,1)S(1)}, bf16[256,512]{1,0:T(8,128)(2,1)S(1)}, bf...) custom-call(f32[256,512]{1,0:T(8,128)S(1)} %get-tuple-element.162.x_, ...), custom_call_target="tpu_custom_call" | custom-call | flops 18055000064 | bytes 15450112 | tf_op jit(solution)/shard_map/pallas_call | solution.py:718
  74.2 1.4 %collective-permute-done.25.more_ref = bf16[256,512]{1,0:T(8,128)(2,1)S(1)} collective-permute-done((bf16[256,512]{1,0:T(8,128)(2,1)S(1)}, bf16[256,512]{1,0:T(8,128)(2,1)S(1)}, u32[]{:S(2)}, u32[]{:S(2)}) %collective-permute-start.25) | collective-permute-done | bytes 262176 | tf_op jit(solution)/shard_map/ppermute | solution.py:751
  75.6 2.5 %shard_map.255 = (bf16[256,512]{1,0:T(8,128)(2,1)S(1)}, f32[256,512]{1,0:T(8,128)S(1)}, f32[256,512]{1,0:T(8,128)S(1)}, f32[5,8,512]{2,1,0:T(8,128)S(1)}, bf16[4...) custom-call(s32[4]{0:T(128)S(1)} %pad_add_fusion.place_ref.rest_0_.me_ref.info_ref, ...), custom_call_target="tpu_custom_call" | custom-call | flops 2300000000 | bytes 8028176 | tf_op jit(solution)/shard_map/pallas_call | solution.py:718
  78.3 1.8 %shard_map.256 = (bf16[256,2048]{1,0:T(8,128)(2,1)S(1)}, bf16[256,512]{1,0:T(8,128)(2,1)S(1)}, f32[256,512]{1,0:T(8,128)S(1)}, bf16[256,512]{1,0:T(8,128)(2,1)S(1)}, f32[5,8,512]{2,1,0:T(8,128)S(1)}) custom-call(bf16[256,512]{1,0:T(8,128)(2,1)S(1)} %get-tuple-element.177.b2_ref, f32[256,512]{1,0:T(8,128)S(1)} %get-tuple-element.178.gsec_ref, ...), custom_call_target="tpu_custom_call" | custom-call | flops 2529999872 | bytes 12107776 | tf_op jit(solution)/shard_map/pallas_call | solution.py:718
  80.1 0.7 collective-permute-done.26.got_ref
  81.1 2.2 %shard_map.258 = (bf16[4,4,16,2688]{3,2,1,0:T(8,128)(2,1)S(1)}, bf16[4,4,16,2688]{3,2,1,0:T(8,128)(2,1)S(1)}) custom-call(s32[4]{0:T(128)S(1)} %pad_add_fusion.place_ref.rest_0_.me_ref.info_ref, bf16[256,2048]{1,0:T(8,128)(2,1)S(1)} %get-tuple-element.191.b1_ref, bf16[256,512]{1,0:T(8,128)(2,1)S(1)} %get-tuple-element.192.b0_ref, ...), custom_call_target="tpu_custom_call" | custom-call | flops 2300000000 | bytes 6520848 | tf_op jit(solution)/shard_map/pallas_call | solution.py:718
  83.5 0.5 collective-permute-start.28
  84.1 1.5 %collective-permute-start.29 = (bf16[2,64,512]{2,1,0:T(8,128)(2,1)S(1)}, bf16[2,64,512]{2,1,0:T(8,128)(2,1)S(1)}, u32[]{:S(2)}, u32[]{:S(2)}) collective-permute-start(bf16[2,64,512]{2,1,0:T(8,128)(2,1)S(1)} %get-tuple-element.214), channel_id=1, source_target_pairs={{0,4},{1,5},{2,6},{3,7},{4,0},{5,1},{6,2},{7,3},{8,12},{9,13},{10,... | collective-permute-start | bytes 393224 | tf_op jit(solution)/shard_map/ppermute | solution.py:748
  85.6 0.9 collective-permute-done.27.got_ref
  86.8 0.6 collective-permute-start.30
  87.5 1.5 %collective-permute-start.31 = (bf16[2,16,2688]{2,1,0:T(8,128)(2,1)S(1)}, bf16[2,16,2688]{2,1,0:T(8,128)(2,1)S(1)}, u32[]{:S(2)}, u32[]{:S(2)}) collective-permute-start(bf16[2,16,2688]{2,1,0:T(8,128)(2,1)S(1)} %get-tuple-element.217), channel_id=1, source_target_pairs={{0,4},{1,5},{2,6},{3,7},{4,0},{5,1},{6,2},{7,3},{8,12},{9,13},{10,... | collective-permute-start | bytes 516104 | tf_op jit(solution)/shard_map/ppermute | solution.py:748
  88.9 2.2 %shard_map.260 = (bf16[256,1536]{1,0:T(8,128)(2,1)S(1)}, bf16[256,1024]{1,0:T(8,128)(2,1)S(1)}) custom-call(bf16[256,512]{1,0:T(8,128)(2,1)S(1)} %get-tuple-element.202.gctx_ref, bf16[4,512,128]{2,1,0:T(8,128)(2,1)S(1)} %get-tuple-element.203.q2_ref, bf16[512,512]{1,0:T(8,128)(2,1)S(1)} %get-tuple-element.204.k_ref, ...), custom_call_target="tpu_custom_call" | custom-call | flops 3449999872 | bytes 5505024 | tf_op jit(solution)/shard_map/pallas_call | solution.py:718
  91.2 3.2 %shard_map.261 = (f32[256,512]{1,0:T(8,128)S(1)}, bf16[256,512]{1,0:T(8,128)(2,1)S(1)}, bf16[4,4,16,1536]{3,2,1,0:T(8,128)(2,1)S(1)}, bf16[4,4,16,1536]{3,2,1,0:T(8,128)(2,1)S(1)}) custom-call(s32[4]{0:T(128)S(1)} %pad_add_fusion.place_ref.rest_0_.me_ref.info_ref, f32[256,512]{1,0:T(8,128)S(1)} %get-tuple-element.183.base_ref, ...), custom_call_target="tpu_custom_call" | custom-call | flops 57500000 | bytes 9175056 | tf_op jit(solution)/shard_map/pallas_call | solution.py:718
  94.6 0.8 collective-permute-start.35
  95.4 1.5 %collective-permute-start.34 = (bf16[4,16,4736]{2,1,0:T(8,128)(2,1)S(1)}, bf16[4,16,4736]{2,1,0:T(8,128)(2,1)S(1)}, u32[]{:S(2)}, u32[]{:S(2)}) collective-permute-start(bf16[4,16,4736]{2,1,0:T(8,128)(2,1)S(1)} %get-tuple-element.218), channel_id=1, source_target_pairs={{0,2},{1,3},{2,0},{3,1},{4,6},{5,7},{6,4},{7,5},{8,10},{9,11},{10,... | collective-permute-start | bytes 1818632 | tf_op jit(solution)/shard_map/ppermute | solution.py:748
  96.9 1.5 %collective-permute-done.32.more_ref = bf16[256,512]{1,0:T(8,128)(2,1)S(1)} collective-permute-done((bf16[256,512]{1,0:T(8,128)(2,1)S(1)}, bf16[256,512]{1,0:T(8,128)(2,1)S(1)}, u32[]{:S(2)}, u32[]{:S(2)}) %collective-permute-start.32) | collective-permute-done | bytes 262176 | tf_op jit(solution)/shard_map/ppermute | solution.py:751
  98.7 1.4 collective-permute-start.37
  100.1 1.5 %collective-permute-start.38 = (bf16[4,16,1536]{2,1,0:T(8,128)(2,1)S(1)}, bf16[4,16,1536]{2,1,0:T(8,128)(2,1)S(1)}, u32[]{:S(2)}, u32[]{:S(2)}) collective-permute-start(bf16[4,16,1536]{2,1,0:T(8,128)(2,1)S(1)} %get-tuple-element.237), channel_id=1, source_target_pairs={{0,2},{1,3},{2,0},{3,1},{4,6},{5,7},{6,4},{7,5},{8,10},{9,11},{10,... | collective-permute-start | bytes 589832 | tf_op jit(solution)/shard_map/ppermute | solution.py:748
  101.6 0.7 collective-permute-start.39
  102.3 9.0 %collective-permute-done.35.got_y_ref = bf16[4,16,4736]{2,1,0:T(8,128)(2,1)S(1)} collective-permute-done((bf16[4,16,4736]{2,1,0:T(8,128)(2,1)S(1)}, bf16[4,16,4736]{2,1,0:T(8,128)(2,1)S(1)}, u32[]{:S(2)}, u32[]{:S(2)}) %collective-permute-start.35) | collective-permute-done | bytes 606240 | tf_op jit(solution)/shard_map/ppermute | solution.py:748
  111.2 0.7 collective-permute-done.34.got_x_ref
  111.9 0.8 shard_map.265
  112.7 4.8 %collective-permute-start.40 = (bf16[16,4736]{1,0:T(8,128)(2,1)S(1)}, bf16[16,4736]{1,0:T(8,128)(2,1)S(1)}, u32[]{:S(2)}, u32[]{:S(2)}) collective-permute-start(bf16[16,4736]{1,0:T(8,128)(2,1)S(1)} %get-tuple-element.241), channel_id=1, source_target_pairs={{0,8},{1,9},{2,10},{3,11},{4,12},{5,13},{6,14},{7,15},{8,0},{9,1},... | collective-permute-start | bytes 454664 | tf_op jit(solution)/shard_map/ppermute | solution.py:748
  117.6 1.5 %collective-permute-start.36 = (bf16[128,1024]{1,0:T(8,128)(2,1)S(1)}, bf16[128,1024]{1,0:T(8,128)(2,1)S(1)}, u32[]{:S(2)}, u32[]{:S(2)}) collective-permute-start(bf16[128,1024]{1,0:T(8,128)(2,1)S(1)} %get-tuple-element.232), channel_id=1, source_target_pairs={{0,2},{1,3},{2,0},{3,1},{4,6},{5,7},{6,4},{7,5},{8,10},{9,11},{10,... | collective-permute-start | bytes 786440 | tf_op jit(solution)/shard_map/ppermute | solution.py:751
  119.0 1.4 collective-permute-done.38.c_ref
  120.4 0.7 shard_map.267
  121.0 0.7 collective-permute-done.40.got_ref
  121.8 1.6 %collective-permute-done.41.got_ref = bf16[16,4736]{1,0:T(8,128)(2,1)S(1)} collective-permute-done((bf16[16,4736]{1,0:T(8,128)(2,1)S(1)}, bf16[16,4736]{1,0:T(8,128)(2,1)S(1)}, u32[]{:S(2)}, u32[]{:S(2)}) %collective-permute-start.41) | collective-permute-done | bytes 151584 | tf_op jit(solution)/shard_map/ppermute | solution.py:748
  123.4 1.0 collective-permute-start.42
  124.4 1.6 %collective-permute-start.43 = (bf16[16,1536]{1,0:T(8,128)(2,1)S(1)}, bf16[16,1536]{1,0:T(8,128)(2,1)S(1)}, u32[]{:S(2)}, u32[]{:S(2)}) collective-permute-start(bf16[16,1536]{1,0:T(8,128)(2,1)S(1)} %get-tuple-element.249), channel_id=1, source_target_pairs={{0,8},{1,9},{2,10},{3,11},{4,12},{5,13},{6,14},{7,15},{8,0},{9,1},... | collective-permute-start | bytes 147464 | tf_op jit(solution)/shard_map/ppermute | solution.py:748
  126.0 1.9 %collective-permute-start.44 = (bf16[16,1536]{1,0:T(8,128)(2,1)S(1)}, bf16[16,1536]{1,0:T(8,128)(2,1)S(1)}, u32[]{:S(2)}, u32[]{:S(2)}) collective-permute-start(bf16[16,1536]{1,0:T(8,128)(2,1)S(1)} %get-tuple-element.250), channel_id=1, source_target_pairs={{0,16},{1,17},{2,18},{3,19},{4,20},{5,21},{6,22},{7,23},{8,24},{9,... | collective-permute-start | bytes 147464 | tf_op jit(solution)/shard_map/ppermute | solution.py:748
  127.9 1.6 %shard_map.266 = (f32[2,128,512]{2,1,0:T(8,128)}, f32[2,128,512]{2,1,0:T(8,128)}) custom-call(s32[4]{0:T(128)S(1)} %pad_add_fusion.place_ref.rest_0_.me_ref.info_ref, f32[256,512]{1,0:T(8,128)S(1)} %get-tuple-element.168.out_ref, f32[256,512]{1,0:T(8,128)S(1)} %get-tuple-element.220.in_ref, bf16[128,1024]{1,0:T(8,128)(2,1)S(1)} %collective-permute-done.36.back_ref), custom_call_target="tpu_custom_call" | custom-call | flops 57500000 | bytes 2359312 | tf_op jit(solution)/shard_map/pallas_call | solution.py:718
  129.4 1.8 %collective-permute-done.42.far_ref = bf16[16,6272]{1,0:T(8,128)(2,1)S(1)} collective-permute-done((bf16[16,6272]{1,0:T(8,128)(2,1)S(1)}, bf16[16,6272]{1,0:T(8,128)(2,1)S(1)}, u32[]{:S(2)}, u32[]{:S(2)}) %collective-permute-start.42) | collective-permute-done | bytes 200736 | tf_op jit(solution)/shard_map/ppermute | solution.py:748
  131.2 0.7 shard_map.269
  132.0 4.5 %collective-permute-done.44.c_ref = bf16[16,1536]{1,0:T(8,128)(2,1)S(1)} collective-permute-done((bf16[16,1536]{1,0:T(8,128)(2,1)S(1)}, bf16[16,1536]{1,0:T(8,128)(2,1)S(1)}, u32[]{:S(2)}, u32[]{:S(2)}) %collective-permute-start.44) | collective-permute-done | bytes 49184 | tf_op jit(solution)/shard_map/ppermute | solution.py:748
  136.5 0.6 shard_map.270
  (54 shorter events, 5.8 us)
Async XLA Ops:
  0.6 32.2 %copy-start = (s32[2,1,8]{2,1,0:T(1,128)S(1)}, s32[2,1,8]{2,1,0:T(1,128)}, u32[]{:S(2)}) copy-start(s32[2,1,8]{2,1,0:T(1,128)} %param.17) | copy-start | bytes 196
  3.2 12.7 %collective-permute-start = (bf16[128,1152]{1,0:T(8,128)(2,1)S(1)}, bf16[128,1152]{1,0:T(8,128)(2,1)S(1)}, u32[]{:S(2)}, u32[]{:S(2)}) collective-permute-start(bf16[128,1152]{1,0:T(8,128)(2,1)S(1)} %get-tuple-element.138), channel_id=1, source_target_pairs={{0,2},{1,3},{2,0},{3,1},{4,6},{5,7},{6,4},{7,5},{8,10},{9,11},{10,... | collective-permute-start | bytes 884744 | tf_op jit(solution)/shard_map/ppermute | solution.py:751
  6.2 7.0 %collective-permute-start.4 = (bf16[17,16,128]{2,1,0:T(8,128)(2,1)S(1)}, bf16[17,16,128]{2,1,0:T(8,128)(2,1)S(1)}, u32[]{:S(2)}, u32[]{:S(2)}) collective-permute-start(bf16[17,16,128]{2,1,0:T(8,128)(2,1)S(1)} %get-tuple-element.143.refs_0_), channel_id=1, source_target_pairs={{0,24},{1,25},{2,26},{3,27},{4,28},{5,29},{6,30},{7,31},{8,16},{9,... | collective-permute-start | bytes 208904 | tf_op jit(solution)/shard_map/ppermute | solution.py:748
  9.8 5.7 %collective-permute-start.3 = (bf16[17,16,128]{2,1,0:T(8,128)(2,1)S(1)}, bf16[17,16,128]{2,1,0:T(8,128)(2,1)S(1)}, u32[]{:S(2)}, u32[]{:S(2)}) collective-permute-start(bf16[17,16,128]{2,1,0:T(8,128)(2,1)S(1)} %get-tuple-element.143.refs_0_), channel_id=1, source_target_pairs={{0,16},{1,17},{2,18},{3,19},{4,20},{5,21},{6,22},{7,23},{8,24},{9,... | collective-permute-start | bytes 208904 | tf_op jit(solution)/shard_map/ppermute | solution.py:748
  9.8 5.7 %collective-permute-start.2 = (bf16[17,16,128]{2,1,0:T(8,128)(2,1)S(1)}, bf16[17,16,128]{2,1,0:T(8,128)(2,1)S(1)}, u32[]{:S(2)}, u32[]{:S(2)}) collective-permute-start(bf16[17,16,128]{2,1,0:T(8,128)(2,1)S(1)} %get-tuple-element.143.refs_0_), channel_id=1, source_target_pairs={{0,8},{1,9},{2,10},{3,11},{4,12},{5,13},{6,14},{7,15},{8,0},{9,1},... | collective-permute-start | bytes 208904 | tf_op jit(solution)/shard_map/ppermute | solution.py:748
  15.9 14.4 %collective-permute-start.6 = (bf16[4,17,16,128]{3,2,1,0:T(8,128)(2,1)S(1)}, bf16[4,17,16,128]{3,2,1,0:T(8,128)(2,1)S(1)}, u32[]{:S(2)}, u32[]{:S(2)}) collective-permute-start(bf16[4,17,16,128]{3,2,1,0:T(8,128)(2,1)S(1)} %shard_map.248.rest_1_), channel_id=1, source_target_pairs={{0,4},{1,5},{2,6},{3,7},{4,0},{5,1},{6,2},{7,3},{8,12},{9,13},{10,... | collective-permute-start | bytes 835592 | tf_op jit(solution)/shard_map/ppermute | solution.py:748
  17.5 12.8 %collective-permute-start.5 = (bf16[4,17,16,128]{3,2,1,0:T(8,128)(2,1)S(1)}, bf16[4,17,16,128]{3,2,1,0:T(8,128)(2,1)S(1)}, u32[]{:S(2)}, u32[]{:S(2)}) collective-permute-start(bf16[4,17,16,128]{3,2,1,0:T(8,128)(2,1)S(1)} %shard_map.248.rest_1_), channel_id=1, source_target_pairs={{0,2},{1,3},{2,0},{3,1},{4,6},{5,7},{6,4},{7,5},{8,10},{9,11},{10,... | collective-permute-start | bytes 835592 | tf_op jit(solution)/shard_map/ppermute | solution.py:748
  18.0 11.5 %collective-permute-start.10 = (bf16[8,16,512]{2,1,0:T(8,128)(2,1)S(1)}, bf16[8,16,512]{2,1,0:T(8,128)(2,1)S(1)}, u32[]{:S(2)}, u32[]{:S(2)}) collective-permute-start(bf16[8,16,512]{2,1,0:T(8,128)(2,1)S(1)} %get-tuple-element.146.refs_0_), channel_id=1, source_target_pairs={{0,16},{1,17},{2,18},{3,19},{4,20},{5,21},{6,22},{7,23},{8,24},{9,... | collective-permute-start | bytes 393224 | tf_op jit(solution)/shard_map/ppermute | solution.py:748
  19.5 10.1 %collective-permute-start.9 = (bf16[8,16,512]{2,1,0:T(8,128)(2,1)S(1)}, bf16[8,16,512]{2,1,0:T(8,128)(2,1)S(1)}, u32[]{:S(2)}, u32[]{:S(2)}) collective-permute-start(bf16[8,16,512]{2,1,0:T(8,128)(2,1)S(1)} %get-tuple-element.146.refs_0_), channel_id=1, source_target_pairs={{0,8},{1,9},{2,10},{3,11},{4,12},{5,13},{6,14},{7,15},{8,0},{9,1},... | collective-permute-start | bytes 393224 | tf_op jit(solution)/shard_map/ppermute | solution.py:748
  21.1 8.4 %collective-permute-start.7 = (bf16[8,16,512]{2,1,0:T(8,128)(2,1)S(1)}, bf16[8,16,512]{2,1,0:T(8,128)(2,1)S(1)}, u32[]{:S(2)}, u32[]{:S(2)}) collective-permute-start(bf16[8,16,512]{2,1,0:T(8,128)(2,1)S(1)} %get-tuple-element.146.refs_0_), channel_id=1, source_target_pairs={{0,24},{1,25},{2,26},{3,27},{4,28},{5,29},{6,30},{7,31},{8,16},{9,... | collective-permute-start | bytes 393224 | tf_op jit(solution)/shard_map/ppermute | solution.py:748
  30.3 10.4 %collective-permute-start.11 = (bf16[4,8,16,512]{3,2,1,0:T(8,128)(2,1)S(1)}, bf16[4,8,16,512]{3,2,1,0:T(8,128)(2,1)S(1)}, u32[]{:S(2)}, u32[]{:S(2)}) collective-permute-start(bf16[4,8,16,512]{3,2,1,0:T(8,128)(2,1)S(1)} %shard_map.249.rest_1_), channel_id=1, source_target_pairs={{0,4},{1,5},{2,6},{3,7},{4,0},{5,1},{6,2},{7,3},{8,12},{9,13},{10,... | collective-permute-start | bytes 1572872 | tf_op jit(solution)/shard_map/ppermute | solution.py:748
  30.8 13.1 %collective-permute-start.12 = (bf16[4,8,16,512]{3,2,1,0:T(8,128)(2,1)S(1)}, bf16[4,8,16,512]{3,2,1,0:T(8,128)(2,1)S(1)}, u32[]{:S(2)}, u32[]{:S(2)}) collective-permute-start(bf16[4,8,16,512]{3,2,1,0:T(8,128)(2,1)S(1)} %shard_map.249.rest_1_), channel_id=1, source_target_pairs={{0,2},{1,3},{2,0},{3,1},{4,6},{5,7},{6,4},{7,5},{8,10},{9,11},{10,... | collective-permute-start | bytes 1572872 | tf_op jit(solution)/shard_map/ppermute | solution.py:748
  32.4 14.5 %collective-permute-start.8 = (bf16[4,17,16,128]{3,2,1,0:T(8,128)(2,1)S(1)}, bf16[4,17,16,128]{3,2,1,0:T(8,128)(2,1)S(1)}, u32[]{:S(2)}, u32[]{:S(2)}) collective-permute-start(bf16[4,17,16,128]{3,2,1,0:T(8,128)(2,1)S(1)} %collective-permute-done.6.rest_3_), channel_id=1, source_target_pairs={{0,2},{1,3},{2,0},{3,1},{4,6},{5,7},{6,4},{7,5},{8,10},{9,11},{10,... | collective-permute-start | bytes 835592 | tf_op jit(solution)/shard_map/ppermute | solution.py:748
  34.7 1.6 %collective-permute-start.1 = (bf16[1,256,512]{2,1,0:T(8,128)(2,1)S(1)}, bf16[1,256,512]{2,1,0:T(8,128)(2,1)S(1)}, u32[]{:S(2)}, u32[]{:S(2)}) collective-permute-start(bf16[1,256,512]{2,1,0:T(8,128)(2,1)S(1)} %bitcast.29), channel_id=1, source_target_pairs={{0,1},{1,0},{2,3},{3,2},{4,5},{5,4},{6,7},{7,6},{8,9},{9,8},{10,11... | collective-permute-start | bytes 786440 | tf_op jit(solution)/shard_map/ppermute | solution.py:751
  34.7 12.7 %collective-permute-start.13 = (bf16[4,17,16,128]{3,2,1,0:T(8,128)(2,1)S(1)}, bf16[4,17,16,128]{3,2,1,0:T(8,128)(2,1)S(1)}, u32[]{:S(2)}, u32[]{:S(2)}) collective-permute-start(bf16[4,17,16,128]{3,2,1,0:T(8,128)(2,1)S(1)} %shard_map.248.rest_1_), channel_id=1, source_target_pairs={{0,1},{1,0},{2,3},{3,2},{4,5},{5,4},{6,7},{7,6},{8,9},{9,8},{10,11... | collective-permute-start | bytes 835592 | tf_op jit(solution)/shard_map/ppermute | solution.py:748
  36.3 12.6 %collective-permute-start.15 = (bf16[4,17,16,128]{3,2,1,0:T(8,128)(2,1)S(1)}, bf16[4,17,16,128]{3,2,1,0:T(8,128)(2,1)S(1)}, u32[]{:S(2)}, u32[]{:S(2)}) collective-permute-start(bf16[4,17,16,128]{3,2,1,0:T(8,128)(2,1)S(1)} %collective-permute-done.6.rest_3_), channel_id=1, source_target_pairs={{0,1},{1,0},{2,3},{3,2},{4,5},{5,4},{6,7},{7,6},{8,9},{9,8},{10,11... | collective-permute-start | bytes 835592 | tf_op jit(solution)/shard_map/ppermute | solution.py:748
  40.7 9.7 %collective-permute-start.14 = (bf16[4,17,16,128]{3,2,1,0:T(8,128)(2,1)S(1)}, bf16[4,17,16,128]{3,2,1,0:T(8,128)(2,1)S(1)}, u32[]{:S(2)}, u32[]{:S(2)}) collective-permute-start(bf16[4,17,16,128]{3,2,1,0:T(8,128)(2,1)S(1)} %collective-permute-done.5.rest_2_), channel_id=1, source_target_pairs={{0,1},{1,0},{2,3},{3,2},{4,5},{5,4},{6,7},{7,6},{8,9},{9,8},{10,11... | collective-permute-start | bytes 835592 | tf_op jit(solution)/shard_map/ppermute | solution.py:748
  46.9 3.5 %collective-permute-start.16 = (bf16[4,17,16,128]{3,2,1,0:T(8,128)(2,1)S(1)}, bf16[4,17,16,128]{3,2,1,0:T(8,128)(2,1)S(1)}, u32[]{:S(2)}, u32[]{:S(2)}) collective-permute-start(bf16[4,17,16,128]{3,2,1,0:T(8,128)(2,1)S(1)} %collective-permute-done.8.rest_4_), channel_id=1, source_target_pairs={{0,1},{1,0},{2,3},{3,2},{4,5},{5,4},{6,7},{7,6},{8,9},{9,8},{10,11... | collective-permute-start | bytes 835592 | tf_op jit(solution)/shard_map/ppermute | solution.py:748
  46.9 11.0 %collective-permute-start.17 = (bf16[4,8,16,512]{3,2,1,0:T(8,128)(2,1)S(1)}, bf16[4,8,16,512]{3,2,1,0:T(8,128)(2,1)S(1)}, u32[]{:S(2)}, u32[]{:S(2)}) collective-permute-start(bf16[4,8,16,512]{3,2,1,0:T(8,128)(2,1)S(1)} %shard_map.249.rest_1_), channel_id=1, source_target_pairs={{0,1},{1,0},{2,3},{3,2},{4,5},{5,4},{6,7},{7,6},{8,9},{9,8},{10,11... | collective-permute-start | bytes 1572872 | tf_op jit(solution)/shard_map/ppermute | solution.py:748
  47.4 9.4 %collective-permute-start.20 = (bf16[2,8,16,512]{3,2,1,0:T(8,128)(2,1)S(1)}, bf16[2,8,16,512]{3,2,1,0:T(8,128)(2,1)S(1)}, u32[]{:S(2)}, u32[]{:S(2)}) collective-permute-start(bf16[2,8,16,512]{3,2,1,0:T(8,128)(2,1)S(1)} %get-tuple-element.150), channel_id=1, source_target_pairs={{0,2},{1,3},{2,0},{3,1},{4,6},{5,7},{6,4},{7,5},{8,10},{9,11},{10,... | collective-permute-start | bytes 786440 | tf_op jit(solution)/shard_map/ppermute | solution.py:748
  48.9 7.9 %collective-permute-start.21 = (bf16[2,8,16,512]{3,2,1,0:T(8,128)(2,1)S(1)}, bf16[2,8,16,512]{3,2,1,0:T(8,128)(2,1)S(1)}, u32[]{:S(2)}, u32[]{:S(2)}) collective-permute-start(bf16[2,8,16,512]{3,2,1,0:T(8,128)(2,1)S(1)} %get-tuple-element.160), channel_id=1, source_target_pairs={{0,4},{1,5},{2,6},{3,7},{4,0},{5,1},{6,2},{7,3},{8,12},{9,13},{10,... | collective-permute-start | bytes 786440 | tf_op jit(solution)/shard_map/ppermute | solution.py:748
  50.4 7.4 %collective-permute-start.18 = (bf16[4,8,16,512]{3,2,1,0:T(8,128)(2,1)S(1)}, bf16[4,8,16,512]{3,2,1,0:T(8,128)(2,1)S(1)}, u32[]{:S(2)}, u32[]{:S(2)}) collective-permute-start(bf16[4,8,16,512]{3,2,1,0:T(8,128)(2,1)S(1)} %collective-permute-done.12.by_x_ref.rest_2_), channel_id=1, source_target_pairs={{0,1},{1,0},{2,3},{3,2},{4,5},{5,4},{6,7},{7,6},{8,9},{9,8},{10,11... | collective-permute-start | bytes 1572872 | tf_op jit(solution)/shard_map/ppermute | solution.py:748
  50.4 7.4 %collective-permute-start.19 = (bf16[4,8,16,512]{3,2,1,0:T(8,128)(2,1)S(1)}, bf16[4,8,16,512]{3,2,1,0:T(8,128)(2,1)S(1)}, u32[]{:S(2)}, u32[]{:S(2)}) collective-permute-start(bf16[4,8,16,512]{3,2,1,0:T(8,128)(2,1)S(1)} %collective-permute-done.11.by_y_ref.rest_3_), channel_id=1, source_target_pairs={{0,1},{1,0},{2,3},{3,2},{4,5},{5,4},{6,7},{7,6},{8,9},{9,8},{10,11... | collective-permute-start | bytes 1572872 | tf_op jit(solution)/shard_map/ppermute | solution.py:748
  56.8 1.5 %collective-permute-start.22 = (bf16[2,8,16,512]{3,2,1,0:T(8,128)(2,1)S(1)}, bf16[2,8,16,512]{3,2,1,0:T(8,128)(2,1)S(1)}, u32[]{:S(2)}, u32[]{:S(2)}) collective-permute-start(bf16[2,8,16,512]{3,2,1,0:T(8,128)(2,1)S(1)} %collective-permute-done.20.rest_7_), channel_id=1, source_target_pairs={{0,1},{1,0},{2,3},{3,2},{4,5},{5,4},{6,7},{7,6},{8,9},{9,8},{10,11... | collective-permute-start | bytes 786440 | tf_op jit(solution)/shard_map/ppermute | solution.py:748
  56.8 1.9 %collective-permute-start.23 = (bf16[2,8,16,512]{3,2,1,0:T(8,128)(2,1)S(1)}, bf16[2,8,16,512]{3,2,1,0:T(8,128)(2,1)S(1)}, u32[]{:S(2)}, u32[]{:S(2)}) collective-permute-start(bf16[2,8,16,512]{3,2,1,0:T(8,128)(2,1)S(1)} %collective-permute-done.21.rest_8_), channel_id=1, source_target_pairs={{0,1},{1,0},{2,3},{3,2},{4,5},{5,4},{6,7},{7,6},{8,9},{9,8},{10,11... | collective-permute-start | bytes 786440 | tf_op jit(solution)/shard_map/ppermute | solution.py:748
  62.1 1.6 %collective-permute-start.24 = (bf16[1,256,512]{2,1,0:T(8,128)(2,1)S(1)}, bf16[1,256,512]{2,1,0:T(8,128)(2,1)S(1)}, u32[]{:S(2)}, u32[]{:S(2)}) collective-permute-start(bf16[1,256,512]{2,1,0:T(8,128)(2,1)S(1)} %bitcast.32), channel_id=1, source_target_pairs={{0,1},{1,0},{2,3},{3,2},{4,5},{5,4},{6,7},{7,6},{8,9},{9,8},{10,11... | collective-permute-start | bytes 786440 | tf_op jit(solution)/shard_map/ppermute | solution.py:751
  74.0 1.6 %collective-permute-start.25 = (bf16[256,512]{1,0:T(8,128)(2,1)S(1)}, bf16[256,512]{1,0:T(8,128)(2,1)S(1)}, u32[]{:S(2)}, u32[]{:S(2)}) collective-permute-start(bf16[256,512]{1,0:T(8,128)(2,1)S(1)} %get-tuple-element.170), channel_id=1, source_target_pairs={{0,1},{1,0},{2,3},{3,2},{4,5},{5,4},{6,7},{7,6},{8,9},{9,8},{10,11... | collective-permute-start | bytes 786440 | tf_op jit(solution)/shard_map/ppermute | solution.py:751
  78.1 2.7 %collective-permute-start.26 = (bf16[4,4,64,512]{3,2,1,0:T(8,128)(2,1)S(1)}, bf16[4,4,64,512]{3,2,1,0:T(8,128)(2,1)S(1)}, u32[]{:S(2)}, u32[]{:S(2)}) collective-permute-start(bf16[4,4,64,512]{3,2,1,0:T(8,128)(2,1)S(1)} %get-tuple-element.189), channel_id=1, source_target_pairs={{0,1},{1,0},{2,3},{3,2},{4,5},{5,4},{6,7},{7,6},{8,9},{9,8},{10,11... | collective-permute-start | bytes 3145736 | tf_op jit(solution)/shard_map/ppermute | solution.py:748
  83.3 3.2 %collective-permute-start.27 = (bf16[4,4,16,2688]{3,2,1,0:T(8,128)(2,1)S(1)}, bf16[4,4,16,2688]{3,2,1,0:T(8,128)(2,1)S(1)}, u32[]{:S(2)}, u32[]{:S(2)}) collective-permute-start(bf16[4,4,16,2688]{3,2,1,0:T(8,128)(2,1)S(1)} %get-tuple-element.200), channel_id=1, source_target_pairs={{0,1},{1,0},{2,3},{3,2},{4,5},{5,4},{6,7},{7,6},{8,9},{9,8},{10,11... | collective-permute-start | bytes 4128776 | tf_op jit(solution)/shard_map/ppermute | solution.py:748
  83.5 10.8 %collective-permute-start.28 = (bf16[2,64,512]{2,1,0:T(8,128)(2,1)S(1)}, bf16[2,64,512]{2,1,0:T(8,128)(2,1)S(1)}, u32[]{:S(2)}, u32[]{:S(2)}) collective-permute-start(bf16[2,64,512]{2,1,0:T(8,128)(2,1)S(1)} %get-tuple-element.190), channel_id=1, source_target_pairs={{0,2},{1,3},{2,0},{3,1},{4,6},{5,7},{6,4},{7,5},{8,10},{9,11},{10,... | collective-permute-start | bytes 393224 | tf_op jit(solution)/shard_map/ppermute | solution.py:748
  84.1 10.3 %collective-permute-start.29 = (bf16[2,64,512]{2,1,0:T(8,128)(2,1)S(1)}, bf16[2,64,512]{2,1,0:T(8,128)(2,1)S(1)}, u32[]{:S(2)}, u32[]{:S(2)}) collective-permute-start(bf16[2,64,512]{2,1,0:T(8,128)(2,1)S(1)} %get-tuple-element.214), channel_id=1, source_target_pairs={{0,4},{1,5},{2,6},{3,7},{4,0},{5,1},{6,2},{7,3},{8,12},{9,13},{10,... | collective-permute-start | bytes 393224 | tf_op jit(solution)/shard_map/ppermute | solution.py:748
  86.8 7.6 %collective-permute-start.30 = (bf16[2,16,2688]{2,1,0:T(8,128)(2,1)S(1)}, bf16[2,16,2688]{2,1,0:T(8,128)(2,1)S(1)}, u32[]{:S(2)}, u32[]{:S(2)}) collective-permute-start(bf16[2,16,2688]{2,1,0:T(8,128)(2,1)S(1)} %get-tuple-element.201), channel_id=1, source_target_pairs={{0,2},{1,3},{2,0},{3,1},{4,6},{5,7},{6,4},{7,5},{8,10},{9,11},{10,... | collective-permute-start | bytes 516104 | tf_op jit(solution)/shard_map/ppermute | solution.py:748
  87.5 6.9 %collective-permute-start.31 = (bf16[2,16,2688]{2,1,0:T(8,128)(2,1)S(1)}, bf16[2,16,2688]{2,1,0:T(8,128)(2,1)S(1)}, u32[]{:S(2)}, u32[]{:S(2)}) collective-permute-start(bf16[2,16,2688]{2,1,0:T(8,128)(2,1)S(1)} %get-tuple-element.217), channel_id=1, source_target_pairs={{0,4},{1,5},{2,6},{3,7},{4,0},{5,1},{6,2},{7,3},{8,12},{9,13},{10,... | collective-permute-start | bytes 516104 | tf_op jit(solution)/shard_map/ppermute | solution.py:748
  94.5 4.0 %collective-permute-start.33 = (bf16[4,4,16,1536]{3,2,1,0:T(8,128)(2,1)S(1)}, bf16[4,4,16,1536]{3,2,1,0:T(8,128)(2,1)S(1)}, u32[]{:S(2)}, u32[]{:S(2)}) collective-permute-start(bf16[4,4,16,1536]{3,2,1,0:T(8,128)(2,1)S(1)} %get-tuple-element.226), channel_id=1, source_target_pairs={{0,1},{1,0},{2,3},{3,2},{4,5},{5,4},{6,7},{7,6},{8,9},{9,8},{10,11... | collective-permute-start | bytes 2359304 | tf_op jit(solution)/shard_map/ppermute | solution.py:748
  94.6 16.6 %collective-permute-start.35 = (bf16[4,16,4736]{2,1,0:T(8,128)(2,1)S(1)}, bf16[4,16,4736]{2,1,0:T(8,128)(2,1)S(1)}, u32[]{:S(2)}, u32[]{:S(2)}) collective-permute-start(bf16[4,16,4736]{2,1,0:T(8,128)(2,1)S(1)} %get-tuple-element.230), channel_id=1, source_target_pairs={{0,4},{1,5},{2,6},{3,7},{4,0},{5,1},{6,2},{7,3},{8,12},{9,13},{10,... | collective-permute-start | bytes 1818632 | tf_op jit(solution)/shard_map/ppermute | solution.py:748
  95.4 16.5 %collective-permute-start.34 = (bf16[4,16,4736]{2,1,0:T(8,128)(2,1)S(1)}, bf16[4,16,4736]{2,1,0:T(8,128)(2,1)S(1)}, u32[]{:S(2)}, u32[]{:S(2)}) collective-permute-start(bf16[4,16,4736]{2,1,0:T(8,128)(2,1)S(1)} %get-tuple-element.218), channel_id=1, source_target_pairs={{0,2},{1,3},{2,0},{3,1},{4,6},{5,7},{6,4},{7,5},{8,10},{9,11},{10,... | collective-permute-start | bytes 1818632 | tf_op jit(solution)/shard_map/ppermute | solution.py:748
  96.9 1.5 %collective-permute-start.32 = (bf16[256,512]{1,0:T(8,128)(2,1)S(1)}, bf16[256,512]{1,0:T(8,128)(2,1)S(1)}, u32[]{:S(2)}, u32[]{:S(2)}) collective-permute-start(bf16[256,512]{1,0:T(8,128)(2,1)S(1)} %get-tuple-element.219), channel_id=1, source_target_pairs={{0,1},{1,0},{2,3},{3,2},{4,5},{5,4},{6,7},{7,6},{8,9},{9,8},{10,11... | collective-permute-start | bytes 786440 | tf_op jit(solution)/shard_map/ppermute | solution.py:751
  98.7 18.9 %collective-permute-start.37 = (bf16[4,16,1536]{2,1,0:T(8,128)(2,1)S(1)}, bf16[4,16,1536]{2,1,0:T(8,128)(2,1)S(1)}, u32[]{:S(2)}, u32[]{:S(2)}) collective-permute-start(bf16[4,16,1536]{2,1,0:T(8,128)(2,1)S(1)} %get-tuple-element.236), channel_id=1, source_target_pairs={{0,6},{1,7},{2,4},{3,5},{4,2},{5,3},{6,0},{7,1},{8,14},{9,15},{10,... | collective-permute-start | bytes 589832 | tf_op jit(solution)/shard_map/ppermute | solution.py:748
  100.1 20.3 %collective-permute-start.38 = (bf16[4,16,1536]{2,1,0:T(8,128)(2,1)S(1)}, bf16[4,16,1536]{2,1,0:T(8,128)(2,1)S(1)}, u32[]{:S(2)}, u32[]{:S(2)}) collective-permute-start(bf16[4,16,1536]{2,1,0:T(8,128)(2,1)S(1)} %get-tuple-element.237), channel_id=1, source_target_pairs={{0,2},{1,3},{2,0},{3,1},{4,6},{5,7},{6,4},{7,5},{8,10},{9,11},{10,... | collective-permute-start | bytes 589832 | tf_op jit(solution)/shard_map/ppermute | solution.py:748
  101.6 18.8 %collective-permute-start.39 = (bf16[4,16,1536]{2,1,0:T(8,128)(2,1)S(1)}, bf16[4,16,1536]{2,1,0:T(8,128)(2,1)S(1)}, u32[]{:S(2)}, u32[]{:S(2)}) collective-permute-start(bf16[4,16,1536]{2,1,0:T(8,128)(2,1)S(1)} %get-tuple-element.238), channel_id=1, source_target_pairs={{0,4},{1,5},{2,6},{3,7},{4,0},{5,1},{6,2},{7,3},{8,12},{9,13},{10,... | collective-permute-start | bytes 589832 | tf_op jit(solution)/shard_map/ppermute | solution.py:748
  112.7 9.1 %collective-permute-start.40 = (bf16[16,4736]{1,0:T(8,128)(2,1)S(1)}, bf16[16,4736]{1,0:T(8,128)(2,1)S(1)}, u32[]{:S(2)}, u32[]{:S(2)}) collective-permute-start(bf16[16,4736]{1,0:T(8,128)(2,1)S(1)} %get-tuple-element.241), channel_id=1, source_target_pairs={{0,8},{1,9},{2,10},{3,11},{4,12},{5,13},{6,14},{7,15},{8,0},{9,1},... | collective-permute-start | bytes 454664 | tf_op jit(solution)/shard_map/ppermute | solution.py:748
  117.5 5.9 %collective-permute-start.41 = (bf16[16,4736]{1,0:T(8,128)(2,1)S(1)}, bf16[16,4736]{1,0:T(8,128)(2,1)S(1)}, u32[]{:S(2)}, u32[]{:S(2)}) collective-permute-start(bf16[16,4736]{1,0:T(8,128)(2,1)S(1)} %get-tuple-element.245), channel_id=1, source_target_pairs={{0,8},{1,9},{2,10},{3,11},{4,12},{5,13},{6,14},{7,15},{8,0},{9,1},... | collective-permute-start | bytes 454664 | tf_op jit(solution)/shard_map/ppermute | solution.py:748
  117.6 10.3 %collective-permute-start.36 = (bf16[128,1024]{1,0:T(8,128)(2,1)S(1)}, bf16[128,1024]{1,0:T(8,128)(2,1)S(1)}, u32[]{:S(2)}, u32[]{:S(2)}) collective-permute-start(bf16[128,1024]{1,0:T(8,128)(2,1)S(1)} %get-tuple-element.232), channel_id=1, source_target_pairs={{0,2},{1,3},{2,0},{3,1},{4,6},{5,7},{6,4},{7,5},{8,10},{9,11},{10,... | collective-permute-start | bytes 786440 | tf_op jit(solution)/shard_map/ppermute | solution.py:751
  123.4 7.8 %collective-permute-start.42 = (bf16[16,6272]{1,0:T(8,128)(2,1)S(1)}, bf16[16,6272]{1,0:T(8,128)(2,1)S(1)}, u32[]{:S(2)}, u32[]{:S(2)}) collective-permute-start(bf16[16,6272]{1,0:T(8,128)(2,1)S(1)} %shard_map.268), channel_id=1, source_target_pairs={{0,24},{1,25},{2,26},{3,27},{4,28},{5,29},{6,30},{7,31},{8,16},{9,... | collective-permute-start | bytes 602120 | tf_op jit(solution)/shard_map/ppermute | solution.py:748
  124.4 7.5 %collective-permute-start.43 = (bf16[16,1536]{1,0:T(8,128)(2,1)S(1)}, bf16[16,1536]{1,0:T(8,128)(2,1)S(1)}, u32[]{:S(2)}, u32[]{:S(2)}) collective-permute-start(bf16[16,1536]{1,0:T(8,128)(2,1)S(1)} %get-tuple-element.249), channel_id=1, source_target_pairs={{0,8},{1,9},{2,10},{3,11},{4,12},{5,13},{6,14},{7,15},{8,0},{9,1},... | collective-permute-start | bytes 147464 | tf_op jit(solution)/shard_map/ppermute | solution.py:748
  126.0 10.5 %collective-permute-start.44 = (bf16[16,1536]{1,0:T(8,128)(2,1)S(1)}, bf16[16,1536]{1,0:T(8,128)(2,1)S(1)}, u32[]{:S(2)}, u32[]{:S(2)}) collective-permute-start(bf16[16,1536]{1,0:T(8,128)(2,1)S(1)} %get-tuple-element.250), channel_id=1, source_target_pairs={{0,16},{1,17},{2,18},{3,19},{4,20},{5,21},{6,22},{7,23},{8,24},{9,... | collective-permute-start | bytes 147464 | tf_op jit(solution)/shard_map/ppermute | solution.py:748

commit v4 on v1

--- a/solution.py
+++ b/solution.py
@@ -891,7 +891,6 @@
             [((5, 4, 8, fine, BLOCK), BF16), vg_t, *attend_out],
             [row_b, bias_t, o_t],
             scalars=(4,),
-            micros=8,
         )
         full_a = full_a.reshape(5, width, BLOCK)
     else:

time: 137 us -> 138 us (level)
    ppermute x40, starting transfers between devices: 36.5 us -> 38.2 us  [flip(): return lax.ppermute(value, AXES, [(i, i ^ bit) for i in range(self.count)])]
where the time goes in v4:
time: 138 us; the launch traced here: 137 us
  waiting for transfers between devices  52.4 us (38%)
  starting transfers between devices  42.3 us (31%)
  Pallas kernels  40.9 us (30%)
    ppermute x40, waiting for transfers between devices, flip(): return lax.ppermute(value, AXES, [(i, i ^ bit) for i in range(self.count)])  48.1 us
    pallas_call x25, Pallas kernels, run(): pl.pallas_call(kernel, out_shape=[jax.ShapeDtypeStruct(s, t) for s, t in...  40.9 us
    ppermute x40, starting transfers between devices, flip(): return lax.ppermute(value, AXES, [(i, i ^ bit) for i in range(self.count)])  38.2 us
    ppermute x6, waiting for transfers between devices, flip_head(): lax.ppermute(value, 'head', [(i, i ^ bit) for i in range(self.heads)])  4.33 us
    ppermute x6, starting transfers between devices, flip_head(): lax.ppermute(value, 'head', [(i, i ^ bit) for i in range(self.heads)])  4.06 us
  transfers between devices with their start and end apart: 46, of which 22 were waited for; matrix products, arithmetic and copies ran while one was open for 0% of the time, Pallas kernels for 14%

profile of v4, /device:TPU:0, one launch (start us, length us, event | category | flops | bytes accessed | tf_op | source)
XLA Modules:
  0.0 137.4 jit_solution(14463489994651110586)
XLA Ops:
  0.7 2.4 %shard_map.246 = (bf16[128,1152]{1,0:T(8,128)(2,1)S(1)}, bf16[128,1152]{1,0:T(8,128)(2,1)S(1)}, bf16[17,16,128]{2,1,0:T(8,128)(2,1)S(1)}, bf16[8,16,512]{2,1,0:T(8,128)(2,1)S(1)}) custom-call(s32[4]{0:T(128)S(1)} %pad_add_fusion.place_ref.rest_0_.me_ref.info_ref, bf16[2,128,512]{2,1,0:T(8,128)(2,1)} %tok_ref.1, bf16[2,128,512]{2,1,0:T(8,128)(2,1)} %cot_ref.1, ...), custom_call_target="tpu_custom_call" | custom-call | flops 57500000 | bytes 1513648 | tf_op jit(solution)/shard_map/pallas_call | solution.py:714
  3.2 3.0 %collective-permute-start = (bf16[128,1152]{1,0:T(8,128)(2,1)S(1)}, bf16[128,1152]{1,0:T(8,128)(2,1)S(1)}, u32[]{:S(2)}, u32[]{:S(2)}) collective-permute-start(bf16[128,1152]{1,0:T(8,128)(2,1)S(1)} %get-tuple-element.137), channel_id=1, source_target_pairs={{0,2},{1,3},{2,0},{3,1},{4,6},{5,7},{6,4},{7,5},{8,10},{9,11},{10,... | collective-permute-start | bytes 884744 | tf_op jit(solution)/shard_map/ppermute | solution.py:747
  6.2 3.6 %collective-permute-start.4 = (bf16[17,16,128]{2,1,0:T(8,128)(2,1)S(1)}, bf16[17,16,128]{2,1,0:T(8,128)(2,1)S(1)}, u32[]{:S(2)}, u32[]{:S(2)}) collective-permute-start(bf16[17,16,128]{2,1,0:T(8,128)(2,1)S(1)} %get-tuple-element.142.refs_0_), channel_id=1, source_target_pairs={{0,24},{1,25},{2,26},{3,27},{4,28},{5,29},{6,30},{7,31},{8,16},{9,... | collective-permute-start | bytes 208904 | tf_op jit(solution)/shard_map/ppermute | solution.py:744
  9.8 0.8 collective-permute-start.2
  10.6 2.6 %collective-permute-done.4.refs_3_ = bf16[17,16,128]{2,1,0:T(8,128)(2,1)S(1)} collective-permute-done((bf16[17,16,128]{2,1,0:T(8,128)(2,1)S(1)}, bf16[17,16,128]{2,1,0:T(8,128)(2,1)S(1)}, u32[]{:S(2)}, u32[]{:S(2)}) %collective-permute-start.4) | collective-permute-done | bytes 69664 | tf_op jit(solution)/shard_map/ppermute | solution.py:744
  13.1 2.3 %collective-permute-done.3.refs_2_ = bf16[17,16,128]{2,1,0:T(8,128)(2,1)S(1)} collective-permute-done((bf16[17,16,128]{2,1,0:T(8,128)(2,1)S(1)}, bf16[17,16,128]{2,1,0:T(8,128)(2,1)S(1)}, u32[]{:S(2)}, u32[]{:S(2)}) %collective-permute-start.3) | collective-permute-done | bytes 69664 | tf_op jit(solution)/shard_map/ppermute | solution.py:744
  15.9 1.6 %collective-permute-start.6 = (bf16[4,17,16,128]{3,2,1,0:T(8,128)(2,1)S(1)}, bf16[4,17,16,128]{3,2,1,0:T(8,128)(2,1)S(1)}, u32[]{:S(2)}, u32[]{:S(2)}) collective-permute-start(bf16[4,17,16,128]{3,2,1,0:T(8,128)(2,1)S(1)} %shard_map.248.rest_1_), channel_id=1, source_target_pairs={{0,4},{1,5},{2,6},{3,7},{4,0},{5,1},{6,2},{7,3},{8,12},{9,13},{10,... | collective-permute-start | bytes 835592 | tf_op jit(solution)/shard_map/ppermute | solution.py:744
  17.5 0.5 collective-permute-start.5
  18.0 1.5 %collective-permute-start.10 = (bf16[8,16,512]{2,1,0:T(8,128)(2,1)S(1)}, bf16[8,16,512]{2,1,0:T(8,128)(2,1)S(1)}, u32[]{:S(2)}, u32[]{:S(2)}) collective-permute-start(bf16[8,16,512]{2,1,0:T(8,128)(2,1)S(1)} %get-tuple-element.145.refs_0_), channel_id=1, source_target_pairs={{0,16},{1,17},{2,18},{3,19},{4,20},{5,21},{6,22},{7,23},{8,24},{9,... | collective-permute-start | bytes 393224 | tf_op jit(solution)/shard_map/ppermute | solution.py:744
  19.5 0.7 copy-done
  20.2 1.8 %shard_map.247 = (bf16[256,1152]{1,0:T(8,128)(2,1)S(1)}, f32[256,512]{1,0:T(8,128)S(1)}, bf16[256,512]{1,0:T(8,128)(2,1)S(1)}, f32[256,512]{1,0:T(8,128)S(1)}, s...) custom-call(s32[4]{0:T(128)S(1)} %pad_add_fusion.place_ref.rest_0_.me_ref.info_ref, s32[2,8]{1,0:T(2,128)S(1)} %bitcast.35, ...), custom_call_target="tpu_custom_call" | custom-call | flops 57500000 | bytes 2637904 | tf_op jit(solution)/shard_map/pallas_call | solution.py:714
  22.1 1.7 %collective-permute-start.9 = (bf16[8,16,512]{2,1,0:T(8,128)(2,1)S(1)}, bf16[8,16,512]{2,1,0:T(8,128)(2,1)S(1)}, u32[]{:S(2)}, u32[]{:S(2)}) collective-permute-start(bf16[8,16,512]{2,1,0:T(8,128)(2,1)S(1)} %get-tuple-element.145.refs_0_), channel_id=1, source_target_pairs={{0,8},{1,9},{2,10},{3,11},{4,12},{5,13},{6,14},{7,15},{8,0},{9,1},... | collective-permute-start | bytes 393224 | tf_op jit(solution)/shard_map/ppermute | solution.py:744
  23.8 1.9 %collective-permute-done.10.refs_2_ = bf16[8,16,512]{2,1,0:T(8,128)(2,1)S(1)} collective-permute-done((bf16[8,16,512]{2,1,0:T(8,128)(2,1)S(1)}, bf16[8,16,512]{2,1,0:T(8,128)(2,1)S(1)}, u32[]{:S(2)}, u32[]{:S(2)}) %collective-permute-start.10) | collective-permute-done | bytes 131104 | tf_op jit(solution)/shard_map/ppermute | solution.py:744
  25.7 2.1 %collective-permute-start.7 = (bf16[8,16,512]{2,1,0:T(8,128)(2,1)S(1)}, bf16[8,16,512]{2,1,0:T(8,128)(2,1)S(1)}, u32[]{:S(2)}, u32[]{:S(2)}) collective-permute-start(bf16[8,16,512]{2,1,0:T(8,128)(2,1)S(1)} %get-tuple-element.145.refs_0_), channel_id=1, source_target_pairs={{0,24},{1,25},{2,26},{3,27},{4,28},{5,29},{6,30},{7,31},{8,16},{9,... | collective-permute-start | bytes 393224 | tf_op jit(solution)/shard_map/ppermute | solution.py:744
  27.8 0.7 collective-permute-done.9.refs_1_
  28.4 4.0 %collective-permute-done.7.refs_3_ = bf16[8,16,512]{2,1,0:T(8,128)(2,1)S(1)} collective-permute-done((bf16[8,16,512]{2,1,0:T(8,128)(2,1)S(1)}, bf16[8,16,512]{2,1,0:T(8,128)(2,1)S(1)}, u32[]{:S(2)}, u32[]{:S(2)}) %collective-permute-start.7) | collective-permute-done | bytes 131104 | tf_op jit(solution)/shard_map/ppermute | solution.py:744
  32.4 0.7 shard_map.249.rest_1_
  33.2 1.5 %collective-permute-start.12 = (bf16[4,8,16,512]{3,2,1,0:T(8,128)(2,1)S(1)}, bf16[4,8,16,512]{3,2,1,0:T(8,128)(2,1)S(1)}, u32[]{:S(2)}, u32[]{:S(2)}) collective-permute-start(bf16[4,8,16,512]{3,2,1,0:T(8,128)(2,1)S(1)} %shard_map.249.rest_1_), channel_id=1, source_target_pairs={{0,2},{1,3},{2,0},{3,1},{4,6},{5,7},{6,4},{7,5},{8,10},{9,11},{10,... | collective-permute-start | bytes 1572872 | tf_op jit(solution)/shard_map/ppermute | solution.py:744
  34.7 0.5 collective-permute-start.11
  35.2 0.5 collective-permute-start.8
  35.8 0.5 collective-permute-start.15
  36.3 11.7 %collective-permute-done.12.by_x_ref.rest_2_ = bf16[4,8,16,512]{3,2,1,0:T(8,128)(2,1)S(1)} collective-permute-done((bf16[4,8,16,512]{3,2,1,0:T(8,128)(2,1)S(1)}, bf16[4,8,16,512]{3,2,1,0:T(8,128)(2,1)S(1)}, u32[]{:S(2)}, u32[]{:S(2)}) %collective-permute-start.12) | collective-permute-done | bytes 524320 | tf_op jit(solution)/shard_map/ppermute | solution.py:744
  48.2 2.7 %collective-permute-done.8.rest_4_ = bf16[4,17,16,128]{3,2,1,0:T(8,128)(2,1)S(1)} collective-permute-done((bf16[4,17,16,128]{3,2,1,0:T(8,128)(2,1)S(1)}, bf16[4,17,16,128]{3,2,1,0:T(8,128)(2,1)S(1)}, u32[]{:S(2)}, u32[]{:S(2)}) %collective-permute-start.8) | collective-permute-done | bytes 278560 | tf_op jit(solution)/shard_map/ppermute | solution.py:744
  50.9 0.6 collective-permute-start.21
  51.7 1.4 %collective-permute-start.20 = (bf16[2,8,16,512]{3,2,1,0:T(8,128)(2,1)S(1)}, bf16[2,8,16,512]{3,2,1,0:T(8,128)(2,1)S(1)}, u32[]{:S(2)}, u32[]{:S(2)}) collective-permute-start(bf16[2,8,16,512]{3,2,1,0:T(8,128)(2,1)S(1)} %get-tuple-element.148), channel_id=1, source_target_pairs={{0,2},{1,3},{2,0},{3,1},{4,6},{5,7},{6,4},{7,5},{8,10},{9,11},{10,... | collective-permute-start | bytes 786440 | tf_op jit(solution)/shard_map/ppermute | solution.py:744
  53.6 3.9 %shard_map.251 = (bf16[5,4,8,16,512]{4,3,2,1,0:T(8,128)(2,1)S(1)}, f32[8,512]{1,0:T(8,128)S(1)}, bf16[4,512,128]{2,1,0:T(8,128)(2,1)S(1)}, bf16[512,512]{1,0:T(8...) custom-call(bf16[256,512]{1,0:T(8,128)(2,1)S(1)} %get-tuple-element.139, ...), custom_call_target="tpu_custom_call" | custom-call | flops 57500000 | bytes 9469968 | tf_op jit(solution)/shard_map/pallas_call | solution.py:714
  57.5 2.1 %collective-permute-done.21.rest_8_ = bf16[2,8,16,512]{3,2,1,0:T(8,128)(2,1)S(1)} collective-permute-done((bf16[2,8,16,512]{3,2,1,0:T(8,128)(2,1)S(1)}, bf16[2,8,16,512]{3,2,1,0:T(8,128)(2,1)S(1)}, u32[]{:S(2)}, u32[]{:S(2)}) %collective-permute-start.21) | collective-permute-done | bytes 262176 | tf_op jit(solution)/shard_map/ppermute | solution.py:744
  59.6 0.6 collective-permute-done.20.rest_7_
  60.2 0.5 collective-permute-start.23
  62.1 3.3 %shard_map.253 = (bf16[4,4,8,16,512]{4,3,2,1,0:T(8,128)(2,1)S(1)}, bf16[4,8,4,16,512]{4,3,2,1,0:T(8,128)(2,1)S(1)}, bf16[256,2048]{1,0:T(8,128)(2,1)S(1)}, bf16[...) custom-call(f32[256,512]{1,0:T(8,128)S(1)} %get-tuple-element.153.n1, ...), custom_call_target="tpu_custom_call" | custom-call | flops 6325000192 | bytes 15024144 | tf_op jit(solution)/shard_map/pallas_call | solution.py:714
  65.7 1.4 %collective-permute-done.24 = bf16[1,256,512]{2,1,0:T(8,128)(2,1)S(1)} collective-permute-done((bf16[1,256,512]{2,1,0:T(8,128)(2,1)S(1)}, bf16[1,256,512]{2,1,0:T(8,128)(2,1)S(1)}, u32[]{:S(2)}, u32[]{:S(2)}) %collective-permute-start.24) | collective-permute-done | bytes 262176 | tf_op jit(solution)/shard_map/ppermute | solution.py:747
  67.1 10.4 %shard_map.254 = (f32[256,512]{1,0:T(8,128)S(1)}, f32[256,512]{1,0:T(8,128)S(1)}, bf16[256,512]{1,0:T(8,128)(2,1)S(1)}, bf16[256,512]{1,0:T(8,128)(2,1)S(1)}, bf...) custom-call(f32[256,512]{1,0:T(8,128)S(1)} %get-tuple-element.160.x_, ...), custom_call_target="tpu_custom_call" | custom-call | flops 18055000064 | bytes 15450112 | tf_op jit(solution)/shard_map/pallas_call | solution.py:714
  77.7 1.4 %collective-permute-done.25.more_ref = bf16[256,512]{1,0:T(8,128)(2,1)S(1)} collective-permute-done((bf16[256,512]{1,0:T(8,128)(2,1)S(1)}, bf16[256,512]{1,0:T(8,128)(2,1)S(1)}, u32[]{:S(2)}, u32[]{:S(2)}) %collective-permute-start.25) | collective-permute-done | bytes 262176 | tf_op jit(solution)/shard_map/ppermute | solution.py:747
  79.1 2.5 %shard_map.255 = (bf16[256,512]{1,0:T(8,128)(2,1)S(1)}, f32[256,512]{1,0:T(8,128)S(1)}, f32[256,512]{1,0:T(8,128)S(1)}, f32[5,8,512]{2,1,0:T(8,128)S(1)}, bf16[4...) custom-call(s32[4]{0:T(128)S(1)} %pad_add_fusion.place_ref.rest_0_.me_ref.info_ref, ...), custom_call_target="tpu_custom_call" | custom-call | flops 2300000000 | bytes 8028176 | tf_op jit(solution)/shard_map/pallas_call | solution.py:714
  81.8 1.8 %shard_map.256 = (bf16[256,2048]{1,0:T(8,128)(2,1)S(1)}, bf16[256,512]{1,0:T(8,128)(2,1)S(1)}, f32[256,512]{1,0:T(8,128)S(1)}, bf16[256,512]{1,0:T(8,128)(2,1)S(1)}, f32[5,8,512]{2,1,0:T(8,128)S(1)}) custom-call(bf16[256,512]{1,0:T(8,128)(2,1)S(1)} %get-tuple-element.175.b2_ref, f32[256,512]{1,0:T(8,128)S(1)} %get-tuple-element.176.gsec_ref, ...), custom_call_target="tpu_custom_call" | custom-call | flops 2529999872 | bytes 12107776 | tf_op jit(solution)/shard_map/pallas_call | solution.py:714
  83.6 0.7 collective-permute-done.26.got_ref
  84.6 2.2 %shard_map.258 = (bf16[4,4,16,2688]{3,2,1,0:T(8,128)(2,1)S(1)}, bf16[4,4,16,2688]{3,2,1,0:T(8,128)(2,1)S(1)}) custom-call(s32[4]{0:T(128)S(1)} %pad_add_fusion.place_ref.rest_0_.me_ref.info_ref, bf16[256,2048]{1,0:T(8,128)(2,1)S(1)} %get-tuple-element.189.b1_ref, bf16[256,512]{1,0:T(8,128)(2,1)S(1)} %get-tuple-element.190.b0_ref, ...), custom_call_target="tpu_custom_call" | custom-call | flops 2300000000 | bytes 6520848 | tf_op jit(solution)/shard_map/pallas_call | solution.py:714
  87.0 1.4 %collective-permute-start.28 = (bf16[2,64,512]{2,1,0:T(8,128)(2,1)S(1)}, bf16[2,64,512]{2,1,0:T(8,128)(2,1)S(1)}, u32[]{:S(2)}, u32[]{:S(2)}) collective-permute-start(bf16[2,64,512]{2,1,0:T(8,128)(2,1)S(1)} %get-tuple-element.188), channel_id=1, source_target_pairs={{0,2},{1,3},{2,0},{3,1},{4,6},{5,7},{6,4},{7,5},{8,10},{9,11},{10,... | collective-permute-start | bytes 393224 | tf_op jit(solution)/shard_map/ppermute | solution.py:744
  88.4 1.5 %collective-permute-start.29 = (bf16[2,64,512]{2,1,0:T(8,128)(2,1)S(1)}, bf16[2,64,512]{2,1,0:T(8,128)(2,1)S(1)}, u32[]{:S(2)}, u32[]{:S(2)}) collective-permute-start(bf16[2,64,512]{2,1,0:T(8,128)(2,1)S(1)} %get-tuple-element.212), channel_id=1, source_target_pairs={{0,4},{1,5},{2,6},{3,7},{4,0},{5,1},{6,2},{7,3},{8,12},{9,13},{10,... | collective-permute-start | bytes 393224 | tf_op jit(solution)/shard_map/ppermute | solution.py:744
  90.3 1.5 %collective-permute-start.30 = (bf16[2,16,2688]{2,1,0:T(8,128)(2,1)S(1)}, bf16[2,16,2688]{2,1,0:T(8,128)(2,1)S(1)}, u32[]{:S(2)}, u32[]{:S(2)}) collective-permute-start(bf16[2,16,2688]{2,1,0:T(8,128)(2,1)S(1)} %get-tuple-element.199), channel_id=1, source_target_pairs={{0,2},{1,3},{2,0},{3,1},{4,6},{5,7},{6,4},{7,5},{8,10},{9,11},{10,... | collective-permute-start | bytes 516104 | tf_op jit(solution)/shard_map/ppermute | solution.py:744
  91.8 1.5 %collective-permute-start.31 = (bf16[2,16,2688]{2,1,0:T(8,128)(2,1)S(1)}, bf16[2,16,2688]{2,1,0:T(8,128)(2,1)S(1)}, u32[]{:S(2)}, u32[]{:S(2)}) collective-permute-start(bf16[2,16,2688]{2,1,0:T(8,128)(2,1)S(1)} %get-tuple-element.215), channel_id=1, source_target_pairs={{0,4},{1,5},{2,6},{3,7},{4,0},{5,1},{6,2},{7,3},{8,12},{9,13},{10,... | collective-permute-start | bytes 516104 | tf_op jit(solution)/shard_map/ppermute | solution.py:744
  93.3 2.2 %shard_map.260 = (bf16[256,1536]{1,0:T(8,128)(2,1)S(1)}, bf16[256,1024]{1,0:T(8,128)(2,1)S(1)}) custom-call(bf16[256,512]{1,0:T(8,128)(2,1)S(1)} %get-tuple-element.200.gctx_ref, bf16[4,512,128]{2,1,0:T(8,128)(2,1)S(1)} %get-tuple-element.201.q2_ref, bf16[512,512]{1,0:T(8,128)(2,1)S(1)} %get-tuple-element.202.k_ref, ...), custom_call_target="tpu_custom_call" | custom-call | flops 3449999872 | bytes 5505024 | tf_op jit(solution)/shard_map/pallas_call | solution.py:714
  95.5 3.2 %shard_map.261 = (f32[256,512]{1,0:T(8,128)S(1)}, bf16[256,512]{1,0:T(8,128)(2,1)S(1)}, bf16[4,4,16,1536]{3,2,1,0:T(8,128)(2,1)S(1)}, bf16[4,4,16,1536]{3,2,1,0:T(8,128)(2,1)S(1)}) custom-call(s32[4]{0:T(128)S(1)} %pad_add_fusion.place_ref.rest_0_.me_ref.info_ref, f32[256,512]{1,0:T(8,128)S(1)} %get-tuple-element.181.base_ref, ...), custom_call_target="tpu_custom_call" | custom-call | flops 57500000 | bytes 9175056 | tf_op jit(solution)/shard_map/pallas_call | solution.py:714
  99.0 0.8 collective-permute-start.35
  99.7 0.6 collective-permute-start.34
  100.3 1.5 %collective-permute-done.32.more_ref = bf16[256,512]{1,0:T(8,128)(2,1)S(1)} collective-permute-done((bf16[256,512]{1,0:T(8,128)(2,1)S(1)}, bf16[256,512]{1,0:T(8,128)(2,1)S(1)}, u32[]{:S(2)}, u32[]{:S(2)}) %collective-permute-start.32) | collective-permute-done | bytes 262176 | tf_op jit(solution)/shard_map/ppermute | solution.py:747
  102.1 2.3 %collective-permute-start.37 = (bf16[4,16,1536]{2,1,0:T(8,128)(2,1)S(1)}, bf16[4,16,1536]{2,1,0:T(8,128)(2,1)S(1)}, u32[]{:S(2)}, u32[]{:S(2)}) collective-permute-start(bf16[4,16,1536]{2,1,0:T(8,128)(2,1)S(1)} %get-tuple-element.234), channel_id=1, source_target_pairs={{0,6},{1,7},{2,4},{3,5},{4,2},{5,3},{6,0},{7,1},{8,14},{9,15},{10,... | collective-permute-start | bytes 589832 | tf_op jit(solution)/shard_map/ppermute | solution.py:744
  104.4 0.6 collective-permute-start.38
  105.0 0.7 collective-permute-start.39
  105.7 9.9 %collective-permute-done.35.got_y_ref = bf16[4,16,4736]{2,1,0:T(8,128)(2,1)S(1)} collective-permute-done((bf16[4,16,4736]{2,1,0:T(8,128)(2,1)S(1)}, bf16[4,16,4736]{2,1,0:T(8,128)(2,1)S(1)}, u32[]{:S(2)}, u32[]{:S(2)}) %collective-permute-start.35) | collective-permute-done | bytes 606240 | tf_op jit(solution)/shard_map/ppermute | solution.py:744
  115.6 0.7 collective-permute-done.34.got_x_ref
  116.3 0.8 shard_map.265
  117.1 2.0 %collective-permute-start.41 = (bf16[16,4736]{1,0:T(8,128)(2,1)S(1)}, bf16[16,4736]{1,0:T(8,128)(2,1)S(1)}, u32[]{:S(2)}, u32[]{:S(2)}) collective-permute-start(bf16[16,4736]{1,0:T(8,128)(2,1)S(1)} %get-tuple-element.243), channel_id=1, source_target_pairs={{0,8},{1,9},{2,10},{3,11},{4,12},{5,13},{6,14},{7,15},{8,0},{9,1},... | collective-permute-start | bytes 454664 | tf_op jit(solution)/shard_map/ppermute | solution.py:744
  119.1 2.2 %collective-permute-done.37.b_ref = bf16[4,16,1536]{2,1,0:T(8,128)(2,1)S(1)} collective-permute-done((bf16[4,16,1536]{2,1,0:T(8,128)(2,1)S(1)}, bf16[4,16,1536]{2,1,0:T(8,128)(2,1)S(1)}, u32[]{:S(2)}, u32[]{:S(2)}) %collective-permute-start.37) | collective-permute-done | bytes 196640 | tf_op jit(solution)/shard_map/ppermute | solution.py:744
  121.3 0.6 collective-permute-start.36
  121.9 2.9 %collective-permute-done.38.c_ref = bf16[4,16,1536]{2,1,0:T(8,128)(2,1)S(1)} collective-permute-done((bf16[4,16,1536]{2,1,0:T(8,128)(2,1)S(1)}, bf16[4,16,1536]{2,1,0:T(8,128)(2,1)S(1)}, u32[]{:S(2)}, u32[]{:S(2)}) %collective-permute-start.38) | collective-permute-done | bytes 196640 | tf_op jit(solution)/shard_map/ppermute | solution.py:744
  124.7 0.7 shard_map.267
  125.5 2.4 %collective-permute-start.42 = (bf16[16,4736]{1,0:T(8,128)(2,1)S(1)}, bf16[16,4736]{1,0:T(8,128)(2,1)S(1)}, u32[]{:S(2)}, u32[]{:S(2)}) collective-permute-start(bf16[16,4736]{1,0:T(8,128)(2,1)S(1)} %shard_map.268), channel_id=1, source_target_pairs={{0,24},{1,25},{2,26},{3,27},{4,28},{5,29},{6,30},{7,31},{8,16},{9,... | collective-permute-start | bytes 454664 | tf_op jit(solution)/shard_map/ppermute | solution.py:744
  127.9 2.0 %collective-permute-start.44 = (bf16[16,1536]{1,0:T(8,128)(2,1)S(1)}, bf16[16,1536]{1,0:T(8,128)(2,1)S(1)}, u32[]{:S(2)}, u32[]{:S(2)}) collective-permute-start(bf16[16,1536]{1,0:T(8,128)(2,1)S(1)} %get-tuple-element.247), channel_id=1, source_target_pairs={{0,16},{1,17},{2,18},{3,19},{4,20},{5,21},{6,22},{7,23},{8,24},{9,... | collective-permute-start | bytes 147464 | tf_op jit(solution)/shard_map/ppermute | solution.py:744
  129.9 2.3 %collective-permute-start.45 = (bf16[16,1536]{1,0:T(8,128)(2,1)S(1)}, bf16[16,1536]{1,0:T(8,128)(2,1)S(1)}, u32[]{:S(2)}, u32[]{:S(2)}) collective-permute-start(bf16[16,1536]{1,0:T(8,128)(2,1)S(1)} %get-tuple-element.248), channel_id=1, source_target_pairs={{0,24},{1,25},{2,26},{3,27},{4,28},{5,29},{6,30},{7,31},{8,16},{9,... | collective-permute-start | bytes 147464 | tf_op jit(solution)/shard_map/ppermute | solution.py:744
  132.3 1.6 %shard_map.266 = (f32[2,128,512]{2,1,0:T(8,128)}, f32[2,128,512]{2,1,0:T(8,128)}) custom-call(s32[4]{0:T(128)S(1)} %pad_add_fusion.place_ref.rest_0_.me_ref.info_ref, f32[256,512]{1,0:T(8,128)S(1)} %get-tuple-element.166.out_ref, f32[256,512]{1,0:T(8,128)S(1)} %get-tuple-element.218.in_ref, bf16[128,1024]{1,0:T(8,128)(2,1)S(1)} %collective-permute-done.36.back_ref), custom_call_target="tpu_custom_call" | custom-call | flops 57500000 | bytes 2359312 | tf_op jit(solution)/shard_map/pallas_call | solution.py:714
  133.8 0.7 shard_map.269
  134.6 2.1 %collective-permute-done.44.c_ref = bf16[16,1536]{1,0:T(8,128)(2,1)S(1)} collective-permute-done((bf16[16,1536]{1,0:T(8,128)(2,1)S(1)}, bf16[16,1536]{1,0:T(8,128)(2,1)S(1)}, u32[]{:S(2)}, u32[]{:S(2)}) %collective-permute-start.44) | collective-permute-done | bytes 49184 | tf_op jit(solution)/shard_map/ppermute | solution.py:744
  136.7 0.6 shard_map.270
  (56 shorter events, 5.0 us)
Async XLA Ops:
  3.2 12.7 %collective-permute-start = (bf16[128,1152]{1,0:T(8,128)(2,1)S(1)}, bf16[128,1152]{1,0:T(8,128)(2,1)S(1)}, u32[]{:S(2)}, u32[]{:S(2)}) collective-permute-start(bf16[128,1152]{1,0:T(8,128)(2,1)S(1)} %get-tuple-element.137), channel_id=1, source_target_pairs={{0,2},{1,3},{2,0},{3,1},{4,6},{5,7},{6,4},{7,5},{8,10},{9,11},{10,... | collective-permute-start | bytes 884744 | tf_op jit(solution)/shard_map/ppermute | solution.py:747
  6.2 7.0 %collective-permute-start.4 = (bf16[17,16,128]{2,1,0:T(8,128)(2,1)S(1)}, bf16[17,16,128]{2,1,0:T(8,128)(2,1)S(1)}, u32[]{:S(2)}, u32[]{:S(2)}) collective-permute-start(bf16[17,16,128]{2,1,0:T(8,128)(2,1)S(1)} %get-tuple-element.142.refs_0_), channel_id=1, source_target_pairs={{0,24},{1,25},{2,26},{3,27},{4,28},{5,29},{6,30},{7,31},{8,16},{9,... | collective-permute-start | bytes 208904 | tf_op jit(solution)/shard_map/ppermute | solution.py:744
  9.8 5.7 %collective-permute-start.3 = (bf16[17,16,128]{2,1,0:T(8,128)(2,1)S(1)}, bf16[17,16,128]{2,1,0:T(8,128)(2,1)S(1)}, u32[]{:S(2)}, u32[]{:S(2)}) collective-permute-start(bf16[17,16,128]{2,1,0:T(8,128)(2,1)S(1)} %get-tuple-element.142.refs_0_), channel_id=1, source_target_pairs={{0,16},{1,17},{2,18},{3,19},{4,20},{5,21},{6,22},{7,23},{8,24},{9,... | collective-permute-start | bytes 208904 | tf_op jit(solution)/shard_map/ppermute | solution.py:744
  9.8 5.7 %collective-permute-start.2 = (bf16[17,16,128]{2,1,0:T(8,128)(2,1)S(1)}, bf16[17,16,128]{2,1,0:T(8,128)(2,1)S(1)}, u32[]{:S(2)}, u32[]{:S(2)}) collective-permute-start(bf16[17,16,128]{2,1,0:T(8,128)(2,1)S(1)} %get-tuple-element.142.refs_0_), channel_id=1, source_target_pairs={{0,8},{1,9},{2,10},{3,11},{4,12},{5,13},{6,14},{7,15},{8,0},{9,1},... | collective-permute-start | bytes 208904 | tf_op jit(solution)/shard_map/ppermute | solution.py:744
  15.9 17.2 %collective-permute-start.6 = (bf16[4,17,16,128]{3,2,1,0:T(8,128)(2,1)S(1)}, bf16[4,17,16,128]{3,2,1,0:T(8,128)(2,1)S(1)}, u32[]{:S(2)}, u32[]{:S(2)}) collective-permute-start(bf16[4,17,16,128]{3,2,1,0:T(8,128)(2,1)S(1)} %shard_map.248.rest_1_), channel_id=1, source_target_pairs={{0,4},{1,5},{2,6},{3,7},{4,0},{5,1},{6,2},{7,3},{8,12},{9,13},{10,... | collective-permute-start | bytes 835592 | tf_op jit(solution)/shard_map/ppermute | solution.py:744
  17.5 15.7 %collective-permute-start.5 = (bf16[4,17,16,128]{3,2,1,0:T(8,128)(2,1)S(1)}, bf16[4,17,16,128]{3,2,1,0:T(8,128)(2,1)S(1)}, u32[]{:S(2)}, u32[]{:S(2)}) collective-permute-start(bf16[4,17,16,128]{3,2,1,0:T(8,128)(2,1)S(1)} %shard_map.248.rest_1_), channel_id=1, source_target_pairs={{0,2},{1,3},{2,0},{3,1},{4,6},{5,7},{6,4},{7,5},{8,10},{9,11},{10,... | collective-permute-start | bytes 835592 | tf_op jit(solution)/shard_map/ppermute | solution.py:744
  18.0 7.7 %collective-permute-start.10 = (bf16[8,16,512]{2,1,0:T(8,128)(2,1)S(1)}, bf16[8,16,512]{2,1,0:T(8,128)(2,1)S(1)}, u32[]{:S(2)}, u32[]{:S(2)}) collective-permute-start(bf16[8,16,512]{2,1,0:T(8,128)(2,1)S(1)} %get-tuple-element.145.refs_0_), channel_id=1, source_target_pairs={{0,16},{1,17},{2,18},{3,19},{4,20},{5,21},{6,22},{7,23},{8,24},{9,... | collective-permute-start | bytes 393224 | tf_op jit(solution)/shard_map/ppermute | solution.py:744
  19.5 0.7 copy-start
  22.0 11.1 %collective-permute-start.1 = (bf16[1,256,512]{2,1,0:T(8,128)(2,1)S(1)}, bf16[1,256,512]{2,1,0:T(8,128)(2,1)S(1)}, u32[]{:S(2)}, u32[]{:S(2)}) collective-permute-start(bf16[1,256,512]{2,1,0:T(8,128)(2,1)S(1)} %bitcast.29), channel_id=1, source_target_pairs={{0,1},{1,0},{2,3},{3,2},{4,5},{5,4},{6,7},{7,6},{8,9},{9,8},{10,11... | collective-permute-start | bytes 786440 | tf_op jit(solution)/shard_map/ppermute | solution.py:747
  22.1 6.3 %collective-permute-start.9 = (bf16[8,16,512]{2,1,0:T(8,128)(2,1)S(1)}, bf16[8,16,512]{2,1,0:T(8,128)(2,1)S(1)}, u32[]{:S(2)}, u32[]{:S(2)}) collective-permute-start(bf16[8,16,512]{2,1,0:T(8,128)(2,1)S(1)} %get-tuple-element.145.refs_0_), channel_id=1, source_target_pairs={{0,8},{1,9},{2,10},{3,11},{4,12},{5,13},{6,14},{7,15},{8,0},{9,1},... | collective-permute-start | bytes 393224 | tf_op jit(solution)/shard_map/ppermute | solution.py:744
  25.7 6.8 %collective-permute-start.7 = (bf16[8,16,512]{2,1,0:T(8,128)(2,1)S(1)}, bf16[8,16,512]{2,1,0:T(8,128)(2,1)S(1)}, u32[]{:S(2)}, u32[]{:S(2)}) collective-permute-start(bf16[8,16,512]{2,1,0:T(8,128)(2,1)S(1)} %get-tuple-element.145.refs_0_), channel_id=1, source_target_pairs={{0,24},{1,25},{2,26},{3,27},{4,28},{5,29},{6,30},{7,31},{8,16},{9,... | collective-permute-start | bytes 393224 | tf_op jit(solution)/shard_map/ppermute | solution.py:744
  33.2 14.8 %collective-permute-start.12 = (bf16[4,8,16,512]{3,2,1,0:T(8,128)(2,1)S(1)}, bf16[4,8,16,512]{3,2,1,0:T(8,128)(2,1)S(1)}, u32[]{:S(2)}, u32[]{:S(2)}) collective-permute-start(bf16[4,8,16,512]{3,2,1,0:T(8,128)(2,1)S(1)} %shard_map.249.rest_1_), channel_id=1, source_target_pairs={{0,2},{1,3},{2,0},{3,1},{4,6},{5,7},{6,4},{7,5},{8,10},{9,11},{10,... | collective-permute-start | bytes 1572872 | tf_op jit(solution)/shard_map/ppermute | solution.py:744
  34.7 13.2 %collective-permute-start.11 = (bf16[4,8,16,512]{3,2,1,0:T(8,128)(2,1)S(1)}, bf16[4,8,16,512]{3,2,1,0:T(8,128)(2,1)S(1)}, u32[]{:S(2)}, u32[]{:S(2)}) collective-permute-start(bf16[4,8,16,512]{3,2,1,0:T(8,128)(2,1)S(1)} %shard_map.249.rest_1_), channel_id=1, source_target_pairs={{0,4},{1,5},{2,6},{3,7},{4,0},{5,1},{6,2},{7,3},{8,12},{9,13},{10,... | collective-permute-start | bytes 1572872 | tf_op jit(solution)/shard_map/ppermute | solution.py:744
  35.2 15.7 %collective-permute-start.8 = (bf16[4,17,16,128]{3,2,1,0:T(8,128)(2,1)S(1)}, bf16[4,17,16,128]{3,2,1,0:T(8,128)(2,1)S(1)}, u32[]{:S(2)}, u32[]{:S(2)}) collective-permute-start(bf16[4,17,16,128]{3,2,1,0:T(8,128)(2,1)S(1)} %collective-permute-done.6.rest_3_), channel_id=1, source_target_pairs={{0,2},{1,3},{2,0},{3,1},{4,6},{5,7},{6,4},{7,5},{8,10},{9,11},{10,... | collective-permute-start | bytes 835592 | tf_op jit(solution)/shard_map/ppermute | solution.py:744
  35.8 15.7 %collective-permute-start.13 = (bf16[4,17,16,128]{3,2,1,0:T(8,128)(2,1)S(1)}, bf16[4,17,16,128]{3,2,1,0:T(8,128)(2,1)S(1)}, u32[]{:S(2)}, u32[]{:S(2)}) collective-permute-start(bf16[4,17,16,128]{3,2,1,0:T(8,128)(2,1)S(1)} %shard_map.248.rest_1_), channel_id=1, source_target_pairs={{0,1},{1,0},{2,3},{3,2},{4,5},{5,4},{6,7},{7,6},{8,9},{9,8},{10,11... | collective-permute-start | bytes 835592 | tf_op jit(solution)/shard_map/ppermute | solution.py:744
  35.8 16.0 %collective-permute-start.15 = (bf16[4,17,16,128]{3,2,1,0:T(8,128)(2,1)S(1)}, bf16[4,17,16,128]{3,2,1,0:T(8,128)(2,1)S(1)}, u32[]{:S(2)}, u32[]{:S(2)}) collective-permute-start(bf16[4,17,16,128]{3,2,1,0:T(8,128)(2,1)S(1)} %collective-permute-done.6.rest_3_), channel_id=1, source_target_pairs={{0,1},{1,0},{2,3},{3,2},{4,5},{5,4},{6,7},{7,6},{8,9},{9,8},{10,11... | collective-permute-start | bytes 835592 | tf_op jit(solution)/shard_map/ppermute | solution.py:744
  47.9 5.2 %collective-permute-start.14 = (bf16[4,17,16,128]{3,2,1,0:T(8,128)(2,1)S(1)}, bf16[4,17,16,128]{3,2,1,0:T(8,128)(2,1)S(1)}, u32[]{:S(2)}, u32[]{:S(2)}) collective-permute-start(bf16[4,17,16,128]{3,2,1,0:T(8,128)(2,1)S(1)} %collective-permute-done.5.rest_2_), channel_id=1, source_target_pairs={{0,1},{1,0},{2,3},{3,2},{4,5},{5,4},{6,7},{7,6},{8,9},{9,8},{10,11... | collective-permute-start | bytes 835592 | tf_op jit(solution)/shard_map/ppermute | solution.py:744
  50.9 2.2 %collective-permute-start.16 = (bf16[4,17,16,128]{3,2,1,0:T(8,128)(2,1)S(1)}, bf16[4,17,16,128]{3,2,1,0:T(8,128)(2,1)S(1)}, u32[]{:S(2)}, u32[]{:S(2)}) collective-permute-start(bf16[4,17,16,128]{3,2,1,0:T(8,128)(2,1)S(1)} %collective-permute-done.8.rest_4_), channel_id=1, source_target_pairs={{0,1},{1,0},{2,3},{3,2},{4,5},{5,4},{6,7},{7,6},{8,9},{9,8},{10,11... | collective-permute-start | bytes 835592 | tf_op jit(solution)/shard_map/ppermute | solution.py:744
  50.9 8.7 %collective-permute-start.21 = (bf16[2,8,16,512]{3,2,1,0:T(8,128)(2,1)S(1)}, bf16[2,8,16,512]{3,2,1,0:T(8,128)(2,1)S(1)}, u32[]{:S(2)}, u32[]{:S(2)}) collective-permute-start(bf16[2,8,16,512]{3,2,1,0:T(8,128)(2,1)S(1)} %get-tuple-element.158), channel_id=1, source_target_pairs={{0,4},{1,5},{2,6},{3,7},{4,0},{5,1},{6,2},{7,3},{8,12},{9,13},{10,... | collective-permute-start | bytes 786440 | tf_op jit(solution)/shard_map/ppermute | solution.py:744
  51.5 9.7 %collective-permute-start.17 = (bf16[4,8,16,512]{3,2,1,0:T(8,128)(2,1)S(1)}, bf16[4,8,16,512]{3,2,1,0:T(8,128)(2,1)S(1)}, u32[]{:S(2)}, u32[]{:S(2)}) collective-permute-start(bf16[4,8,16,512]{3,2,1,0:T(8,128)(2,1)S(1)} %shard_map.249.rest_1_), channel_id=1, source_target_pairs={{0,1},{1,0},{2,3},{3,2},{4,5},{5,4},{6,7},{7,6},{8,9},{9,8},{10,11... | collective-permute-start | bytes 1572872 | tf_op jit(solution)/shard_map/ppermute | solution.py:744
  51.7 8.5 %collective-permute-start.20 = (bf16[2,8,16,512]{3,2,1,0:T(8,128)(2,1)S(1)}, bf16[2,8,16,512]{3,2,1,0:T(8,128)(2,1)S(1)}, u32[]{:S(2)}, u32[]{:S(2)}) collective-permute-start(bf16[2,8,16,512]{3,2,1,0:T(8,128)(2,1)S(1)} %get-tuple-element.148), channel_id=1, source_target_pairs={{0,2},{1,3},{2,0},{3,1},{4,6},{5,7},{6,4},{7,5},{8,10},{9,11},{10,... | collective-permute-start | bytes 786440 | tf_op jit(solution)/shard_map/ppermute | solution.py:744
  53.1 8.1 %collective-permute-start.18 = (bf16[4,8,16,512]{3,2,1,0:T(8,128)(2,1)S(1)}, bf16[4,8,16,512]{3,2,1,0:T(8,128)(2,1)S(1)}, u32[]{:S(2)}, u32[]{:S(2)}) collective-permute-start(bf16[4,8,16,512]{3,2,1,0:T(8,128)(2,1)S(1)} %collective-permute-done.12.by_x_ref.rest_2_), channel_id=1, source_target_pairs={{0,1},{1,0},{2,3},{3,2},{4,5},{5,4},{6,7},{7,6},{8,9},{9,8},{10,11... | collective-permute-start | bytes 1572872 | tf_op jit(solution)/shard_map/ppermute | solution.py:744
  53.1 8.1 %collective-permute-start.19 = (bf16[4,8,16,512]{3,2,1,0:T(8,128)(2,1)S(1)}, bf16[4,8,16,512]{3,2,1,0:T(8,128)(2,1)S(1)}, u32[]{:S(2)}, u32[]{:S(2)}) collective-permute-start(bf16[4,8,16,512]{3,2,1,0:T(8,128)(2,1)S(1)} %collective-permute-done.11.by_y_ref.rest_3_), channel_id=1, source_target_pairs={{0,1},{1,0},{2,3},{3,2},{4,5},{5,4},{6,7},{7,6},{8,9},{9,8},{10,11... | collective-permute-start | bytes 1572872 | tf_op jit(solution)/shard_map/ppermute | solution.py:744
  60.2 1.5 %collective-permute-start.22 = (bf16[2,8,16,512]{3,2,1,0:T(8,128)(2,1)S(1)}, bf16[2,8,16,512]{3,2,1,0:T(8,128)(2,1)S(1)}, u32[]{:S(2)}, u32[]{:S(2)}) collective-permute-start(bf16[2,8,16,512]{3,2,1,0:T(8,128)(2,1)S(1)} %collective-permute-done.20.rest_7_), channel_id=1, source_target_pairs={{0,1},{1,0},{2,3},{3,2},{4,5},{5,4},{6,7},{7,6},{8,9},{9,8},{10,11... | collective-permute-start | bytes 786440 | tf_op jit(solution)/shard_map/ppermute | solution.py:744
  60.2 1.9 %collective-permute-start.23 = (bf16[2,8,16,512]{3,2,1,0:T(8,128)(2,1)S(1)}, bf16[2,8,16,512]{3,2,1,0:T(8,128)(2,1)S(1)}, u32[]{:S(2)}, u32[]{:S(2)}) collective-permute-start(bf16[2,8,16,512]{3,2,1,0:T(8,128)(2,1)S(1)} %collective-permute-done.21.rest_8_), channel_id=1, source_target_pairs={{0,1},{1,0},{2,3},{3,2},{4,5},{5,4},{6,7},{7,6},{8,9},{9,8},{10,11... | collective-permute-start | bytes 786440 | tf_op jit(solution)/shard_map/ppermute | solution.py:744
  65.5 1.6 %collective-permute-start.24 = (bf16[1,256,512]{2,1,0:T(8,128)(2,1)S(1)}, bf16[1,256,512]{2,1,0:T(8,128)(2,1)S(1)}, u32[]{:S(2)}, u32[]{:S(2)}) collective-permute-start(bf16[1,256,512]{2,1,0:T(8,128)(2,1)S(1)} %bitcast.32), channel_id=1, source_target_pairs={{0,1},{1,0},{2,3},{3,2},{4,5},{5,4},{6,7},{7,6},{8,9},{9,8},{10,11... | collective-permute-start | bytes 786440 | tf_op jit(solution)/shard_map/ppermute | solution.py:747
  77.5 1.6 %collective-permute-start.25 = (bf16[256,512]{1,0:T(8,128)(2,1)S(1)}, bf16[256,512]{1,0:T(8,128)(2,1)S(1)}, u32[]{:S(2)}, u32[]{:S(2)}) collective-permute-start(bf16[256,512]{1,0:T(8,128)(2,1)S(1)} %get-tuple-element.168), channel_id=1, source_target_pairs={{0,1},{1,0},{2,3},{3,2},{4,5},{5,4},{6,7},{7,6},{8,9},{9,8},{10,11... | collective-permute-start | bytes 786440 | tf_op jit(solution)/shard_map/ppermute | solution.py:747
  81.6 2.7 %collective-permute-start.26 = (bf16[4,4,64,512]{3,2,1,0:T(8,128)(2,1)S(1)}, bf16[4,4,64,512]{3,2,1,0:T(8,128)(2,1)S(1)}, u32[]{:S(2)}, u32[]{:S(2)}) collective-permute-start(bf16[4,4,64,512]{3,2,1,0:T(8,128)(2,1)S(1)} %get-tuple-element.187), channel_id=1, source_target_pairs={{0,1},{1,0},{2,3},{3,2},{4,5},{5,4},{6,7},{7,6},{8,9},{9,8},{10,11... | collective-permute-start | bytes 3145736 | tf_op jit(solution)/shard_map/ppermute | solution.py:744
  86.8 3.2 %collective-permute-start.27 = (bf16[4,4,16,2688]{3,2,1,0:T(8,128)(2,1)S(1)}, bf16[4,4,16,2688]{3,2,1,0:T(8,128)(2,1)S(1)}, u32[]{:S(2)}, u32[]{:S(2)}) collective-permute-start(bf16[4,4,16,2688]{3,2,1,0:T(8,128)(2,1)S(1)} %get-tuple-element.198), channel_id=1, source_target_pairs={{0,1},{1,0},{2,3},{3,2},{4,5},{5,4},{6,7},{7,6},{8,9},{9,8},{10,11... | collective-permute-start | bytes 4128776 | tf_op jit(solution)/shard_map/ppermute | solution.py:744
  87.0 11.7 %collective-permute-start.28 = (bf16[2,64,512]{2,1,0:T(8,128)(2,1)S(1)}, bf16[2,64,512]{2,1,0:T(8,128)(2,1)S(1)}, u32[]{:S(2)}, u32[]{:S(2)}) collective-permute-start(bf16[2,64,512]{2,1,0:T(8,128)(2,1)S(1)} %get-tuple-element.188), channel_id=1, source_target_pairs={{0,2},{1,3},{2,0},{3,1},{4,6},{5,7},{6,4},{7,5},{8,10},{9,11},{10,... | collective-permute-start | bytes 393224 | tf_op jit(solution)/shard_map/ppermute | solution.py:744
  88.4 10.3 %collective-permute-start.29 = (bf16[2,64,512]{2,1,0:T(8,128)(2,1)S(1)}, bf16[2,64,512]{2,1,0:T(8,128)(2,1)S(1)}, u32[]{:S(2)}, u32[]{:S(2)}) collective-permute-start(bf16[2,64,512]{2,1,0:T(8,128)(2,1)S(1)} %get-tuple-element.212), channel_id=1, source_target_pairs={{0,4},{1,5},{2,6},{3,7},{4,0},{5,1},{6,2},{7,3},{8,12},{9,13},{10,... | collective-permute-start | bytes 393224 | tf_op jit(solution)/shard_map/ppermute | solution.py:744
  90.3 8.4 %collective-permute-start.30 = (bf16[2,16,2688]{2,1,0:T(8,128)(2,1)S(1)}, bf16[2,16,2688]{2,1,0:T(8,128)(2,1)S(1)}, u32[]{:S(2)}, u32[]{:S(2)}) collective-permute-start(bf16[2,16,2688]{2,1,0:T(8,128)(2,1)S(1)} %get-tuple-element.199), channel_id=1, source_target_pairs={{0,2},{1,3},{2,0},{3,1},{4,6},{5,7},{6,4},{7,5},{8,10},{9,11},{10,... | collective-permute-start | bytes 516104 | tf_op jit(solution)/shard_map/ppermute | solution.py:744
  91.8 6.9 %collective-permute-start.31 = (bf16[2,16,2688]{2,1,0:T(8,128)(2,1)S(1)}, bf16[2,16,2688]{2,1,0:T(8,128)(2,1)S(1)}, u32[]{:S(2)}, u32[]{:S(2)}) collective-permute-start(bf16[2,16,2688]{2,1,0:T(8,128)(2,1)S(1)} %get-tuple-element.215), channel_id=1, source_target_pairs={{0,4},{1,5},{2,6},{3,7},{4,0},{5,1},{6,2},{7,3},{8,12},{9,13},{10,... | collective-permute-start | bytes 516104 | tf_op jit(solution)/shard_map/ppermute | solution.py:744
  98.9 3.0 %collective-permute-start.33 = (bf16[4,4,16,1536]{3,2,1,0:T(8,128)(2,1)S(1)}, bf16[4,4,16,1536]{3,2,1,0:T(8,128)(2,1)S(1)}, u32[]{:S(2)}, u32[]{:S(2)}) collective-permute-start(bf16[4,4,16,1536]{3,2,1,0:T(8,128)(2,1)S(1)} %get-tuple-element.224), channel_id=1, source_target_pairs={{0,1},{1,0},{2,3},{3,2},{4,5},{5,4},{6,7},{7,6},{8,9},{9,8},{10,11... | collective-permute-start | bytes 2359304 | tf_op jit(solution)/shard_map/ppermute | solution.py:744
  99.0 16.6 %collective-permute-start.35 = (bf16[4,16,4736]{2,1,0:T(8,128)(2,1)S(1)}, bf16[4,16,4736]{2,1,0:T(8,128)(2,1)S(1)}, u32[]{:S(2)}, u32[]{:S(2)}) collective-permute-start(bf16[4,16,4736]{2,1,0:T(8,128)(2,1)S(1)} %get-tuple-element.228), channel_id=1, source_target_pairs={{0,4},{1,5},{2,6},{3,7},{4,0},{5,1},{6,2},{7,3},{8,12},{9,13},{10,... | collective-permute-start | bytes 1818632 | tf_op jit(solution)/shard_map/ppermute | solution.py:744
  99.7 16.5 %collective-permute-start.34 = (bf16[4,16,4736]{2,1,0:T(8,128)(2,1)S(1)}, bf16[4,16,4736]{2,1,0:T(8,128)(2,1)S(1)}, u32[]{:S(2)}, u32[]{:S(2)}) collective-permute-start(bf16[4,16,4736]{2,1,0:T(8,128)(2,1)S(1)} %get-tuple-element.216), channel_id=1, source_target_pairs={{0,2},{1,3},{2,0},{3,1},{4,6},{5,7},{6,4},{7,5},{8,10},{9,11},{10,... | collective-permute-start | bytes 1818632 | tf_op jit(solution)/shard_map/ppermute | solution.py:744
  100.3 1.5 %collective-permute-start.32 = (bf16[256,512]{1,0:T(8,128)(2,1)S(1)}, bf16[256,512]{1,0:T(8,128)(2,1)S(1)}, u32[]{:S(2)}, u32[]{:S(2)}) collective-permute-start(bf16[256,512]{1,0:T(8,128)(2,1)S(1)} %get-tuple-element.217), channel_id=1, source_target_pairs={{0,1},{1,0},{2,3},{3,2},{4,5},{5,4},{6,7},{7,6},{8,9},{9,8},{10,11... | collective-permute-start | bytes 786440 | tf_op jit(solution)/shard_map/ppermute | solution.py:747
  102.1 19.2 %collective-permute-start.37 = (bf16[4,16,1536]{2,1,0:T(8,128)(2,1)S(1)}, bf16[4,16,1536]{2,1,0:T(8,128)(2,1)S(1)}, u32[]{:S(2)}, u32[]{:S(2)}) collective-permute-start(bf16[4,16,1536]{2,1,0:T(8,128)(2,1)S(1)} %get-tuple-element.234), channel_id=1, source_target_pairs={{0,6},{1,7},{2,4},{3,5},{4,2},{5,3},{6,0},{7,1},{8,14},{9,15},{10,... | collective-permute-start | bytes 589832 | tf_op jit(solution)/shard_map/ppermute | solution.py:744
  104.4 20.3 %collective-permute-start.38 = (bf16[4,16,1536]{2,1,0:T(8,128)(2,1)S(1)}, bf16[4,16,1536]{2,1,0:T(8,128)(2,1)S(1)}, u32[]{:S(2)}, u32[]{:S(2)}) collective-permute-start(bf16[4,16,1536]{2,1,0:T(8,128)(2,1)S(1)} %get-tuple-element.235), channel_id=1, source_target_pairs={{0,2},{1,3},{2,0},{3,1},{4,6},{5,7},{6,4},{7,5},{8,10},{9,11},{10,... | collective-permute-start | bytes 589832 | tf_op jit(solution)/shard_map/ppermute | solution.py:744
  105.0 19.8 %collective-permute-start.39 = (bf16[4,16,1536]{2,1,0:T(8,128)(2,1)S(1)}, bf16[4,16,1536]{2,1,0:T(8,128)(2,1)S(1)}, u32[]{:S(2)}, u32[]{:S(2)}) collective-permute-start(bf16[4,16,1536]{2,1,0:T(8,128)(2,1)S(1)} %get-tuple-element.236), channel_id=1, source_target_pairs={{0,4},{1,5},{2,6},{3,7},{4,0},{5,1},{6,2},{7,3},{8,12},{9,13},{10,... | collective-permute-start | bytes 589832 | tf_op jit(solution)/shard_map/ppermute | solution.py:744
  117.0 8.4 %collective-permute-start.40 = (bf16[16,4736]{1,0:T(8,128)(2,1)S(1)}, bf16[16,4736]{1,0:T(8,128)(2,1)S(1)}, u32[]{:S(2)}, u32[]{:S(2)}) collective-permute-start(bf16[16,4736]{1,0:T(8,128)(2,1)S(1)} %get-tuple-element.239), channel_id=1, source_target_pairs={{0,8},{1,9},{2,10},{3,11},{4,12},{5,13},{6,14},{7,15},{8,0},{9,1},... | collective-permute-start | bytes 454664 | tf_op jit(solution)/shard_map/ppermute | solution.py:744
  117.1 8.3 %collective-permute-start.41 = (bf16[16,4736]{1,0:T(8,128)(2,1)S(1)}, bf16[16,4736]{1,0:T(8,128)(2,1)S(1)}, u32[]{:S(2)}, u32[]{:S(2)}) collective-permute-start(bf16[16,4736]{1,0:T(8,128)(2,1)S(1)} %get-tuple-element.243), channel_id=1, source_target_pairs={{0,8},{1,9},{2,10},{3,11},{4,12},{5,13},{6,14},{7,15},{8,0},{9,1},... | collective-permute-start | bytes 454664 | tf_op jit(solution)/shard_map/ppermute | solution.py:744
  121.3 11.0 %collective-permute-start.36 = (bf16[128,1024]{1,0:T(8,128)(2,1)S(1)}, bf16[128,1024]{1,0:T(8,128)(2,1)S(1)}, u32[]{:S(2)}, u32[]{:S(2)}) collective-permute-start(bf16[128,1024]{1,0:T(8,128)(2,1)S(1)} %get-tuple-element.230), channel_id=1, source_target_pairs={{0,2},{1,3},{2,0},{3,1},{4,6},{5,7},{6,4},{7,5},{8,10},{9,11},{10,... | collective-permute-start | bytes 786440 | tf_op jit(solution)/shard_map/ppermute | solution.py:747
  125.5 8.4 %collective-permute-start.42 = (bf16[16,4736]{1,0:T(8,128)(2,1)S(1)}, bf16[16,4736]{1,0:T(8,128)(2,1)S(1)}, u32[]{:S(2)}, u32[]{:S(2)}) collective-permute-start(bf16[16,4736]{1,0:T(8,128)(2,1)S(1)} %shard_map.268), channel_id=1, source_target_pairs={{0,24},{1,25},{2,26},{3,27},{4,28},{5,29},{6,30},{7,31},{8,16},{9,... | collective-permute-start | bytes 454664 | tf_op jit(solution)/shard_map/ppermute | solution.py:744
  127.9 6.7 %collective-permute-start.43 = (bf16[16,1536]{1,0:T(8,128)(2,1)S(1)}, bf16[16,1536]{1,0:T(8,128)(2,1)S(1)}, u32[]{:S(2)}, u32[]{:S(2)}) collective-permute-start(bf16[16,1536]{1,0:T(8,128)(2,1)S(1)} %get-tuple-element.246), channel_id=1, source_target_pairs={{0,8},{1,9},{2,10},{3,11},{4,12},{5,13},{6,14},{7,15},{8,0},{9,1},... | collective-permute-start | bytes 147464 | tf_op jit(solution)/shard_map/ppermute | solution.py:744
  127.9 8.8 %collective-permute-start.44 = (bf16[16,1536]{1,0:T(8,128)(2,1)S(1)}, bf16[16,1536]{1,0:T(8,128)(2,1)S(1)}, u32[]{:S(2)}, u32[]{:S(2)}) collective-permute-start(bf16[16,1536]{1,0:T(8,128)(2,1)S(1)} %get-tuple-element.247), channel_id=1, source_target_pairs={{0,16},{1,17},{2,18},{3,19},{4,20},{5,21},{6,22},{7,23},{8,24},{9,... | collective-permute-start | bytes 147464 | tf_op jit(solution)/shard_map/ppermute | solution.py:744
  129.9 6.8 %collective-permute-start.45 = (bf16[16,1536]{1,0:T(8,128)(2,1)S(1)}, bf16[16,1536]{1,0:T(8,128)(2,1)S(1)}, u32[]{:S(2)}, u32[]{:S(2)}) collective-permute-start(bf16[16,1536]{1,0:T(8,128)(2,1)S(1)} %get-tuple-element.248), channel_id=1, source_target_pairs={{0,24},{1,25},{2,26},{3,27},{4,28},{5,29},{6,30},{7,31},{8,16},{9,... | collective-permute-start | bytes 147464 | tf_op jit(solution)/shard_map/ppermute | solution.py:744
